TPU v7x, 768 devices: a whole 4x8x12 slice. The times are simulated.
768 devices in a mesh: occ: 96 (over z, y_hi, x), vir: 8 (over y_lo, core).
Axes of the slice: x: 4, y: 8 (y_hi: 2, y_lo: 4; y = y_hi * 4 + y_lo), z: 12, core: 2. Of those that a mesh axis runs over, the one named last changes fastest.
Arguments:
- amplitudes: float32 [96, 128, 128, 256], P('occ', 'vir'), may hold values from -6 to 6
- integrals: float32 [384, 256, 128], P('occ', 'vir'), may hold values from -0.09375 to 0.09375
- irrep_occ: int32 [128], replicated, may hold values from 0 to 7
- irrep_j: int32 [3], replicated, may hold values from 0 to 7
- irrep_vir: int32 [256], replicated, may hold values from 0 to 7
- irrep_b: int32 [128], replicated, may hold values from 0 to 7
Outputs:
- cycle_term: float32 [96, 3, 128, 128], P('occ', None, 'vir')
Inputs may be any that keep to these rules, and one draw needn't show every extreme that they name: `irrep_occ`: D2h irrep labels. `irrep_j`: D2h irrep labels. `irrep_vir`: D2h irrep labels. `irrep_b`: D2h irrep labels.
All inputs are finite; a program needn't handle non-finite values.
Results may differ from a plain program's by a relative error of at most 0.00007.
Values sent between devices are 32-bit elements; how exact they have to be, the bound alone decides.
No kernel may reach another device: no remote copies, remote signals or barrier semaphores. Data moves between devices by JAX's collectives and lax.ppermute only.
A program may use at most 128 MiB of HBM per device.

v0:
```python
import jax
import jax.numpy as jnp
from jax import lax
from jax.sharding import PartitionSpec as P

K = 128
B = 128
J = 3


def local(amplitudes, integrals, irrep_occ, irrep_j, irrep_vir, irrep_b):
    relaid = lax.all_to_all(amplitudes, "vir", split_axis=3, concat_axis=1, tiled=True)
    slab_width = relaid.shape[3]
    label_vir = lax.dynamic_slice_in_dim(irrep_vir, lax.axis_index("vir") * slab_width, slab_width)
    right_part = jnp.bitwise_xor(label_vir[:, None], irrep_b[None, :])
    gathered = lax.all_gather(integrals, "occ", axis=0, tiled=True)
    table = gathered.reshape(K, J, slab_width, B)
    left_part = jnp.bitwise_xor(irrep_occ[:, None], irrep_j[None, :])
    parity = jnp.bitwise_xor(left_part[:, :, None, None], right_part[None, None, :, :])
    table = jnp.where(parity == 0, table, jnp.zeros_like(table))
    partial_sums = jnp.einsum("ikac,kjcb->ijab", relaid, table, precision=lax.Precision.HIGHEST)
    return lax.psum_scatter(partial_sums, "vir", scatter_dimension=2, tiled=True)


def solution(mesh):
    return jax.shard_map(
        local,
        mesh=mesh,
        in_specs=(P("occ", "vir", None, None), P("occ", "vir", None), P(), P(), P(), P()),
        out_specs=P("occ", None, "vir", None),
        check_vma=False,
    )
```

profile of v0, /device:TPU:1, one launch (start us, length us, event | category | flops | bytes accessed | tf_op | source)
XLA Modules:
  0.0 338.4 jit_solution(18112723191168358729)
XLA Ops:
  6.5 0.0 copy-start.3
  6.5 0.0 copy-start.1
  6.5 0.0 copy-start.2
  6.5 0.0 copy-start
  6.5 0.0 all-gather.2.cloned.1.call-start
  6.6 0.7 all-gather.2.cloned.1.call-update
  7.3 3.1 copy.15
  10.3 14.0 %all-to-all-start = ((f32[1,16,128,256]{2,1,0,3:T(8,128)}), f32[1,16,128,256]{2,1,0,3:T(8,128)S(1)}, u32[]{:S(2)}, u32[]{:S(2)}) async-start(f32[1,16,128,256]{2,1,0,3:T(8,128)} %copy.15), calls=%async_computation | async-start | bytes 4194304 | tf_op jit(solution)/shard_map/all_to_all | solution.py:12
  24.4 0.0 all-reduce.3.cloned.1.call-start
  24.4 0.0 copy-done.3
  24.4 0.1 dynamic_slice.3
  24.5 0.0 copy-done.1
  24.5 0.0 copy-done.2
  24.5 0.1 broadcast_xor_fusion.1
  24.5 0.0 copy-done
  24.5 0.1 broadcast_xor_fusion
  24.6 48.9 %all-to-all-done = f32[1,16,128,256]{2,1,0,3:T(8,128)S(1)} async-done(((f32[1,16,128,256]{2,1,0,3:T(8,128)}), f32[1,16,128,256]{2,1,0,3:T(8,128)S(1)}, u32[]{:S(2)}, u32[]{:S(2)}) %all-to-all-start) | async-done | bytes 2097184 | tf_op jit(solution)/shard_map/all_to_all | solution.py:12
  73.5 0.7 copy.16
  74.2 1.2 copy.17
  75.4 155.2 %all-gather.2.cloned.1.call-done = f32[384,32,128]{2,1,0:T(8,128)} async-done(((f32[4,32,128]{2,1,0:T(8,128)}), f32[384,32,128]{2,1,0:T(8,128)}) %all-gather.2.cloned.1.call-update) | async-done | bytes 6291472 | tf_op jit(solution)/shard_map/all_gather | solution.py:16
  230.6 6.6 %copy.14 = f32[128,3,32,128]{0,3,2,1:T(8,128)} copy(f32[128,3,32,128]{3,2,1,0:T(8,128)} %bitcast.17) | data formatting | bytes 12582912 | tf_op jit(solution)/shard_map/reshape | solution.py:17
  237.2 7.9 %fusion.6 = f32[1,3,128,128]{2,3,1,0:T(8,128)S(1)} fusion(f32[128,128,32,1]{1,0,2,3:T(8,128)S(1)} %bitcast.15, f32[128,3,32,128]{0,3,2,1:T(8,128)} %copy.14, s32[32,128]{1,0:T(8,128)S(1)} %broadcast_xor_fusion, s32[128,3]{0,1:T(4,128)S(1)} %broadcast_xor_fusion.1), kind=kOutput, calls=%fused_computation.7 | convolution fusion | flops 2420637696 | bytes 8603136 | tf_op jit(solution)/shard_map/ikac,kjcb->ijab/dot_general | solution.py:21
  245.1 0.8 copy.18
  245.9 0.0 all-reduce.3.cloned.1.call-update
  245.9 1.3 dynamic-slice
  247.8 82.3 %all-reduce.3.cloned.1.call-done = f32[1,3,128,128]{3,0,1,2:T(1,128)} async-done(((f32[1,3,128,128]{3,0,1,2:T(1,128)}), f32[1,3,128,128]{3,0,1,2:T(1,128)}) %all-reduce.3.cloned.1.call-update) | async-done | bytes 196624
  330.2 0.7 constant_dynamic-slice_fusion
  330.9 0.6 copy.19
Async XLA Ops:
  6.5 17.8 %copy-start.3 = (s32[256]{0:T(256)S(1)}, s32[256]{0:T(256)}, u32[]{:S(2)}) copy-start(s32[256]{0:T(256)} %param.10) | copy-start | bytes 3076
  6.5 17.9 %copy-start.1 = (s32[3]{0:T(128)S(1)}, s32[3]{0:T(128)}, u32[]{:S(2)}) copy-start(s32[3]{0:T(128)} %param.9) | copy-start | bytes 40
  6.5 17.9 %copy-start.2 = (s32[128]{0:T(128)S(1)}, s32[128]{0:T(128)}, u32[]{:S(2)}) copy-start(s32[128]{0:T(128)} %param.8) | copy-start | bytes 1540
  6.5 18.0 %copy-start = (s32[128]{0:T(128)S(1)}, s32[128]{0:T(128)}, u32[]{:S(2)}) copy-start(s32[128]{0:T(128)} %param.11) | copy-start | bytes 1540
  6.5 224.1 %all-gather.2.cloned.1.call-start = ((), (), s32[]{:S(2)}) async-start(), calls=%async_computation.1 | async-start | bytes 6356992 | tf_op jit(solution)/shard_map/all_gather | solution.py:16
  10.3 63.2 %all-to-all-start = ((f32[1,16,128,256]{2,1,0,3:T(8,128)}), f32[1,16,128,256]{2,1,0,3:T(8,128)S(1)}, u32[]{:S(2)}, u32[]{:S(2)}) async-start(f32[1,16,128,256]{2,1,0,3:T(8,128)} %copy.15), calls=%async_computation | async-start | bytes 4194304 | tf_op jit(solution)/shard_map/all_to_all | solution.py:12
  24.4 305.8 %all-reduce.3.cloned.1.call-start = ((), (), s32[]{:S(2)}) async-start(), calls=%async_computation.2 | async-start | bytes 393216
Sparse Core Ops, SparseCore 0:
  12.7 217.8 all-gather.1
  246.0 84.0 all-reduce.2
where the time goes:
time: 339 us; the launch traced here: 338 us
  waiting for transfers between devices  287 us (85%)
  local copies, waits for them, and re-layouts  15 us (4%)
  starting transfers between devices  14.1 us (4%)
  between operations  14.1 us (4%)
  matrix products  7.91 us (2%)
    all_gather x1, waiting for transfers between devices, local(): gathered = lax.all_gather(integrals, 'occ', axis=0, tiled=True)  155 us
    unnamed x3, waiting for transfers between devices  83 us
    all_to_all x1, waiting for transfers between devices, local(): lax.all_to_all(amplitudes, 'vir', split_axis=3, concat_axis=1, tiled=True)  48.9 us
    all_to_all x1, starting transfers between devices, local(): lax.all_to_all(amplitudes, 'vir', split_axis=3, concat_axis=1, tiled=True)  14 us
    dot_general x1, matrix products, local(): jnp.einsum('ikac,kjcb->ijab', relaid, table, precision=lax.Precision.HIGH...  7.91 us
  transfers between devices with their start and end apart: 3, of which 3 were waited for; matrix products, arithmetic and copies ran while one was open for 2% of the time, Pallas kernels for 0%

commit v1 on v0

v1 whole, which is shorter than its diff:
```python
import jax
import jax.numpy as jnp
from jax import lax
from jax.experimental import pallas as pl
from jax.experimental.pallas import tpu as pltpu
from jax.sharding import Mesh
from jax.sharding import PartitionSpec as P

J = 3
LANES = 128
ROWS = 4
SLAB = 32
PLACES = 32
HOPS = ("z", "y_hi")
PLANE = ("x", "y_lo", "core")
AXES = ("z", "y_hi", "x", "y_lo", "core")


def columns(row):
    return jnp.broadcast_to(row, (LANES, LANES)).T


def ranks(label_b):
    same = columns(label_b) == label_b
    before = lax.broadcasted_iota(jnp.int32, (LANES, LANES), 0) < lax.broadcasted_iota(jnp.int32, (LANES, LANES), 1)
    return jnp.sum(jnp.where(same & before, 1, 0), axis=0, keepdims=True)


def placing(rank, round_index, part):
    place = rank - round_index * PLACES
    lane = lax.broadcasted_iota(jnp.int32, (LANES, LANES), 0)
    return (lane == place + part * PLACES) & (place >= 0) & (place < PLACES)


def occ_index():
    return (lax.axis_index("z") * 2 + lax.axis_index("y_hi")) * 4 + lax.axis_index("x")


def vir_index():
    return lax.axis_index("y_lo") * 2 + lax.axis_index("core")


def pack_kernel(round_ref, occ_ref, j_ref, vir_ref, b_ref, w_ref, out_ref, rounds_ref, labels):
    label_b = b_ref[...]
    rank = ranks(label_b)
    for half in range(2):
        labels[half * LANES:(half + 1) * LANES, :] = columns(vir_ref[half:half + 1, :])
    start = pl.multiple_of(vir_index() * SLAB, SLAB)
    right = jnp.bitwise_xor(labels[pl.ds(start, SLAB), :], label_b)
    first = occ_index() * ROWS
    total = jnp.zeros((SLAB, LANES), jnp.float32)
    for part in range(ROWS):
        k = lax.div(first + part, J)
        left = jnp.bitwise_xor(occ_ref[k], j_ref[first + part - k * J])
        kept = jnp.where(right == left, w_ref[part], 0.0)
        put = jnp.where(placing(rank, round_ref[0], part), 1.0, 0.0)
        total = total + lax.dot_general(
            kept, put, (((1,), (1,)), ((), ())), precision=lax.Precision.HIGHEST, preferred_element_type=jnp.float32
        )
    out_ref[...] = total
    rounds_ref[0] = lax.div(jnp.max(rank) + PLACES, PLACES)


def halves(values):
    high = values.astype(jnp.bfloat16)
    return high, (values - high.astype(jnp.float32)).astype(jnp.bfloat16)


def multiply_kernel(with_sum, round_ref, occ_ref, j_ref, vir_ref, b_ref, w_ref, t_ref, *rest):
    if with_sum:
        sum_ref, out_ref, w_high, w_low, t_high, t_low = rest
    else:
        out_ref, w_high, w_low, t_high, t_low = rest
    label_b = b_ref[...]
    rank = ranks(label_b)
    label_c = jnp.concatenate([columns(vir_ref[half:half + 1, :]) for half in range(2)], axis=0)
    right = jnp.bitwise_xor(label_c, label_b)
    puts = [jnp.where(placing(rank, round_ref[0], part), 1.0, 0.0).astype(jnp.bfloat16) for part in range(ROWS)]
    split = [halves(w_ref[group]) for group in range(3)]
    first = vir_index() * 16 + lax.axis_index("x") * 4
    for k in range(4):
        for j in range(J):
            group, part = divmod(k * J + j, ROWS)
            keep = right == jnp.bitwise_xor(occ_ref[first + k], j_ref[j])
            for piece, target in zip(split[group], (w_high, w_low)):
                spread = jnp.dot(piece, puts[part], preferred_element_type=jnp.float32)
                target[k * 256:(k + 1) * 256, j * LANES:(j + 1) * LANES] = jnp.where(keep, spread, 0.0).astype(jnp.bfloat16)
        high, low = halves(t_ref[:, k].reshape(4 * LANES, 256))
        t_high[:, k * 256:(k + 1) * 256] = high
        t_low[:, k * 256:(k + 1) * 256] = low
    total = jnp.dot(t_high[...], w_high[...], preferred_element_type=jnp.float32)
    total = total + jnp.dot(t_high[...], w_low[...], preferred_element_type=jnp.float32)
    total = total + jnp.dot(t_low[...], w_high[...], preferred_element_type=jnp.float32)
    for block in range(32):
        for j in range(J):
            piece = total[block * 16:(block + 1) * 16, j * LANES:(j + 1) * LANES]
            if with_sum:
                piece = piece + sum_ref[block, j]
            out_ref[block, j] = piece


SMEM = pl.BlockSpec(memory_space=pltpu.SMEM)
VMEM = pl.BlockSpec(memory_space=pltpu.VMEM)


def pack(round_index, occ, j, vir, b, integrals):
    return pl.pallas_call(
        pack_kernel,
        out_shape=(jax.ShapeDtypeStruct((SLAB, LANES), jnp.float32), jax.ShapeDtypeStruct((1,), jnp.int32)),
        in_specs=[SMEM, SMEM, SMEM, VMEM, VMEM, VMEM],
        out_specs=(VMEM, SMEM),
        scratch_shapes=[pltpu.VMEM((256, LANES), jnp.int32)],
        compiler_params=pltpu.CompilerParams(vmem_limit_bytes=8 << 20),
        name="pack",
    )(round_index, occ, j, vir, b, integrals)


def multiply(round_index, occ, j, vir, b, w, t, total=None):
    with_sum = total is not None
    return pl.pallas_call(
        lambda *refs: multiply_kernel(with_sum, *refs),
        out_shape=jax.ShapeDtypeStruct((32, J, 16, LANES), jnp.float32),
        in_specs=[SMEM, SMEM, SMEM, VMEM, VMEM, VMEM, VMEM] + [VMEM] * with_sum,
        out_specs=VMEM,
        scratch_shapes=[
            pltpu.VMEM((1024, J * LANES), jnp.bfloat16),
            pltpu.VMEM((1024, J * LANES), jnp.bfloat16),
            pltpu.VMEM((512, 1024), jnp.bfloat16),
            pltpu.VMEM((512, 1024), jnp.bfloat16),
        ],
        compiler_params=pltpu.CompilerParams(vmem_limit_bytes=24 << 20),
        cost_estimate=pl.CostEstimate(flops=3 * 2 * 512 * 1024 * 384, bytes_accessed=4 << 20, transcendentals=0),
        name="multiply",
    )(round_index, occ, j, vir, b, w, t, *([total] if with_sum else []))


def owners():
    pairs = []
    for o in range(96):
        for v in range(8):
            place = o % 3 * 8 + v
            pairs.append((o * 8 + v, (place * 4 + o % 12 // 3) * 8 + o // 12))
    return pairs


def local(amplitudes, integrals, irrep_occ, irrep_j, irrep_vir, irrep_b):
    vir, b = irrep_vir.reshape(2, LANES), irrep_b.reshape(1, LANES)
    labels = (irrep_occ, irrep_j, vir, b)

    def column(round_index):
        packed, rounds = pack(round_index, *labels, integrals)
        packed = lax.ppermute(packed, AXES, owners())
        copies = jnp.broadcast_to(packed[None], (24, SLAB, LANES))
        gathered = lax.all_to_all(copies, HOPS, split_axis=0, concat_axis=0, tiled=True)
        return gathered.reshape(3, 256, LANES), rounds

    w, rounds = column(jnp.zeros((1,), jnp.int32))
    t = lax.all_to_all(amplitudes.reshape(4, 4, LANES, 256), "x", split_axis=0, concat_axis=0, tiled=True)
    total = multiply(jnp.zeros((1,), jnp.int32), *labels, w, t)

    def another(state):
        index, total = state
        return index + 1, multiply(index[None], *labels, column(index[None])[0], t, total)

    _, total = lax.while_loop(lambda state: state[0] < rounds[0], another, (jnp.int32(1), total))
    parts = lax.all_to_all(total, PLANE, split_axis=0, concat_axis=0, tiled=True)
    return jnp.sum(parts, axis=0, keepdims=True)


def solution(mesh):
    parts = Mesh(mesh.devices.reshape(12, 2, 4, 4, 2), AXES)
    occ, vir = ("z", "y_hi", "x"), ("y_lo", "core")
    return jax.shard_map(
        local,
        mesh=parts,
        in_specs=(P(occ, vir, None, None), P(occ, vir, None), P(), P(), P(), P()),
        out_specs=P(occ, None, vir, None),
        check_vma=False,
    )
```

time: 339 us -> 121 us (0.36)
  waiting for transfers between devices: 287 us -> 24 us
  blocking collectives: 0 us -> 76.3 us
  local copies, waits for them, and re-layouts: 15 us -> 0.05 us
  between operations: 14.1 us -> 0.08 us
  matrix products: 7.91 us -> 0 us
  Pallas kernels: 0 us -> 5.62 us
    all_gather x1 -> x0, waiting for transfers between devices: 155 us -> none  [local(): gathered = lax.all_gather(integrals, 'occ', axis=0, tiled=True)]
    unnamed x3 -> x0, waiting for transfers between devices: 83 us -> none
    all_to_all x0 -> x2, blocking collectives: none -> 76.3 us  [the longest x1 42.2 us: column(): lax.all_to_all(copies, HOPS, split_axis=0, concat_axis=0, tiled=True)]
    all_to_all x1, waiting for transfers between devices: 48.9 us -> 20.7 us  [local(): lax.all_to_all(amplitudes.reshape(4, 4, LANES, 256), 'x', split_axis=0, c...]
    all_to_all x1, starting transfers between devices: 14 us -> 4.59 us  [local(): lax.all_to_all(amplitudes.reshape(4, 4, LANES, 256), 'x', split_axis=0, c...]
    ppermute x0 -> x1, starting transfers between devices: none -> 8.84 us  [column(): packed = lax.ppermute(packed, AXES, owners())]
    dot_general x1 -> x0, matrix products: 7.91 us -> none  [local(): jnp.einsum('ikac,kjcb->ijab', relaid, table, precision=lax.Precision.HIGH...]
    reshape x1 -> x0, local copies, waits for them, and re-layouts: 6.55 us -> none  [local(): table = gathered.reshape(K, J, slab_width, B)]
  transfers between devices with their start and end apart: 3 -> 2, of which waited for: 3 -> 2; matrix products, arithmetic and copies ran while one was open for 2% -> 0% of each run, Pallas kernels for 0% -> 0%
where the time goes in v1:
time: 121 us
  blocking collectives  76.3 us (63%)
  waiting for transfers between devices  24 us (20%)
  starting transfers between devices  13.4 us (11%)
  Pallas kernels  5.62 us (5%)
    all_to_all x1, blocking collectives, column(): lax.all_to_all(copies, HOPS, split_axis=0, concat_axis=0, tiled=True)  42.2 us
    all_to_all x1, blocking collectives, local(): lax.all_to_all(total, PLANE, split_axis=0, concat_axis=0, tiled=True)  34.1 us
    all_to_all x1, waiting for transfers between devices, local(): lax.all_to_all(amplitudes.reshape(4, 4, LANES, 256), 'x', split_axis=0, c...  20.7 us
    ppermute x1, starting transfers between devices, column(): packed = lax.ppermute(packed, AXES, owners())  8.84 us
    all_to_all x1, starting transfers between devices, local(): lax.all_to_all(amplitudes.reshape(4, 4, LANES, 256), 'x', split_axis=0, c...  4.59 us
    pallas_call x1, Pallas kernels, multiply(): pl.pallas_call(lambda *refs: multiply_kernel(with_sum, *refs), out_shape=...  3.92 us
    ppermute x1, waiting for transfers between devices, column(): packed = lax.ppermute(packed, AXES, owners())  3.22 us
  transfers between devices with their start and end apart: 2, of which 2 were waited for; matrix products, arithmetic and copies ran while one was open for 0% of the time, Pallas kernels for 0%

profile of v1, /device:TPU:1, one launch (start us, length us, event | category | flops | bytes accessed | tf_op | source)
XLA Modules:
  0.0 120.8 jit_solution(18303297698864985253)
XLA Ops:
  0.0 1.7 %pack.2 = (f32[32,128]{1,0:T(8,128)S(1)}, s32[1]{0:T(128)}) custom-call(s32[1]{0:T(128)} %constant.1.clone.1.round_ref.refs_0_, s32[128]{0:T(128)} %refs_1_.1, s32[3]{0:T(128)} %refs_2_.1, s32[2,128]{1,0:T(2,128)} %bitcast.16, s32[1,128]{1,0:T(1,128)} %bitcast.19, f32[4,32,128]{2,1,0:T(8,128)} %w_ref.1), custom_call_target="tpu_custom_call" | custom-call | tf_op jit(solution)/shard_map/pack/pallas_call | solution.py:107
  1.7 8.8 %collective-permute-start.1 = (f32[32,128]{1,0:T(8,128)S(1)}, f32[32,128]{1,0:T(8,128)S(1)}, u32[]{:S(2)}, u32[]{:S(2)}) collective-permute-start(f32[32,128]{1,0:T(8,128)S(1)} %get-tuple-element.56), channel_id=1, source_target_pairs={{0,0},{1,32},{2,64},{3,96},{4,128},{5,160},{6,192},{7,224},{8,256}... | collective-permute-start | bytes 49160 | tf_op jit(solution)/shard_map/ppermute | solution.py:152
  10.6 3.2 %collective-permute-done.1 = f32[32,128]{1,0:T(8,128)S(1)} collective-permute-done((f32[32,128]{1,0:T(8,128)S(1)}, f32[32,128]{1,0:T(8,128)S(1)}, u32[]{:S(2)}, u32[]{:S(2)}) %collective-permute-start.1) | collective-permute-done | bytes 16416 | tf_op jit(solution)/shard_map/ppermute | solution.py:152
  13.8 42.2 %all_to_all.21 = f32[24,32,128]{2,1,0:T(8,128)S(1)} all-to-all(f32[24,32,128]{2,1,0:T(8,128)S(1)} %broadcast_in_dim.8), channel_id=1, replica_groups=mesh['z'=12,'y_hi'=2,'x'=4,'y_lo'=4,'core'=2] {'z','y_hi'}, dimensions={0} | all-to-all | bytes 786432 | tf_op jit(solution)/shard_map/all_to_all | solution.py:154
  56.0 0.0 copy-start.1
  56.0 0.0 copy-start.2
  56.0 0.0 copy-start.3
  56.0 0.0 copy-start.4
  56.0 4.6 %all-to-all-start.2 = ((f32[4,4,128,256]{3,2,1,0:T(8,128)}), f32[4,4,128,256]{3,2,1,0:T(8,128)}, u32[]{:S(2)}, u32[]{:S(2)}) async-start(f32[4,4,128,256]{3,2,1,0:T(8,128)} %bitcast.15), calls=%async_computation.2 | async-start | bytes 4194304 | tf_op jit(solution)/shard_map/all_to_all | solution.py:158
  60.6 20.7 %all-to-all-done.2.refs_6_ = f32[4,4,128,256]{3,2,1,0:T(8,128)} async-done(((f32[4,4,128,256]{3,2,1,0:T(8,128)}), f32[4,4,128,256]{3,2,1,0:T(8,128)}, u32[]{:S(2)}, u32[]{:S(2)}) %all-to-all-start.2) | async-done | bytes 2097184 | tf_op jit(solution)/shard_map/all_to_all | solution.py:158
  81.3 0.0 copy-done.1
  81.3 0.0 copy-done.2
  81.3 0.0 copy-done.3
  81.3 0.0 copy-done.4
  81.4 0.0 copy-start
  81.4 3.9 %multiply.2 = f32[32,3,16,128]{3,2,1,0:T(8,128)S(1)} custom-call(s32[1]{0:T(128)} %constant.1.clone.1.round_ref.refs_0_, s32[128]{0:T(128)S(1)} %copy-done.2, s32[3]{0:T(128)S(1)} %copy-done.3, s32[2,128]{1,0:T(2,128)S(1)} %bitcast.17, s32[1,128]{1,0:T(1,128)S(1)} %bitcast.20, f32[3,256,128]{2,1,0:T(8,128)S(1)} %bitcast.14, ...), custom_call_target="tpu_custom_call" | custom-call | flops 1207959552 | bytes 4194304 | tf_op jit(solution)/shard_map/multiply/pallas_call | solution.py:120
  85.3 0.0 copy-done
  85.3 0.7 while.10
  86.0 34.1 %all_to_all.22 = f32[32,3,16,128]{3,2,1,0:T(8,128)S(1)} all-to-all(f32[32,3,16,128]{3,2,1,0:T(8,128)S(1)} %get-tuple-element.58), channel_id=1, replica_groups=mesh['z'=12,'y_hi'=2,'x'=4,'y_lo'=4,'core'=2] {'x','y_lo','core'}, dimensions={0} | all-to-all | bytes 1572864 | tf_op jit(solution)/shard_map/all_to_all | solution.py:166
  120.1 0.7 reduce_sum.9
  (1 shorter events, 0.0 us)
Async XLA Ops:
  1.7 12.1 %collective-permute-start.1 = (f32[32,128]{1,0:T(8,128)S(1)}, f32[32,128]{1,0:T(8,128)S(1)}, u32[]{:S(2)}, u32[]{:S(2)}) collective-permute-start(f32[32,128]{1,0:T(8,128)S(1)} %get-tuple-element.56), channel_id=1, source_target_pairs={{0,0},{1,32},{2,64},{3,96},{4,128},{5,160},{6,192},{7,224},{8,256}... | collective-permute-start | bytes 49160 | tf_op jit(solution)/shard_map/ppermute | solution.py:152
  56.0 25.4 %copy-start.1 = (s32[256]{0:T(256)S(1)}, s32[256]{0:T(256)}, u32[]{:S(2)}) copy-start(s32[256]{0:T(256)} %param.12) | copy-start | bytes 3076
  56.0 25.4 %copy-start.2 = (s32[128]{0:T(128)S(1)}, s32[128]{0:T(128)}, u32[]{:S(2)}) copy-start(s32[128]{0:T(128)} %refs_1_.1) | copy-start | bytes 1540
  56.0 25.4 %copy-start.3 = (s32[3]{0:T(128)S(1)}, s32[3]{0:T(128)}, u32[]{:S(2)}) copy-start(s32[3]{0:T(128)} %refs_2_.1) | copy-start | bytes 40
  56.0 25.4 %copy-start.4 = (s32[128]{0:T(128)S(1)}, s32[128]{0:T(128)}, u32[]{:S(2)}) copy-start(s32[128]{0:T(128)} %param.13) | copy-start | bytes 1540
  56.0 25.3 %all-to-all-start.2 = ((f32[4,4,128,256]{3,2,1,0:T(8,128)}), f32[4,4,128,256]{3,2,1,0:T(8,128)}, u32[]{:S(2)}, u32[]{:S(2)}) async-start(f32[4,4,128,256]{3,2,1,0:T(8,128)} %bitcast.15), calls=%async_computation.2 | async-start | bytes 4194304 | tf_op jit(solution)/shard_map/all_to_all | solution.py:158
  81.4 3.9 %copy-start = (f32[4,32,128]{2,1,0:T(8,128)S(1)}, f32[4,32,128]{2,1,0:T(8,128)}, u32[]{:S(2)}) copy-start(f32[4,32,128]{2,1,0:T(8,128)} %w_ref.1) | copy-start | bytes 196612

commit v2 on v1

--- a/solution.py
+++ b/solution.py
@@ -66,7 +66,8 @@
     return high, (values - high.astype(jnp.float32)).astype(jnp.bfloat16)
 
 
-def multiply_kernel(with_sum, round_ref, occ_ref, j_ref, vir_ref, b_ref, w_ref, t_ref, *rest):
+def multiply_kernel(with_sum, round_ref, occ_ref, j_ref, vir_ref, b_ref, w_ref, *rest):
+    t_refs, rest = rest[:4], rest[4:]
     if with_sum:
         sum_ref, out_ref, w_high, w_low, t_high, t_low = rest
     else:
@@ -85,18 +86,22 @@
             for piece, target in zip(split[group], (w_high, w_low)):
                 spread = jnp.dot(piece, puts[part], preferred_element_type=jnp.float32)
                 target[k * 256:(k + 1) * 256, j * LANES:(j + 1) * LANES] = jnp.where(keep, spread, 0.0).astype(jnp.bfloat16)
-        high, low = halves(t_ref[:, k].reshape(4 * LANES, 256))
-        t_high[:, k * 256:(k + 1) * 256] = high
-        t_low[:, k * 256:(k + 1) * 256] = low
+        for shift, t_ref in enumerate(t_refs):
+            high, low = halves(t_ref[k])
+            t_high[shift * LANES:(shift + 1) * LANES, k * 256:(k + 1) * 256] = high
+            t_low[shift * LANES:(shift + 1) * LANES, k * 256:(k + 1) * 256] = low
     total = jnp.dot(t_high[...], w_high[...], preferred_element_type=jnp.float32)
     total = total + jnp.dot(t_high[...], w_low[...], preferred_element_type=jnp.float32)
     total = total + jnp.dot(t_low[...], w_high[...], preferred_element_type=jnp.float32)
-    for block in range(32):
-        for j in range(J):
-            piece = total[block * 16:(block + 1) * 16, j * LANES:(j + 1) * LANES]
-            if with_sum:
-                piece = piece + sum_ref[block, j]
-            out_ref[block, j] = piece
+    for shift in range(4):
+        source = lax.rem(lax.axis_index("x") + 4 - shift, 4)
+        for tile in range(8):
+            top = shift * LANES + tile * 16
+            for j in range(J):
+                piece = total[top:top + 16, j * LANES:(j + 1) * LANES]
+                if with_sum:
+                    piece = piece + sum_ref[source * 8 + tile, j]
+                out_ref[source * 8 + tile, j] = piece
 
 
 SMEM = pl.BlockSpec(memory_space=pltpu.SMEM)
@@ -120,7 +125,7 @@
     return pl.pallas_call(
         lambda *refs: multiply_kernel(with_sum, *refs),
         out_shape=jax.ShapeDtypeStruct((32, J, 16, LANES), jnp.float32),
-        in_specs=[SMEM, SMEM, SMEM, VMEM, VMEM, VMEM, VMEM] + [VMEM] * with_sum,
+        in_specs=[SMEM] * 3 + [VMEM] * 7 + [VMEM] * with_sum,
         out_specs=VMEM,
         scratch_shapes=[
             pltpu.VMEM((1024, J * LANES), jnp.bfloat16),
@@ -131,7 +136,7 @@
         compiler_params=pltpu.CompilerParams(vmem_limit_bytes=24 << 20),
         cost_estimate=pl.CostEstimate(flops=3 * 2 * 512 * 1024 * 384, bytes_accessed=4 << 20, transcendentals=0),
         name="multiply",
-    )(round_index, occ, j, vir, b, w, t, *([total] if with_sum else []))
+    )(round_index, occ, j, vir, b, w, *t, *([total] if with_sum else []))
 
 
 def owners():
@@ -155,7 +160,11 @@
         return gathered.reshape(3, 256, LANES), rounds
 
     w, rounds = column(jnp.zeros((1,), jnp.int32))
-    t = lax.all_to_all(amplitudes.reshape(4, 4, LANES, 256), "x", split_axis=0, concat_axis=0, tiled=True)
+    x = lax.axis_index("x")
+    t = []
+    for shift in range(4):
+        piece = lax.dynamic_slice_in_dim(amplitudes[0], lax.rem(x + shift, 4) * 4, 4)
+        t.append(lax.ppermute(piece, "x", [(s, (s + shift) % 4) for s in range(4)]) if shift else piece)
     total = multiply(jnp.zeros((1,), jnp.int32), *labels, w, t)
 
     def another(state):

time: 121 us -> 103 us (0.85)
  blocking collectives: 76.3 us -> 27.9 us
  starting transfers between devices: 13.4 us -> 41.7 us
  local copies, waits for them, and re-layouts: 0.05 us -> 2.56 us
    all_to_all x1 -> x0, blocking collectives: 42.2 us -> none  [column(): lax.all_to_all(copies, HOPS, split_axis=0, concat_axis=0, tiled=True)]
    all_to_all x1, waiting for transfers between devices: 20.7 us -> 0.01 us  [column(): lax.all_to_all(copies, HOPS, split_axis=0, concat_axis=0, tiled=True)]
    ppermute x0 -> x3, waiting for transfers between devices: none -> 20.3 us  [local(): lax.ppermute(piece, 'x', [(s, (s + shift) % 4) for s in range(4)])]
    all_to_all x1, starting transfers between devices: 4.59 us -> 23.5 us  [column(): lax.all_to_all(copies, HOPS, split_axis=0, concat_axis=0, tiled=True)]
    ppermute x0 -> x3, starting transfers between devices: none -> 9.35 us  [local(): lax.ppermute(piece, 'x', [(s, (s + shift) % 4) for s in range(4)])]
    all_to_all x1, blocking collectives: 34.1 us -> 27.9 us  [local(): lax.all_to_all(total, PLANE, split_axis=0, concat_axis=0, tiled=True)]
    dynamic_slice x0 -> x1, local copies, waits for them, and re-layouts: none -> 1.73 us  [local(): lax.dynamic_slice_in_dim(amplitudes[0], lax.rem(x + shift, 4) * 4, 4)]
  transfers between devices with their start and end apart: 2 -> 5, of which waited for: 2 -> 4; matrix products, arithmetic and copies ran while one was open for 0% -> 2% of each run, Pallas kernels for 0% -> 0%
where the time goes in v2:
time: 103 us; the launch traced here: 102 us
  starting transfers between devices  41.7 us (40%)
  blocking collectives  27.9 us (27%)
  waiting for transfers between devices  23.5 us (23%)
  Pallas kernels  5.23 us (5%)
  local copies, waits for them, and re-layouts  2.56 us (2%)
    all_to_all x1, blocking collectives, local(): lax.all_to_all(total, PLANE, split_axis=0, concat_axis=0, tiled=True)  27.9 us
    all_to_all x1, starting transfers between devices, column(): lax.all_to_all(copies, HOPS, split_axis=0, concat_axis=0, tiled=True)  23.5 us
    ppermute x3, waiting for transfers between devices, local(): lax.ppermute(piece, 'x', [(s, (s + shift) % 4) for s in range(4)])  20.3 us
    ppermute x3, starting transfers between devices, local(): lax.ppermute(piece, 'x', [(s, (s + shift) % 4) for s in range(4)])  9.35 us
    ppermute x1, starting transfers between devices, column(): packed = lax.ppermute(packed, AXES, owners())  8.84 us
    pallas_call x1, Pallas kernels, multiply(): pl.pallas_call(lambda *refs: multiply_kernel(with_sum, *refs), out_shape=...  3.53 us
    ppermute x1, waiting for transfers between devices, column(): packed = lax.ppermute(packed, AXES, owners())  3.22 us
  transfers between devices with their start and end apart: 5, of which 4 were waited for; matrix products, arithmetic and copies ran while one was open for 2% of the time, Pallas kernels for 0%

profile of v2, /device:TPU:1, one launch (start us, length us, event | category | flops | bytes accessed | tf_op | source)
XLA Modules:
  0.0 102.3 jit_solution(7004287149997350743)
XLA Ops:
  0.0 1.7 %pack.2 = (f32[32,128]{1,0:T(8,128)S(1)}, s32[1]{0:T(128)}) custom-call(s32[1]{0:T(128)} %constant.27.clone.1.round_ref.refs_0_, s32[128]{0:T(128)} %refs_1_.1, s32[3]{0:T(128)} %refs_2_.1, s32[2,128]{1,0:T(2,128)} %bitcast.22, s32[1,128]{1,0:T(1,128)} %bitcast.25, f32[4,32,128]{2,1,0:T(8,128)} %w_ref.1), custom_call_target="tpu_custom_call" | custom-call | tf_op jit(solution)/shard_map/pack/pallas_call | solution.py:112
  1.7 8.8 %collective-permute-start.1 = (f32[32,128]{1,0:T(8,128)S(1)}, f32[32,128]{1,0:T(8,128)S(1)}, u32[]{:S(2)}, u32[]{:S(2)}) collective-permute-start(f32[32,128]{1,0:T(8,128)S(1)} %get-tuple-element.71), channel_id=1, source_target_pairs={{0,0},{1,32},{2,64},{3,96},{4,128},{5,160},{6,192},{7,224},{8,256}... | collective-permute-start | bytes 49160 | tf_op jit(solution)/shard_map/ppermute | solution.py:157
  10.6 3.2 %collective-permute-done.1 = f32[32,128]{1,0:T(8,128)S(1)} collective-permute-done((f32[32,128]{1,0:T(8,128)S(1)}, f32[32,128]{1,0:T(8,128)S(1)}, u32[]{:S(2)}, u32[]{:S(2)}) %collective-permute-start.1) | collective-permute-done | bytes 16416 | tf_op jit(solution)/shard_map/ppermute | solution.py:157
  13.8 0.8 broadcast_in_dim.8
  14.6 23.5 %all-to-all-start.1 = ((f32[24,32,128]{2,1,0:T(8,128)}), f32[24,32,128]{2,1,0:T(8,128)S(1)}, u32[]{:S(2)}, u32[]{:S(2)}) async-start(f32[24,32,128]{2,1,0:T(8,128)} %broadcast_in_dim.8), calls=%async_computation.1 | async-start | bytes 786432 | tf_op jit(solution)/shard_map/all_to_all | solution.py:159
  38.1 0.0 copy-start.1
  38.1 0.0 copy-start.2
  38.1 0.0 copy-start.3
  38.1 0.0 copy-start.4
  38.2 1.7 %dynamic-slice_bitcast_fusion = (f32[4,128,256]{2,1,0:T(8,128)S(1)}, f32[4,128,256]{2,1,0:T(8,128)S(1)}, f32[4,128,256]{2,1,0:T(8,128)S(1)}, f32[4,128,256]{2,1,0:T(8,128)S(1)}) fusion(f32[1,16,128,256]{3,2,1,0:T(8,128)} %param.8, s32[]{:T(128)S(6)} %select_n.15, s32[]{:T(128)S(6)} %select_n.13, s32[]{:T(128)S(6)} %select_n.12, s32[]{:T(128)S(6)} %select_n.14), kind=kLoop, calls=%fused_computation | loop fusion | bytes 4194320 | tf_op jit(solution)/shard_map/dynamic_slice | solution.py:166
  39.9 3.1 %collective-permute-start.2 = (f32[4,128,256]{2,1,0:T(8,128)S(1)}, f32[4,128,256]{2,1,0:T(8,128)S(1)}, u32[]{:S(2)}, u32[]{:S(2)}) collective-permute-start(f32[4,128,256]{2,1,0:T(8,128)S(1)} %get-tuple-element.99), channel_id=1, source_target_pairs={{0,8},{8,16},{16,24},{24,0},{1,9},{9,17},{17,25},{25,1},{2,10},{10... | collective-permute-start | bytes 1572872 | tf_op jit(solution)/shard_map/ppermute | solution.py:167
  43.0 2.8 %collective-permute-start.3 = (f32[4,128,256]{2,1,0:T(8,128)S(1)}, f32[4,128,256]{2,1,0:T(8,128)}, u32[]{:S(2)}, u32[]{:S(2)}) collective-permute-start(f32[4,128,256]{2,1,0:T(8,128)S(1)} %get-tuple-element.101), channel_id=1, source_target_pairs={{0,16},{8,24},{16,0},{24,8},{1,17},{9,25},{17,1},{25,9},{2,18},{10... | collective-permute-start | bytes 1572872 | tf_op jit(solution)/shard_map/ppermute | solution.py:167
  45.9 3.4 %collective-permute-start.4 = (f32[4,128,256]{2,1,0:T(8,128)S(1)}, f32[4,128,256]{2,1,0:T(8,128)}, u32[]{:S(2)}, u32[]{:S(2)}) collective-permute-start(f32[4,128,256]{2,1,0:T(8,128)S(1)} %get-tuple-element.98), channel_id=1, source_target_pairs={{0,24},{8,0},{16,8},{24,16},{1,25},{9,1},{17,9},{25,17},{2,26},{10... | collective-permute-start | bytes 1572872 | tf_op jit(solution)/shard_map/ppermute | solution.py:167
  49.3 7.3 %collective-permute-done.2.refs_7_ = f32[4,128,256]{2,1,0:T(8,128)S(1)} collective-permute-done((f32[4,128,256]{2,1,0:T(8,128)S(1)}, f32[4,128,256]{2,1,0:T(8,128)S(1)}, u32[]{:S(2)}, u32[]{:S(2)}) %collective-permute-start.2) | collective-permute-done | bytes 524320 | tf_op jit(solution)/shard_map/ppermute | solution.py:167
  56.6 7.9 %collective-permute-done.3.refs_8_ = f32[4,128,256]{2,1,0:T(8,128)} collective-permute-done((f32[4,128,256]{2,1,0:T(8,128)S(1)}, f32[4,128,256]{2,1,0:T(8,128)}, u32[]{:S(2)}, u32[]{:S(2)}) %collective-permute-start.3) | collective-permute-done | bytes 524320 | tf_op jit(solution)/shard_map/ppermute | solution.py:167
  64.5 5.0 %collective-permute-done.4.refs_9_ = f32[4,128,256]{2,1,0:T(8,128)} collective-permute-done((f32[4,128,256]{2,1,0:T(8,128)S(1)}, f32[4,128,256]{2,1,0:T(8,128)}, u32[]{:S(2)}, u32[]{:S(2)}) %collective-permute-start.4) | collective-permute-done | bytes 524320 | tf_op jit(solution)/shard_map/ppermute | solution.py:167
  69.6 0.0 all-to-all-done.1
  69.6 0.0 copy-done.1
  69.6 0.0 copy-done.2
  69.6 0.0 copy-done.3
  69.6 0.0 copy-done.4
  69.6 0.0 copy-start
  69.6 3.5 %multiply.2 = f32[32,3,16,128]{3,2,1,0:T(8,128)S(1)} custom-call(s32[1]{0:T(128)} %constant.27.clone.1.round_ref.refs_0_, s32[128]{0:T(128)S(1)} %copy-done.2, s32[3]{0:T(128)S(1)} %copy-done.3, s32[2,128]{1,0:T(2,128)S(1)} %bitcast.23, s32[1,128]{1,0:T(1,128)S(1)} %bitcast.26, f32[3,256,128]{2,1,0:T(8,128)S(1)} %bitcast.21, ...), custom_call_target="tpu_custom_call" | custom-call | flops 1207959552 | bytes 4194304 | tf_op jit(solution)/shard_map/multiply/pallas_call | solution.py:125
  73.1 0.0 copy-done
  73.1 0.6 while.10
  73.8 27.9 %all_to_all.16 = f32[32,3,16,128]{3,2,1,0:T(8,128)S(1)} all-to-all(f32[32,3,16,128]{3,2,1,0:T(8,128)S(1)} %get-tuple-element.73), channel_id=1, replica_groups=mesh['z'=12,'y_hi'=2,'x'=4,'y_lo'=4,'core'=2] {'x','y_lo','core'}, dimensions={0} | all-to-all | bytes 1572864 | tf_op jit(solution)/shard_map/all_to_all | solution.py:175
  101.7 0.7 reduce_sum.9
Async XLA Ops:
  1.7 12.1 %collective-permute-start.1 = (f32[32,128]{1,0:T(8,128)S(1)}, f32[32,128]{1,0:T(8,128)S(1)}, u32[]{:S(2)}, u32[]{:S(2)}) collective-permute-start(f32[32,128]{1,0:T(8,128)S(1)} %get-tuple-element.71), channel_id=1, source_target_pairs={{0,0},{1,32},{2,64},{3,96},{4,128},{5,160},{6,192},{7,224},{8,256}... | collective-permute-start | bytes 49160 | tf_op jit(solution)/shard_map/ppermute | solution.py:157
  14.6 55.0 %all-to-all-start.1 = ((f32[24,32,128]{2,1,0:T(8,128)}), f32[24,32,128]{2,1,0:T(8,128)S(1)}, u32[]{:S(2)}, u32[]{:S(2)}) async-start(f32[24,32,128]{2,1,0:T(8,128)} %broadcast_in_dim.8), calls=%async_computation.1 | async-start | bytes 786432 | tf_op jit(solution)/shard_map/all_to_all | solution.py:159
  38.1 31.5 %copy-start.1 = (s32[256]{0:T(256)S(1)}, s32[256]{0:T(256)}, u32[]{:S(2)}) copy-start(s32[256]{0:T(256)} %param.12) | copy-start | bytes 3076
  38.1 31.4 %copy-start.2 = (s32[128]{0:T(128)S(1)}, s32[128]{0:T(128)}, u32[]{:S(2)}) copy-start(s32[128]{0:T(128)} %refs_1_.1) | copy-start | bytes 1540
  38.1 31.4 %copy-start.3 = (s32[3]{0:T(128)S(1)}, s32[3]{0:T(128)}, u32[]{:S(2)}) copy-start(s32[3]{0:T(128)} %refs_2_.1) | copy-start | bytes 40
  38.1 31.4 %copy-start.4 = (s32[128]{0:T(128)S(1)}, s32[128]{0:T(128)}, u32[]{:S(2)}) copy-start(s32[128]{0:T(128)} %param.13) | copy-start | bytes 1540
  39.9 16.7 %collective-permute-start.2 = (f32[4,128,256]{2,1,0:T(8,128)S(1)}, f32[4,128,256]{2,1,0:T(8,128)S(1)}, u32[]{:S(2)}, u32[]{:S(2)}) collective-permute-start(f32[4,128,256]{2,1,0:T(8,128)S(1)} %get-tuple-element.99), channel_id=1, source_target_pairs={{0,8},{8,16},{16,24},{24,0},{1,9},{9,17},{17,25},{25,1},{2,10},{10... | collective-permute-start | bytes 1572872 | tf_op jit(solution)/shard_map/ppermute | solution.py:167
  43.0 21.5 %collective-permute-start.3 = (f32[4,128,256]{2,1,0:T(8,128)S(1)}, f32[4,128,256]{2,1,0:T(8,128)}, u32[]{:S(2)}, u32[]{:S(2)}) collective-permute-start(f32[4,128,256]{2,1,0:T(8,128)S(1)} %get-tuple-element.101), channel_id=1, source_target_pairs={{0,16},{8,24},{16,0},{24,8},{1,17},{9,25},{17,1},{25,9},{2,18},{10... | collective-permute-start | bytes 1572872 | tf_op jit(solution)/shard_map/ppermute | solution.py:167
  45.9 23.7 %collective-permute-start.4 = (f32[4,128,256]{2,1,0:T(8,128)S(1)}, f32[4,128,256]{2,1,0:T(8,128)}, u32[]{:S(2)}, u32[]{:S(2)}) collective-permute-start(f32[4,128,256]{2,1,0:T(8,128)S(1)} %get-tuple-element.98), channel_id=1, source_target_pairs={{0,24},{8,0},{16,8},{24,16},{1,25},{9,1},{17,9},{25,17},{2,26},{10... | collective-permute-start | bytes 1572872 | tf_op jit(solution)/shard_map/ppermute | solution.py:167
  69.6 3.6 %copy-start = (f32[4,32,128]{2,1,0:T(8,128)S(1)}, f32[4,32,128]{2,1,0:T(8,128)}, u32[]{:S(2)}) copy-start(f32[4,32,128]{2,1,0:T(8,128)} %w_ref.1) | copy-start | bytes 196612

commit v3 on v2

--- a/solution.py
+++ b/solution.py
@@ -152,24 +152,27 @@
     vir, b = irrep_vir.reshape(2, LANES), irrep_b.reshape(1, LANES)
     labels = (irrep_occ, irrep_j, vir, b)
 
-    def column(round_index):
+    def owned(round_index):
         packed, rounds = pack(round_index, *labels, integrals)
-        packed = lax.ppermute(packed, AXES, owners())
+        return lax.ppermute(packed, AXES, owners()), rounds
+
+    def column(packed):
         copies = jnp.broadcast_to(packed[None], (24, SLAB, LANES))
         gathered = lax.all_to_all(copies, HOPS, split_axis=0, concat_axis=0, tiled=True)
-        return gathered.reshape(3, 256, LANES), rounds
+        return gathered.reshape(3, 256, LANES)
 
-    w, rounds = column(jnp.zeros((1,), jnp.int32))
     x = lax.axis_index("x")
     t = []
     for shift in range(4):
         piece = lax.dynamic_slice_in_dim(amplitudes[0], lax.rem(x + shift, 4) * 4, 4)
         t.append(lax.ppermute(piece, "x", [(s, (s + shift) % 4) for s in range(4)]) if shift else piece)
-    total = multiply(jnp.zeros((1,), jnp.int32), *labels, w, t)
+    packed, rounds = owned(jnp.zeros((1,), jnp.int32))
+    packed, t[1], t[3] = lax.optimization_barrier((packed, t[1], t[3]))
+    total = multiply(jnp.zeros((1,), jnp.int32), *labels, column(packed), t)
 
     def another(state):
         index, total = state
-        return index + 1, multiply(index[None], *labels, column(index[None])[0], t, total)
+        return index + 1, multiply(index[None], *labels, column(owned(index[None])[0]), t, total)
 
     _, total = lax.while_loop(lambda state: state[0] < rounds[0], another, (jnp.int32(1), total))
     parts = lax.all_to_all(total, PLANE, split_axis=0, concat_axis=0, tiled=True)

time: 103 us -> 100 us (0.971)
  waiting for transfers between devices: 23.5 us -> 18.8 us
  blocking collectives: 27.9 us -> 31.6 us
    ppermute x3, waiting for transfers between devices: 20.3 us -> 12.9 us  [local(): lax.ppermute(piece, 'x', [(s, (s + shift) % 4) for s in range(4)])]
    all_to_all x1, blocking collectives: 27.9 us -> 31.6 us  [local(): lax.all_to_all(total, PLANE, split_axis=0, concat_axis=0, tiled=True)]
    all_to_all x1, waiting for transfers between devices: 0.01 us -> 2.66 us  [column(): lax.all_to_all(copies, HOPS, split_axis=0, concat_axis=0, tiled=True)]
  transfers between devices with their start and end apart: 5 -> 5, of which waited for: 4 -> 3; matrix products, arithmetic and copies ran while one was open for 2% -> 0% of each run, Pallas kernels for 0% -> 1%
where the time goes in v3:
time: 100 us
  starting transfers between devices  40.8 us (41%)
  blocking collectives  31.6 us (32%)
  waiting for transfers between devices  18.8 us (19%)
  Pallas kernels  4.89 us (5%)
  local copies, waits for them, and re-layouts  2.6 us (3%)
    all_to_all x1, blocking collectives, local(): lax.all_to_all(total, PLANE, split_axis=0, concat_axis=0, tiled=True)  31.6 us
    all_to_all x1, starting transfers between devices, column(): lax.all_to_all(copies, HOPS, split_axis=0, concat_axis=0, tiled=True)  22.9 us
    ppermute x3, waiting for transfers between devices, local(): lax.ppermute(piece, 'x', [(s, (s + shift) % 4) for s in range(4)])  12.9 us
    ppermute x3, starting transfers between devices, local(): lax.ppermute(piece, 'x', [(s, (s + shift) % 4) for s in range(4)])  9.06 us
    ppermute x1, starting transfers between devices, owned(): return (lax.ppermute(packed, AXES, owners()), rounds)  8.76 us
    pallas_call x1, Pallas kernels, multiply(): pl.pallas_call(lambda *refs: multiply_kernel(with_sum, *refs), out_shape=...  3.5 us
    ppermute x1, waiting for transfers between devices, owned(): return (lax.ppermute(packed, AXES, owners()), rounds)  3.22 us
    all_to_all x1, waiting for transfers between devices, column(): lax.all_to_all(copies, HOPS, split_axis=0, concat_axis=0, tiled=True)  2.66 us
  transfers between devices with their start and end apart: 5, of which 3 were waited for; matrix products, arithmetic and copies ran while one was open for 0% of the time, Pallas kernels for 1%

profile of v3, /device:TPU:1, one launch (start us, length us, event | category | flops | bytes accessed | tf_op | source)
XLA Modules:
  0.0 100.0 jit_solution(7312481543567338952)
XLA Ops:
  0.0 0.0 copy-start
  0.0 0.0 copy-start.1
  0.0 0.0 copy-start.2
  0.0 0.0 copy-start.3
  0.0 0.0 copy-start.4
  0.0 1.8 %dynamic-slice_bitcast_fusion = (f32[4,128,256]{2,1,0:T(8,128)S(1)}, f32[4,128,256]{2,1,0:T(8,128)S(1)}, f32[4,128,256]{2,1,0:T(8,128)S(1)}, f32[4,128,256]{2,1,0:T(8,128)S(1)}) fusion(f32[1,16,128,256]{3,2,1,0:T(8,128)} %param.8, s32[]{:T(128)S(6)} %select_n.15, s32[]{:T(128)S(6)} %select_n.13, s32[]{:T(128)S(6)} %select_n.12, s32[]{:T(128)S(6)} %select_n.14), kind=kLoop, calls=%fused_computation | loop fusion | bytes 4194320 | tf_op jit(solution)/shard_map/dynamic_slice | solution.py:167
  1.8 3.9 %collective-permute-start.2 = (f32[4,128,256]{2,1,0:T(8,128)S(1)}, f32[4,128,256]{2,1,0:T(8,128)S(1)}, u32[]{:S(2)}, u32[]{:S(2)}) collective-permute-start(f32[4,128,256]{2,1,0:T(8,128)S(1)} %get-tuple-element.106), channel_id=1, source_target_pairs={{0,8},{8,16},{16,24},{24,0},{1,9},{9,17},{17,25},{25,1},{2,10},{10... | collective-permute-start | bytes 1572872 | tf_op jit(solution)/shard_map/ppermute | solution.py:168
  5.8 3.2 %collective-permute-start.3 = (f32[4,128,256]{2,1,0:T(8,128)S(1)}, f32[4,128,256]{2,1,0:T(8,128)}, u32[]{:S(2)}, u32[]{:S(2)}) collective-permute-start(f32[4,128,256]{2,1,0:T(8,128)S(1)} %get-tuple-element.105), channel_id=1, source_target_pairs={{0,24},{8,0},{16,8},{24,16},{1,25},{9,1},{17,9},{25,17},{2,26},{10... | collective-permute-start | bytes 1572872 | tf_op jit(solution)/shard_map/ppermute | solution.py:168
  9.0 0.0 copy-done
  9.0 0.0 copy-done.1
  9.0 0.0 copy-done.2
  9.0 0.0 copy-done.3
  9.0 0.0 copy-done.4
  9.0 1.4 %pack.2 = (f32[32,128]{1,0:T(8,128)S(1)}, s32[1]{0:T(128)}) custom-call(s32[1]{0:T(128)} %constant.27.clone.1.round_ref.refs_0_, s32[128]{0:T(128)S(1)} %copy-done.2, s32[3]{0:T(128)S(1)} %copy-done.3, s32[2,128]{1,0:T(2,128)S(1)} %bitcast.22, s32[1,128]{1,0:T(1,128)S(1)} %bitcast.25, f32[4,32,128]{2,1,0:T(8,128)S(1)} %copy-done), custom_call_target="tpu_custom_call" | custom-call | tf_op jit(solution)/shard_map/pack/pallas_call | solution.py:112
  10.4 8.8 %collective-permute-start.1 = (f32[32,128]{1,0:T(8,128)S(1)}, f32[32,128]{1,0:T(8,128)S(1)}, u32[]{:S(2)}, u32[]{:S(2)}) collective-permute-start(f32[32,128]{1,0:T(8,128)S(1)} %get-tuple-element.74), channel_id=1, source_target_pairs={{0,0},{1,32},{2,64},{3,96},{4,128},{5,160},{6,192},{7,224},{8,256}... | collective-permute-start | bytes 49160 | tf_op jit(solution)/shard_map/ppermute | solution.py:157
  19.2 3.2 %collective-permute-done.1 = f32[32,128]{1,0:T(8,128)S(1)} collective-permute-done((f32[32,128]{1,0:T(8,128)S(1)}, f32[32,128]{1,0:T(8,128)S(1)}, u32[]{:S(2)}, u32[]{:S(2)}) %collective-permute-start.1) | collective-permute-done | bytes 16416 | tf_op jit(solution)/shard_map/ppermute | solution.py:157
  22.4 0.0 collective-permute-done.2.refs_7_
  22.4 0.0 collective-permute-done.3.refs_9_
  22.4 0.8 broadcast_in_dim.8
  23.2 22.9 %all-to-all-start.1 = ((f32[24,32,128]{2,1,0:T(8,128)}), f32[24,32,128]{2,1,0:T(8,128)S(1)}, u32[]{:S(2)}, u32[]{:S(2)}) async-start(f32[24,32,128]{2,1,0:T(8,128)} %broadcast_in_dim.8), calls=%async_computation.1 | async-start | bytes 786432 | tf_op jit(solution)/shard_map/all_to_all | solution.py:161
  46.2 1.9 %collective-permute-start.4 = (f32[4,128,256]{2,1,0:T(8,128)S(1)}, f32[4,128,256]{2,1,0:T(8,128)}, u32[]{:S(2)}, u32[]{:S(2)}) collective-permute-start(f32[4,128,256]{2,1,0:T(8,128)S(1)} %get-tuple-element.104), channel_id=1, source_target_pairs={{0,16},{8,24},{16,0},{24,8},{1,17},{9,25},{17,1},{25,9},{2,18},{10... | collective-permute-start | bytes 1572872 | tf_op jit(solution)/shard_map/ppermute | solution.py:168
  48.1 12.9 %collective-permute-done.4.refs_8_ = f32[4,128,256]{2,1,0:T(8,128)} collective-permute-done((f32[4,128,256]{2,1,0:T(8,128)S(1)}, f32[4,128,256]{2,1,0:T(8,128)}, u32[]{:S(2)}, u32[]{:S(2)}) %collective-permute-start.4) | collective-permute-done | bytes 524320 | tf_op jit(solution)/shard_map/ppermute | solution.py:168
  61.0 2.7 %all-to-all-done.1 = f32[24,32,128]{2,1,0:T(8,128)S(1)} async-done(((f32[24,32,128]{2,1,0:T(8,128)}), f32[24,32,128]{2,1,0:T(8,128)S(1)}, u32[]{:S(2)}, u32[]{:S(2)}) %all-to-all-start.1) | async-done | bytes 393248 | tf_op jit(solution)/shard_map/all_to_all | solution.py:161
  63.6 3.5 %multiply.2 = f32[32,3,16,128]{3,2,1,0:T(8,128)S(1)} custom-call(s32[1]{0:T(128)} %constant.27.clone.1.round_ref.refs_0_, s32[128]{0:T(128)S(1)} %copy-done.2, s32[3]{0:T(128)S(1)} %copy-done.3, s32[2,128]{1,0:T(2,128)S(1)} %bitcast.23, s32[1,128]{1,0:T(1,128)S(1)} %bitcast.26, f32[3,256,128]{2,1,0:T(8,128)S(1)} %bitcast.21, ...), custom_call_target="tpu_custom_call" | custom-call | flops 1207959552 | bytes 4194304 | tf_op jit(solution)/shard_map/multiply/pallas_call | solution.py:125
  67.1 0.6 while.10
  67.8 31.6 %all_to_all.16 = f32[32,3,16,128]{3,2,1,0:T(8,128)S(1)} all-to-all(f32[32,3,16,128]{3,2,1,0:T(8,128)S(1)} %get-tuple-element.79), channel_id=1, replica_groups=mesh['z'=12,'y_hi'=2,'x'=4,'y_lo'=4,'core'=2] {'x','y_lo','core'}, dimensions={0} | all-to-all | bytes 1572864 | tf_op jit(solution)/shard_map/all_to_all | solution.py:178
  99.4 0.7 reduce_sum.9
Async XLA Ops:
  0.0 9.0 %copy-start = (f32[4,32,128]{2,1,0:T(8,128)S(1)}, f32[4,32,128]{2,1,0:T(8,128)}, u32[]{:S(2)}) copy-start(f32[4,32,128]{2,1,0:T(8,128)} %w_ref.1) | copy-start | bytes 196612
  0.0 9.0 %copy-start.1 = (s32[256]{0:T(256)S(1)}, s32[256]{0:T(256)}, u32[]{:S(2)}) copy-start(s32[256]{0:T(256)} %param.12) | copy-start | bytes 3076
  0.0 9.0 %copy-start.2 = (s32[128]{0:T(128)S(1)}, s32[128]{0:T(128)}, u32[]{:S(2)}) copy-start(s32[128]{0:T(128)} %refs_1_.1) | copy-start | bytes 1540
  0.0 9.0 %copy-start.3 = (s32[3]{0:T(128)S(1)}, s32[3]{0:T(128)}, u32[]{:S(2)}) copy-start(s32[3]{0:T(128)} %refs_2_.1) | copy-start | bytes 40
  0.0 9.0 %copy-start.4 = (s32[128]{0:T(128)S(1)}, s32[128]{0:T(128)}, u32[]{:S(2)}) copy-start(s32[128]{0:T(128)} %param.13) | copy-start | bytes 1540
  1.8 20.6 %collective-permute-start.2 = (f32[4,128,256]{2,1,0:T(8,128)S(1)}, f32[4,128,256]{2,1,0:T(8,128)S(1)}, u32[]{:S(2)}, u32[]{:S(2)}) collective-permute-start(f32[4,128,256]{2,1,0:T(8,128)S(1)} %get-tuple-element.106), channel_id=1, source_target_pairs={{0,8},{8,16},{16,24},{24,0},{1,9},{9,17},{17,25},{25,1},{2,10},{10... | collective-permute-start | bytes 1572872 | tf_op jit(solution)/shard_map/ppermute | solution.py:168
  5.8 16.6 %collective-permute-start.3 = (f32[4,128,256]{2,1,0:T(8,128)S(1)}, f32[4,128,256]{2,1,0:T(8,128)}, u32[]{:S(2)}, u32[]{:S(2)}) collective-permute-start(f32[4,128,256]{2,1,0:T(8,128)S(1)} %get-tuple-element.105), channel_id=1, source_target_pairs={{0,24},{8,0},{16,8},{24,16},{1,25},{9,1},{17,9},{25,17},{2,26},{10... | collective-permute-start | bytes 1572872 | tf_op jit(solution)/shard_map/ppermute | solution.py:168
  10.4 12.0 %collective-permute-start.1 = (f32[32,128]{1,0:T(8,128)S(1)}, f32[32,128]{1,0:T(8,128)S(1)}, u32[]{:S(2)}, u32[]{:S(2)}) collective-permute-start(f32[32,128]{1,0:T(8,128)S(1)} %get-tuple-element.74), channel_id=1, source_target_pairs={{0,0},{1,32},{2,64},{3,96},{4,128},{5,160},{6,192},{7,224},{8,256}... | collective-permute-start | bytes 49160 | tf_op jit(solution)/shard_map/ppermute | solution.py:157
  23.2 40.4 %all-to-all-start.1 = ((f32[24,32,128]{2,1,0:T(8,128)}), f32[24,32,128]{2,1,0:T(8,128)S(1)}, u32[]{:S(2)}, u32[]{:S(2)}) async-start(f32[24,32,128]{2,1,0:T(8,128)} %broadcast_in_dim.8), calls=%async_computation.1 | async-start | bytes 786432 | tf_op jit(solution)/shard_map/all_to_all | solution.py:161
  46.2 14.8 %collective-permute-start.4 = (f32[4,128,256]{2,1,0:T(8,128)S(1)}, f32[4,128,256]{2,1,0:T(8,128)}, u32[]{:S(2)}, u32[]{:S(2)}) collective-permute-start(f32[4,128,256]{2,1,0:T(8,128)S(1)} %get-tuple-element.104), channel_id=1, source_target_pairs={{0,16},{8,24},{16,0},{24,8},{1,17},{9,25},{17,1},{25,9},{2,18},{10... | collective-permute-start | bytes 1572872 | tf_op jit(solution)/shard_map/ppermute | solution.py:168

commit v4 on v3

--- a/solution.py
+++ b/solution.py
@@ -12,7 +12,7 @@
 SLAB = 32
 PLACES = 32
 HOPS = ("z", "y_hi")
-PLANE = ("x", "y_lo", "core")
+PLANE = ("x", "y_lo")
 AXES = ("z", "y_hi", "x", "y_lo", "core")
 
 
@@ -100,8 +100,8 @@
             for j in range(J):
                 piece = total[top:top + 16, j * LANES:(j + 1) * LANES]
                 if with_sum:
-                    piece = piece + sum_ref[source * 8 + tile, j]
-                out_ref[source * 8 + tile, j] = piece
+                    piece = piece + sum_ref[tile % 2, source * 4 + tile // 2, j]
+                out_ref[tile % 2, source * 4 + tile // 2, j] = piece
 
 
 SMEM = pl.BlockSpec(memory_space=pltpu.SMEM)
@@ -124,7 +124,7 @@
     with_sum = total is not None
     return pl.pallas_call(
         lambda *refs: multiply_kernel(with_sum, *refs),
-        out_shape=jax.ShapeDtypeStruct((32, J, 16, LANES), jnp.float32),
+        out_shape=jax.ShapeDtypeStruct((2, 16, J, 16, LANES), jnp.float32),
         in_specs=[SMEM] * 3 + [VMEM] * 7 + [VMEM] * with_sum,
         out_specs=VMEM,
         scratch_shapes=[
@@ -175,6 +175,10 @@
         return index + 1, multiply(index[None], *labels, column(owned(index[None])[0]), t, total)
 
     _, total = lax.while_loop(lambda state: state[0] < rounds[0], another, (jnp.int32(1), total))
+    core = lax.axis_index("core")
+    given = lax.dynamic_index_in_dim(total, 1 - core, keepdims=False)
+    own = lax.dynamic_index_in_dim(total, core, keepdims=False)
+    total = own + lax.ppermute(given, "core", [(0, 1), (1, 0)])
     parts = lax.all_to_all(total, PLANE, split_axis=0, concat_axis=0, tiled=True)
     return jnp.sum(parts, axis=0, keepdims=True)
 

time: 100 us -> 94.5 us (0.945)
  blocking collectives: 31.6 us -> 15.8 us
  starting transfers between devices: 40.8 us -> 49.1 us
  waiting for transfers between devices: 18.8 us -> 20.1 us
    all_to_all x1, blocking collectives: 31.6 us -> 15.8 us  [local(): lax.all_to_all(total, PLANE, split_axis=0, concat_axis=0, tiled=True)]
    ppermute x0 -> x1, starting transfers between devices: none -> 8.38 us  [local(): total = own + lax.ppermute(given, 'core', [(0, 1), (1, 0)])]
    ppermute x0 -> x1, waiting for transfers between devices: none -> 1.33 us  [local(): total = own + lax.ppermute(given, 'core', [(0, 1), (1, 0)])]
  transfers between devices with their start and end apart: 5 -> 6, of which waited for: 3 -> 4; matrix products, arithmetic and copies ran while one was open for 0% -> 0% of each run, Pallas kernels for 1% -> 1%
where the time goes in v4:
time: 94.5 us; the launch traced here: 94 us
  starting transfers between devices  49.1 us (52%)
  waiting for transfers between devices  20.1 us (21%)
  blocking collectives  15.8 us (17%)
  Pallas kernels  4.89 us (5%)
  local copies, waits for them, and re-layouts  2.64 us (3%)
    all_to_all x1, starting transfers between devices, column(): lax.all_to_all(copies, HOPS, split_axis=0, concat_axis=0, tiled=True)  22.9 us
    all_to_all x1, blocking collectives, local(): lax.all_to_all(total, PLANE, split_axis=0, concat_axis=0, tiled=True)  15.8 us
    ppermute x3, waiting for transfers between devices, local(): lax.ppermute(piece, 'x', [(s, (s + shift) % 4) for s in range(4)])  12.9 us
    ppermute x3, starting transfers between devices, local(): lax.ppermute(piece, 'x', [(s, (s + shift) % 4) for s in range(4)])  9.06 us
    ppermute x1, starting transfers between devices, owned(): return (lax.ppermute(packed, AXES, owners()), rounds)  8.76 us
    ppermute x1, starting transfers between devices, local(): total = own + lax.ppermute(given, 'core', [(0, 1), (1, 0)])  8.38 us
    pallas_call x1, Pallas kernels, multiply(): pl.pallas_call(lambda *refs: multiply_kernel(with_sum, *refs), out_shape=...  3.5 us
    ppermute x1, waiting for transfers between devices, owned(): return (lax.ppermute(packed, AXES, owners()), rounds)  3.22 us
  transfers between devices with their start and end apart: 6, of which 4 were waited for; matrix products, arithmetic and copies ran while one was open for 0% of the time, Pallas kernels for 1%

profile of v4, /device:TPU:1, one launch (start us, length us, event | category | flops | bytes accessed | tf_op | source)
XLA Modules:
  0.0 94.0 jit_solution(14467512902931754434)
XLA Ops:
  0.0 0.0 copy-start
  0.0 0.0 copy-start.1
  0.0 0.0 copy-start.2
  0.0 0.0 copy-start.3
  0.0 0.0 copy-start.4
  0.0 1.8 %dynamic-slice_bitcast_fusion = (f32[4,128,256]{2,1,0:T(8,128)S(1)}, f32[4,128,256]{2,1,0:T(8,128)S(1)}, f32[4,128,256]{2,1,0:T(8,128)S(1)}, f32[4,128,256]{2,1,0:T(8,128)S(1)}) fusion(f32[1,16,128,256]{3,2,1,0:T(8,128)} %param.8, s32[]{:T(128)S(6)} %select_n.22, s32[]{:T(128)S(6)} %select_n.20, s32[]{:T(128)S(6)} %select_n.19, s32[]{:T(128)S(6)} %select_n.21), kind=kLoop, calls=%fused_computation | loop fusion | bytes 4194320 | tf_op jit(solution)/shard_map/dynamic_slice | solution.py:167
  1.8 3.9 %collective-permute-start.2 = (f32[4,128,256]{2,1,0:T(8,128)S(1)}, f32[4,128,256]{2,1,0:T(8,128)S(1)}, u32[]{:S(2)}, u32[]{:S(2)}) collective-permute-start(f32[4,128,256]{2,1,0:T(8,128)S(1)} %get-tuple-element.106), channel_id=1, source_target_pairs={{0,8},{8,16},{16,24},{24,0},{1,9},{9,17},{17,25},{25,1},{2,10},{10... | collective-permute-start | bytes 1572872 | tf_op jit(solution)/shard_map/ppermute | solution.py:168
  5.8 3.2 %collective-permute-start.3 = (f32[4,128,256]{2,1,0:T(8,128)S(1)}, f32[4,128,256]{2,1,0:T(8,128)}, u32[]{:S(2)}, u32[]{:S(2)}) collective-permute-start(f32[4,128,256]{2,1,0:T(8,128)S(1)} %get-tuple-element.105), channel_id=1, source_target_pairs={{0,24},{8,0},{16,8},{24,16},{1,25},{9,1},{17,9},{25,17},{2,26},{10... | collective-permute-start | bytes 1572872 | tf_op jit(solution)/shard_map/ppermute | solution.py:168
  9.0 0.0 copy-done
  9.0 0.0 copy-done.1
  9.0 0.0 copy-done.2
  9.0 0.0 copy-done.3
  9.0 0.0 copy-done.4
  9.0 1.4 %pack.2 = (f32[32,128]{1,0:T(8,128)S(1)}, s32[1]{0:T(128)}) custom-call(s32[1]{0:T(128)} %constant.37.clone.1.round_ref.refs_0_, s32[128]{0:T(128)S(1)} %copy-done.2, s32[3]{0:T(128)S(1)} %copy-done.3, s32[2,128]{1,0:T(2,128)S(1)} %bitcast.26, s32[1,128]{1,0:T(1,128)S(1)} %bitcast.29, f32[4,32,128]{2,1,0:T(8,128)S(1)} %copy-done), custom_call_target="tpu_custom_call" | custom-call | tf_op jit(solution)/shard_map/pack/pallas_call | solution.py:112
  10.4 8.8 %collective-permute-start.1 = (f32[32,128]{1,0:T(8,128)S(1)}, f32[32,128]{1,0:T(8,128)S(1)}, u32[]{:S(2)}, u32[]{:S(2)}) collective-permute-start(f32[32,128]{1,0:T(8,128)S(1)} %get-tuple-element.74), channel_id=1, source_target_pairs={{0,0},{1,32},{2,64},{3,96},{4,128},{5,160},{6,192},{7,224},{8,256}... | collective-permute-start | bytes 49160 | tf_op jit(solution)/shard_map/ppermute | solution.py:157
  19.2 3.2 %collective-permute-done.1 = f32[32,128]{1,0:T(8,128)S(1)} collective-permute-done((f32[32,128]{1,0:T(8,128)S(1)}, f32[32,128]{1,0:T(8,128)S(1)}, u32[]{:S(2)}, u32[]{:S(2)}) %collective-permute-start.1) | collective-permute-done | bytes 16416 | tf_op jit(solution)/shard_map/ppermute | solution.py:157
  22.4 0.0 collective-permute-done.2.refs_7_
  22.4 0.0 collective-permute-done.3.refs_9_
  22.4 0.8 broadcast_in_dim.8
  23.2 22.9 %all-to-all-start.1 = ((f32[24,32,128]{2,1,0:T(8,128)}), f32[24,32,128]{2,1,0:T(8,128)S(1)}, u32[]{:S(2)}, u32[]{:S(2)}) async-start(f32[24,32,128]{2,1,0:T(8,128)} %broadcast_in_dim.8), calls=%async_computation.1 | async-start | bytes 786432 | tf_op jit(solution)/shard_map/all_to_all | solution.py:161
  46.2 1.9 %collective-permute-start.4 = (f32[4,128,256]{2,1,0:T(8,128)S(1)}, f32[4,128,256]{2,1,0:T(8,128)}, u32[]{:S(2)}, u32[]{:S(2)}) collective-permute-start(f32[4,128,256]{2,1,0:T(8,128)S(1)} %get-tuple-element.104), channel_id=1, source_target_pairs={{0,16},{8,24},{16,0},{24,8},{1,17},{9,25},{17,1},{25,9},{2,18},{10... | collective-permute-start | bytes 1572872 | tf_op jit(solution)/shard_map/ppermute | solution.py:168
  48.1 12.9 %collective-permute-done.4.refs_8_ = f32[4,128,256]{2,1,0:T(8,128)} collective-permute-done((f32[4,128,256]{2,1,0:T(8,128)S(1)}, f32[4,128,256]{2,1,0:T(8,128)}, u32[]{:S(2)}, u32[]{:S(2)}) %collective-permute-start.4) | collective-permute-done | bytes 524320 | tf_op jit(solution)/shard_map/ppermute | solution.py:168
  61.0 2.7 %all-to-all-done.1 = f32[24,32,128]{2,1,0:T(8,128)S(1)} async-done(((f32[24,32,128]{2,1,0:T(8,128)}), f32[24,32,128]{2,1,0:T(8,128)S(1)}, u32[]{:S(2)}, u32[]{:S(2)}) %all-to-all-start.1) | async-done | bytes 393248 | tf_op jit(solution)/shard_map/all_to_all | solution.py:161
  63.6 3.5 %multiply.2 = f32[2,16,3,16,128]{4,3,2,1,0:T(8,128)S(1)} custom-call(s32[1]{0:T(128)} %constant.37.clone.1.round_ref.refs_0_, s32[128]{0:T(128)S(1)} %copy-done.2, s32[3]{0:T(128)S(1)} %copy-done.3, s32[2,128]{1,0:T(2,128)S(1)} %bitcast.27, s32[1,128]{1,0:T(1,128)S(1)} %bitcast.30, f32[3,256,128]{2,1,0:T(8,128)S(1)} %bitcast.25, ...), custom_call_target="tpu_custom_call" | custom-call | flops 1207959552 | bytes 4194304 | tf_op jit(solution)/shard_map/multiply/pallas_call | solution.py:125
  67.2 0.7 while.10
  67.9 8.4 %collective-permute-start.5 = (f32[16,3,16,128]{3,2,1,0:T(8,128)S(1)}, f32[16,3,16,128]{3,2,1,0:T(8,128)S(1)}, u32[]{:S(2)}, u32[]{:S(2)}) collective-permute-start(f32[16,3,16,128]{3,2,1,0:T(8,128)S(1)} %dynamic-slice_bitcast_fusion.4), channel_id=1, source_target_pairs={{0,1},{1,0},{2,3},{3,2},{4,5},{5,4},{6,7},{7,6},{8,9},{9,8},{10,11... | collective-permute-start | bytes 1179656 | tf_op jit(solution)/shard_map/ppermute | solution.py:181
  76.3 1.3 %collective-permute-done.5 = f32[16,3,16,128]{3,2,1,0:T(8,128)S(1)} collective-permute-done((f32[16,3,16,128]{3,2,1,0:T(8,128)S(1)}, f32[16,3,16,128]{3,2,1,0:T(8,128)S(1)}, u32[]{:S(2)}, u32[]{:S(2)}) %collective-permute-start.5) | collective-permute-done | bytes 393248 | tf_op jit(solution)/shard_map/ppermute | solution.py:181
  77.6 0.1 bitcast_add_fusion
  77.7 15.8 %all_to_all.16 = f32[16,3,16,128]{3,2,1,0:T(8,128)S(1)} all-to-all(f32[16,3,16,128]{3,2,1,0:T(8,128)S(1)} %bitcast_add_fusion), channel_id=1, replica_groups=mesh['z'=12,'y_hi'=2,'x'=4,'y_lo'=4,'core'=2] {'x','y_lo'}, dimensions={0} | all-to-all | bytes 786432 | tf_op jit(solution)/shard_map/all_to_all | solution.py:182
  93.4 0.6 reduce_sum.9
  (1 shorter events, 0.0 us)
Async XLA Ops:
  0.0 9.0 %copy-start = (f32[4,32,128]{2,1,0:T(8,128)S(1)}, f32[4,32,128]{2,1,0:T(8,128)}, u32[]{:S(2)}) copy-start(f32[4,32,128]{2,1,0:T(8,128)} %w_ref.1) | copy-start | bytes 196612
  0.0 9.0 %copy-start.1 = (s32[256]{0:T(256)S(1)}, s32[256]{0:T(256)}, u32[]{:S(2)}) copy-start(s32[256]{0:T(256)} %param.12) | copy-start | bytes 3076
  0.0 9.0 %copy-start.2 = (s32[128]{0:T(128)S(1)}, s32[128]{0:T(128)}, u32[]{:S(2)}) copy-start(s32[128]{0:T(128)} %refs_1_.1) | copy-start | bytes 1540
  0.0 9.0 %copy-start.3 = (s32[3]{0:T(128)S(1)}, s32[3]{0:T(128)}, u32[]{:S(2)}) copy-start(s32[3]{0:T(128)} %refs_2_.1) | copy-start | bytes 40
  0.0 9.0 %copy-start.4 = (s32[128]{0:T(128)S(1)}, s32[128]{0:T(128)}, u32[]{:S(2)}) copy-start(s32[128]{0:T(128)} %param.13) | copy-start | bytes 1540
  1.8 20.6 %collective-permute-start.2 = (f32[4,128,256]{2,1,0:T(8,128)S(1)}, f32[4,128,256]{2,1,0:T(8,128)S(1)}, u32[]{:S(2)}, u32[]{:S(2)}) collective-permute-start(f32[4,128,256]{2,1,0:T(8,128)S(1)} %get-tuple-element.106), channel_id=1, source_target_pairs={{0,8},{8,16},{16,24},{24,0},{1,9},{9,17},{17,25},{25,1},{2,10},{10... | collective-permute-start | bytes 1572872 | tf_op jit(solution)/shard_map/ppermute | solution.py:168
  5.8 16.6 %collective-permute-start.3 = (f32[4,128,256]{2,1,0:T(8,128)S(1)}, f32[4,128,256]{2,1,0:T(8,128)}, u32[]{:S(2)}, u32[]{:S(2)}) collective-permute-start(f32[4,128,256]{2,1,0:T(8,128)S(1)} %get-tuple-element.105), channel_id=1, source_target_pairs={{0,24},{8,0},{16,8},{24,16},{1,25},{9,1},{17,9},{25,17},{2,26},{10... | collective-permute-start | bytes 1572872 | tf_op jit(solution)/shard_map/ppermute | solution.py:168
  10.4 12.0 %collective-permute-start.1 = (f32[32,128]{1,0:T(8,128)S(1)}, f32[32,128]{1,0:T(8,128)S(1)}, u32[]{:S(2)}, u32[]{:S(2)}) collective-permute-start(f32[32,128]{1,0:T(8,128)S(1)} %get-tuple-element.74), channel_id=1, source_target_pairs={{0,0},{1,32},{2,64},{3,96},{4,128},{5,160},{6,192},{7,224},{8,256}... | collective-permute-start | bytes 49160 | tf_op jit(solution)/shard_map/ppermute | solution.py:157
  23.2 40.4 %all-to-all-start.1 = ((f32[24,32,128]{2,1,0:T(8,128)}), f32[24,32,128]{2,1,0:T(8,128)S(1)}, u32[]{:S(2)}, u32[]{:S(2)}) async-start(f32[24,32,128]{2,1,0:T(8,128)} %broadcast_in_dim.8), calls=%async_computation.1 | async-start | bytes 786432 | tf_op jit(solution)/shard_map/all_to_all | solution.py:161
  46.2 14.8 %collective-permute-start.4 = (f32[4,128,256]{2,1,0:T(8,128)S(1)}, f32[4,128,256]{2,1,0:T(8,128)}, u32[]{:S(2)}, u32[]{:S(2)}) collective-permute-start(f32[4,128,256]{2,1,0:T(8,128)S(1)} %get-tuple-element.104), channel_id=1, source_target_pairs={{0,16},{8,24},{16,0},{24,8},{1,17},{9,25},{17,1},{25,9},{2,18},{10... | collective-permute-start | bytes 1572872 | tf_op jit(solution)/shard_map/ppermute | solution.py:168
  67.9 9.7 %collective-permute-start.5 = (f32[16,3,16,128]{3,2,1,0:T(8,128)S(1)}, f32[16,3,16,128]{3,2,1,0:T(8,128)S(1)}, u32[]{:S(2)}, u32[]{:S(2)}) collective-permute-start(f32[16,3,16,128]{3,2,1,0:T(8,128)S(1)} %dynamic-slice_bitcast_fusion.4), channel_id=1, source_target_pairs={{0,1},{1,0},{2,3},{3,2},{4,5},{5,4},{6,7},{7,6},{8,9},{9,8},{10,11... | collective-permute-start | bytes 1179656 | tf_op jit(solution)/shard_map/ppermute | solution.py:181

commit v5 on v4

--- a/solution.py
+++ b/solution.py
@@ -10,6 +10,7 @@
 LANES = 128
 ROWS = 4
 SLAB = 32
+PREPARE_FLOPS = 6_550_000_000
 PLACES = 32
 HOPS = ("z", "y_hi")
 PLANE = ("x", "y_lo")
@@ -66,12 +67,17 @@
     return high, (values - high.astype(jnp.float32)).astype(jnp.bfloat16)
 
 
-def multiply_kernel(with_sum, round_ref, occ_ref, j_ref, vir_ref, b_ref, w_ref, *rest):
-    t_refs, rest = rest[:4], rest[4:]
-    if with_sum:
-        sum_ref, out_ref, w_high, w_low, t_high, t_low = rest
-    else:
-        out_ref, w_high, w_low, t_high, t_low = rest
+def prepare_kernel(*refs):
+    t_high, t_low = refs[4:]
+    for shift, t_ref in enumerate(refs[:4]):
+        for k in range(4):
+            high, low = halves(t_ref[k])
+            t_high[shift * LANES:(shift + 1) * LANES, k * 256:(k + 1) * 256] = high
+            t_low[shift * LANES:(shift + 1) * LANES, k * 256:(k + 1) * 256] = low
+
+
+def multiply_kernel(with_sum, round_ref, occ_ref, j_ref, vir_ref, b_ref, w_ref, t_high, t_low, *rest):
+    sums, (own_ref, given_ref, w_high, w_low) = rest[:2 * with_sum], rest[2 * with_sum:]
     label_b = b_ref[...]
     rank = ranks(label_b)
     label_c = jnp.concatenate([columns(vir_ref[half:half + 1, :]) for half in range(2)], axis=0)
@@ -86,22 +92,25 @@
             for piece, target in zip(split[group], (w_high, w_low)):
                 spread = jnp.dot(piece, puts[part], preferred_element_type=jnp.float32)
                 target[k * 256:(k + 1) * 256, j * LANES:(j + 1) * LANES] = jnp.where(keep, spread, 0.0).astype(jnp.bfloat16)
-        for shift, t_ref in enumerate(t_refs):
-            high, low = halves(t_ref[k])
-            t_high[shift * LANES:(shift + 1) * LANES, k * 256:(k + 1) * 256] = high
-            t_low[shift * LANES:(shift + 1) * LANES, k * 256:(k + 1) * 256] = low
     total = jnp.dot(t_high[...], w_high[...], preferred_element_type=jnp.float32)
     total = total + jnp.dot(t_high[...], w_low[...], preferred_element_type=jnp.float32)
     total = total + jnp.dot(t_low[...], w_high[...], preferred_element_type=jnp.float32)
-    for shift in range(4):
-        source = lax.rem(lax.axis_index("x") + 4 - shift, 4)
-        for tile in range(8):
-            top = shift * LANES + tile * 16
-            for j in range(J):
-                piece = total[top:top + 16, j * LANES:(j + 1) * LANES]
-                if with_sum:
-                    piece = piece + sum_ref[tile % 2, source * 4 + tile // 2, j]
-                out_ref[tile % 2, source * 4 + tile // 2, j] = piece
+    core = lax.axis_index("core")
+
+    def put_out(own, given):
+        for shift in range(4):
+            source = lax.rem(lax.axis_index("x") + 4 - shift, 4)
+            for tile in range(8):
+                out_ref = (own, given)[tile % 2]
+                top = shift * LANES + tile * 16
+                for j in range(J):
+                    piece = total[top:top + 16, j * LANES:(j + 1) * LANES]
+                    if with_sum:
+                        piece = piece + sums[0 if out_ref is own_ref else 1][source * 4 + tile // 2, j]
+                    out_ref[source * 4 + tile // 2, j] = piece
+
+    pl.when(core == 0)(lambda: put_out(own_ref, given_ref))
+    pl.when(core == 1)(lambda: put_out(given_ref, own_ref))
 
 
 SMEM = pl.BlockSpec(memory_space=pltpu.SMEM)
@@ -120,23 +129,29 @@
     )(round_index, occ, j, vir, b, integrals)
 
 
-def multiply(round_index, occ, j, vir, b, w, t, total=None):
-    with_sum = total is not None
+def prepare(*t):
     return pl.pallas_call(
-        lambda *refs: multiply_kernel(with_sum, *refs),
-        out_shape=jax.ShapeDtypeStruct((2, 16, J, 16, LANES), jnp.float32),
-        in_specs=[SMEM] * 3 + [VMEM] * 7 + [VMEM] * with_sum,
-        out_specs=VMEM,
-        scratch_shapes=[
-            pltpu.VMEM((1024, J * LANES), jnp.bfloat16),
-            pltpu.VMEM((1024, J * LANES), jnp.bfloat16),
-            pltpu.VMEM((512, 1024), jnp.bfloat16),
-            pltpu.VMEM((512, 1024), jnp.bfloat16),
-        ],
+        prepare_kernel,
+        out_shape=(jax.ShapeDtypeStruct((512, 1024), jnp.bfloat16),) * 2,
+        in_specs=[VMEM] * 4,
+        out_specs=(VMEM, VMEM),
+        compiler_params=pltpu.CompilerParams(vmem_limit_bytes=16 << 20),
+        cost_estimate=pl.CostEstimate(flops=PREPARE_FLOPS, bytes_accessed=4 << 20, transcendentals=0),
+        name="prepare",
+    )(*t)
+
+
+def multiply(round_index, occ, j, vir, b, w, t_high, t_low, sums=()):
+    return pl.pallas_call(
+        lambda *refs: multiply_kernel(bool(sums), *refs),
+        out_shape=(jax.ShapeDtypeStruct((16, J, 16, LANES), jnp.float32),) * 2,
+        in_specs=[SMEM] * 3 + [VMEM] * (5 + len(sums)),
+        out_specs=(VMEM, VMEM),
+        scratch_shapes=[pltpu.VMEM((1024, J * LANES), jnp.bfloat16)] * 2,
         compiler_params=pltpu.CompilerParams(vmem_limit_bytes=24 << 20),
         cost_estimate=pl.CostEstimate(flops=3 * 2 * 512 * 1024 * 384, bytes_accessed=4 << 20, transcendentals=0),
         name="multiply",
-    )(round_index, occ, j, vir, b, w, *t, *([total] if with_sum else []))
+    )(round_index, occ, j, vir, b, w, t_high, t_low, *sums)
 
 
 def owners():
@@ -153,31 +168,29 @@
     labels = (irrep_occ, irrep_j, vir, b)
 
     def owned(round_index):
-        packed, rounds = pack(round_index, *labels, integrals)
-        return lax.ppermute(packed, AXES, owners()), rounds
+        return lax.ppermute(pack(round_index, *labels, integrals)[0], AXES, owners())
 
     def column(packed):
         copies = jnp.broadcast_to(packed[None], (24, SLAB, LANES))
         gathered = lax.all_to_all(copies, HOPS, split_axis=0, concat_axis=0, tiled=True)
         return gathered.reshape(3, 256, LANES)
 
+    packed, rounds = pack(jnp.zeros((1,), jnp.int32), *labels, integrals)
+    packed, amplitudes = lax.optimization_barrier((packed, amplitudes))
+    packed = lax.ppermute(packed, AXES, owners())
     x = lax.axis_index("x")
     t = []
     for shift in range(4):
         piece = lax.dynamic_slice_in_dim(amplitudes[0], lax.rem(x + shift, 4) * 4, 4)
         t.append(lax.ppermute(piece, "x", [(s, (s + shift) % 4) for s in range(4)]) if shift else piece)
-    packed, rounds = owned(jnp.zeros((1,), jnp.int32))
-    packed, t[1], t[3] = lax.optimization_barrier((packed, t[1], t[3]))
-    total = multiply(jnp.zeros((1,), jnp.int32), *labels, column(packed), t)
+    t = prepare(*t)
+    sums = multiply(jnp.zeros((1,), jnp.int32), *labels, column(packed), *t)
 
     def another(state):
-        index, total = state
-        return index + 1, multiply(index[None], *labels, column(owned(index[None])[0]), t, total)
-
-    _, total = lax.while_loop(lambda state: state[0] < rounds[0], another, (jnp.int32(1), total))
-    core = lax.axis_index("core")
-    given = lax.dynamic_index_in_dim(total, 1 - core, keepdims=False)
-    own = lax.dynamic_index_in_dim(total, core, keepdims=False)
+        index, sums = state
+        return index + 1, multiply(index[None], *labels, column(owned(index[None])), *t, sums)
+
+    _, (own, given) = lax.while_loop(lambda state: state[0] < rounds[0], another, (jnp.int32(1), sums))
     total = own + lax.ppermute(given, "core", [(0, 1), (1, 0)])
     parts = lax.all_to_all(total, PLANE, split_axis=0, concat_axis=0, tiled=True)
     return jnp.sum(parts, axis=0, keepdims=True)

time: 94.5 us -> 94.9 us (level)
  starting transfers between devices: 49.1 us -> 42.8 us
  blocking collectives: 15.8 us -> 21.1 us
  Pallas kernels: 4.89 us -> 6.5 us
    all_to_all x1, starting transfers between devices: 22.9 us -> 4.16 us  [column(): lax.all_to_all(copies, HOPS, split_axis=0, concat_axis=0, tiled=True)]
    ppermute x3, starting transfers between devices: 9.06 us -> 22.6 us  [local(): lax.ppermute(piece, 'x', [(s, (s + shift) % 4) for s in range(4)])]
    all_to_all x1, blocking collectives: 15.8 us -> 21.1 us  [local(): lax.all_to_all(total, PLANE, split_axis=0, concat_axis=0, tiled=True)]
    all_to_all x1, waiting for transfers between devices: 2.66 us -> 7.84 us  [column(): lax.all_to_all(copies, HOPS, split_axis=0, concat_axis=0, tiled=True)]
    ppermute x1, waiting for transfers between devices: 3.22 us -> 0.01 us  [local(): packed = lax.ppermute(packed, AXES, owners())]
    ppermute x3, waiting for transfers between devices: 12.9 us -> 10 us  [local(): lax.ppermute(piece, 'x', [(s, (s + shift) % 4) for s in range(4)])]
    pallas_call x1 -> x2, Pallas kernels: 3.5 us -> 4.8 us  [the longest x1 3.61 us: multiply(): pl.pallas_call(lambda *refs: multiply_kernel(bool(sums), *refs), out_shap...]
    ppermute x1, starting transfers between devices: 8.38 us -> 7.27 us  [local(): total = own + lax.ppermute(given, 'core', [(0, 1), (1, 0)])]
  transfers between devices with their start and end apart: 6 -> 6, of which waited for: 4 -> 4; matrix products, arithmetic and copies ran while one was open for 0% -> 4% of each run, Pallas kernels for 1% -> 1%
where the time goes in v5:
time: 94.9 us; the launch traced here: 94.4 us
  starting transfers between devices  42.8 us (45%)
  blocking collectives  21.1 us (22%)
  waiting for transfers between devices  19.2 us (20%)
  Pallas kernels  6.5 us (7%)
  local copies, waits for them, and re-layouts  3.37 us (4%)
    ppermute x3, starting transfers between devices, local(): lax.ppermute(piece, 'x', [(s, (s + shift) % 4) for s in range(4)])  22.6 us
    all_to_all x1, blocking collectives, local(): lax.all_to_all(total, PLANE, split_axis=0, concat_axis=0, tiled=True)  21.1 us
    ppermute x3, waiting for transfers between devices, local(): lax.ppermute(piece, 'x', [(s, (s + shift) % 4) for s in range(4)])  10 us
    ppermute x1, starting transfers between devices, local(): packed = lax.ppermute(packed, AXES, owners())  8.84 us
    all_to_all x1, waiting for transfers between devices, column(): lax.all_to_all(copies, HOPS, split_axis=0, concat_axis=0, tiled=True)  7.84 us
    ppermute x1, starting transfers between devices, local(): total = own + lax.ppermute(given, 'core', [(0, 1), (1, 0)])  7.27 us
    all_to_all x1, starting transfers between devices, column(): lax.all_to_all(copies, HOPS, split_axis=0, concat_axis=0, tiled=True)  4.16 us
    pallas_call x1, Pallas kernels, multiply(): pl.pallas_call(lambda *refs: multiply_kernel(bool(sums), *refs), out_shap...  3.61 us
  transfers between devices with their start and end apart: 6, of which 4 were waited for; matrix products, arithmetic and copies ran while one was open for 4% of the time, Pallas kernels for 1%

profile of v5, /device:TPU:1, one launch (start us, length us, event | category | flops | bytes accessed | tf_op | source)
XLA Modules:
  0.0 94.4 jit_solution(17569737356982079372)
XLA Ops:
  0.0 1.7 %pack.2 = (f32[32,128]{1,0:T(8,128)S(1)}, s32[1]{0:T(128)}) custom-call(s32[1]{0:T(128)} %constant.27.clone.1.round_ref.refs_0_, s32[128]{0:T(128)} %refs_1_.1, s32[3]{0:T(128)} %refs_2_.1, s32[2,128]{1,0:T(2,128)} %bitcast.22, s32[1,128]{1,0:T(1,128)} %bitcast.25, f32[4,32,128]{2,1,0:T(8,128)} %w_ref.1), custom_call_target="tpu_custom_call" | custom-call | tf_op jit(solution)/shard_map/pack/pallas_call | solution.py:121
  1.7 8.8 %collective-permute-start.1 = (f32[32,128]{1,0:T(8,128)S(1)}, f32[32,128]{1,0:T(8,128)S(1)}, u32[]{:S(2)}, u32[]{:S(2)}) collective-permute-start(f32[32,128]{1,0:T(8,128)S(1)} %get-tuple-element.76), channel_id=1, source_target_pairs={{0,0},{1,32},{2,64},{3,96},{4,128},{5,160},{6,192},{7,224},{8,256}... | collective-permute-start | bytes 49160 | tf_op jit(solution)/shard_map/ppermute | solution.py:180
  10.6 2.5 %dynamic-slice_bitcast_fusion = (f32[4,128,256]{2,1,0:T(8,128)S(1)}, f32[4,128,256]{2,1,0:T(8,128)S(1)}, f32[4,128,256]{2,1,0:T(8,128)}, f32[4,128,256]{2,1,0:T(8,128)S(1)}) fusion(f32[1,16,128,256]{3,2,1,0:T(8,128)} %param.8, s32[]{:T(128)S(6)} %select_n.15, s32[]{:T(128)S(6)} %select_n.14, s32[]{:T(128)S(6)} %select_n.13, s32[]{:T(128)S(6)} %select_n.12), kind=kLoop, calls=%fused_computation | loop fusion | bytes 4194320 | tf_op jit(solution)/shard_map/dynamic_slice | solution.py:184
  13.1 11.5 %collective-permute-start.2 = (f32[4,128,256]{2,1,0:T(8,128)}, f32[4,128,256]{2,1,0:T(8,128)S(1)}, u32[]{:S(2)}, u32[]{:S(2)}) collective-permute-start(f32[4,128,256]{2,1,0:T(8,128)} %get-tuple-element.109), channel_id=1, source_target_pairs={{0,8},{8,16},{16,24},{24,0},{1,9},{9,17},{17,25},{25,1},{2,10},{10... | collective-permute-start | bytes 1572872 | tf_op jit(solution)/shard_map/ppermute | solution.py:185
  24.7 7.1 %collective-permute-start.3 = (f32[4,128,256]{2,1,0:T(8,128)S(1)}, f32[4,128,256]{2,1,0:T(8,128)S(1)}, u32[]{:S(2)}, u32[]{:S(2)}) collective-permute-start(f32[4,128,256]{2,1,0:T(8,128)S(1)} %get-tuple-element.108), channel_id=1, source_target_pairs={{0,16},{8,24},{16,0},{24,8},{1,17},{9,25},{17,1},{25,9},{2,18},{10... | collective-permute-start | bytes 1572872 | tf_op jit(solution)/shard_map/ppermute | solution.py:185
  31.7 4.0 %collective-permute-start.4 = (f32[4,128,256]{2,1,0:T(8,128)S(1)}, f32[4,128,256]{2,1,0:T(8,128)S(1)}, u32[]{:S(2)}, u32[]{:S(2)}) collective-permute-start(f32[4,128,256]{2,1,0:T(8,128)S(1)} %get-tuple-element.107), channel_id=1, source_target_pairs={{0,24},{8,0},{16,8},{24,16},{1,25},{9,1},{17,9},{25,17},{2,26},{10... | collective-permute-start | bytes 1572872 | tf_op jit(solution)/shard_map/ppermute | solution.py:185
  35.7 0.0 collective-permute-done.1
  35.7 0.8 broadcast_in_dim.8
  36.5 4.2 %all-to-all-start.1 = ((f32[24,32,128]{2,1,0:T(8,128)}), f32[24,32,128]{2,1,0:T(8,128)S(1)}, u32[]{:S(2)}, u32[]{:S(2)}) async-start(f32[24,32,128]{2,1,0:T(8,128)} %broadcast_in_dim.8), calls=%async_computation.1 | async-start | bytes 786432 | tf_op jit(solution)/shard_map/all_to_all | solution.py:175
  40.7 0.0 collective-permute-done.2.refs_1_
  40.7 8.3 %collective-permute-done.3.refs_2_ = f32[4,128,256]{2,1,0:T(8,128)S(1)} collective-permute-done((f32[4,128,256]{2,1,0:T(8,128)S(1)}, f32[4,128,256]{2,1,0:T(8,128)S(1)}, u32[]{:S(2)}, u32[]{:S(2)}) %collective-permute-start.3) | collective-permute-done | bytes 524320 | tf_op jit(solution)/shard_map/ppermute | solution.py:185
  49.0 1.7 %collective-permute-done.4.refs_3_ = f32[4,128,256]{2,1,0:T(8,128)S(1)} collective-permute-done((f32[4,128,256]{2,1,0:T(8,128)S(1)}, f32[4,128,256]{2,1,0:T(8,128)S(1)}, u32[]{:S(2)}, u32[]{:S(2)}) %collective-permute-start.4) | collective-permute-done | bytes 524320 | tf_op jit(solution)/shard_map/ppermute | solution.py:185
  50.7 0.0 copy-start.1
  50.7 0.0 copy-start.2
  50.7 0.0 copy-start.3
  50.7 0.0 copy-start.4
  50.7 1.2 %prepare.1 = (bf16[512,1024]{1,0:T(8,128)(2,1)S(1)}, bf16[512,1024]{1,0:T(8,128)(2,1)}) custom-call(f32[4,128,256]{2,1,0:T(8,128)S(1)} %get-tuple-element.110.refs_0_, f32[4,128,256]{2,1,0:T(8,128)S(1)} %collective-permute-done.2.refs_1_, f32[4,128,256]{2,1,0:T(8,128)S(1)} %collective-permute-done.3.refs_2_, f32[4,128,256]{2,1,0:T(8,128)S(1)} %collective-permute-done.4.refs_3_), custom_call_target="tpu_custom_call" | custom-call | flops 6550000128 | bytes 4194304 | tf_op jit(solution)/shard_map/prepare/pallas_call | solution.py:133
  51.9 7.8 %all-to-all-done.1 = f32[24,32,128]{2,1,0:T(8,128)S(1)} async-done(((f32[24,32,128]{2,1,0:T(8,128)}), f32[24,32,128]{2,1,0:T(8,128)S(1)}, u32[]{:S(2)}, u32[]{:S(2)}) %all-to-all-start.1) | async-done | bytes 393248 | tf_op jit(solution)/shard_map/all_to_all | solution.py:175
  59.7 0.0 copy-done.1
  59.8 0.0 copy-done.2
  59.8 0.0 copy-done.3
  59.8 0.0 copy-done.4
  59.8 0.0 copy-start
  59.8 3.6 %multiply.2 = (f32[16,3,16,128]{3,2,1,0:T(8,128)S(1)}, f32[16,3,16,128]{3,2,1,0:T(8,128)S(1)}) custom-call(s32[1]{0:T(128)} %constant.27.clone.1.round_ref.refs_0_, s32[128]{0:T(128)S(1)} %copy-done.2, s32[3]{0:T(128)S(1)} %copy-done.3, s32[2,128]{1,0:T(2,128)S(1)} %bitcast.23, s32[1,128]{1,0:T(1,128)S(1)} %bitcast.26, f32[3,256,128]{2,1,0:T(8,128)S(1)} %bitcast.21, ...), custom_call_target="tpu_custom_call" | custom-call | flops 1207959552 | bytes 4194304 | tf_op jit(solution)/shard_map/multiply/pallas_call | solution.py:145
  63.4 0.0 copy-done
  63.4 0.6 while.12
  64.1 7.3 %collective-permute-start.5 = (f32[16,3,16,128]{3,2,1,0:T(8,128)S(1)}, f32[16,3,16,128]{3,2,1,0:T(8,128)S(1)}, u32[]{:S(2)}, u32[]{:S(2)}) collective-permute-start(f32[16,3,16,128]{3,2,1,0:T(8,128)S(1)} %get-tuple-element.84), channel_id=1, source_target_pairs={{0,1},{1,0},{2,3},{3,2},{4,5},{5,4},{6,7},{7,6},{8,9},{9,8},{10,11... | collective-permute-start | bytes 1179656 | tf_op jit(solution)/shard_map/ppermute | solution.py:194
  71.3 1.3 %collective-permute-done.5 = f32[16,3,16,128]{3,2,1,0:T(8,128)S(1)} collective-permute-done((f32[16,3,16,128]{3,2,1,0:T(8,128)S(1)}, f32[16,3,16,128]{3,2,1,0:T(8,128)S(1)}, u32[]{:S(2)}, u32[]{:S(2)}) %collective-permute-start.5) | collective-permute-done | bytes 393248 | tf_op jit(solution)/shard_map/ppermute | solution.py:194
  72.7 0.1 add.34
  72.7 21.1 %all_to_all.16 = f32[16,3,16,128]{3,2,1,0:T(8,128)S(1)} all-to-all(f32[16,3,16,128]{3,2,1,0:T(8,128)S(1)} %add.34), channel_id=1, replica_groups=mesh['z'=12,'y_hi'=2,'x'=4,'y_lo'=4,'core'=2] {'x','y_lo'}, dimensions={0} | all-to-all | bytes 786432 | tf_op jit(solution)/shard_map/all_to_all | solution.py:195
  93.8 0.6 reduce_sum.9
Async XLA Ops:
  1.7 34.0 %collective-permute-start.1 = (f32[32,128]{1,0:T(8,128)S(1)}, f32[32,128]{1,0:T(8,128)S(1)}, u32[]{:S(2)}, u32[]{:S(2)}) collective-permute-start(f32[32,128]{1,0:T(8,128)S(1)} %get-tuple-element.76), channel_id=1, source_target_pairs={{0,0},{1,32},{2,64},{3,96},{4,128},{5,160},{6,192},{7,224},{8,256}... | collective-permute-start | bytes 49160 | tf_op jit(solution)/shard_map/ppermute | solution.py:180
  13.1 27.6 %collective-permute-start.2 = (f32[4,128,256]{2,1,0:T(8,128)}, f32[4,128,256]{2,1,0:T(8,128)S(1)}, u32[]{:S(2)}, u32[]{:S(2)}) collective-permute-start(f32[4,128,256]{2,1,0:T(8,128)} %get-tuple-element.109), channel_id=1, source_target_pairs={{0,8},{8,16},{16,24},{24,0},{1,9},{9,17},{17,25},{25,1},{2,10},{10... | collective-permute-start | bytes 1572872 | tf_op jit(solution)/shard_map/ppermute | solution.py:185
  24.7 24.4 %collective-permute-start.3 = (f32[4,128,256]{2,1,0:T(8,128)S(1)}, f32[4,128,256]{2,1,0:T(8,128)S(1)}, u32[]{:S(2)}, u32[]{:S(2)}) collective-permute-start(f32[4,128,256]{2,1,0:T(8,128)S(1)} %get-tuple-element.108), channel_id=1, source_target_pairs={{0,16},{8,24},{16,0},{24,8},{1,17},{9,25},{17,1},{25,9},{2,18},{10... | collective-permute-start | bytes 1572872 | tf_op jit(solution)/shard_map/ppermute | solution.py:185
  31.7 19.0 %collective-permute-start.4 = (f32[4,128,256]{2,1,0:T(8,128)S(1)}, f32[4,128,256]{2,1,0:T(8,128)S(1)}, u32[]{:S(2)}, u32[]{:S(2)}) collective-permute-start(f32[4,128,256]{2,1,0:T(8,128)S(1)} %get-tuple-element.107), channel_id=1, source_target_pairs={{0,24},{8,0},{16,8},{24,16},{1,25},{9,1},{17,9},{25,17},{2,26},{10... | collective-permute-start | bytes 1572872 | tf_op jit(solution)/shard_map/ppermute | solution.py:185
  36.5 23.2 %all-to-all-start.1 = ((f32[24,32,128]{2,1,0:T(8,128)}), f32[24,32,128]{2,1,0:T(8,128)S(1)}, u32[]{:S(2)}, u32[]{:S(2)}) async-start(f32[24,32,128]{2,1,0:T(8,128)} %broadcast_in_dim.8), calls=%async_computation.1 | async-start | bytes 786432 | tf_op jit(solution)/shard_map/all_to_all | solution.py:175
  50.7 9.0 %copy-start.1 = (s32[256]{0:T(256)S(1)}, s32[256]{0:T(256)}, u32[]{:S(2)}) copy-start(s32[256]{0:T(256)} %param.12) | copy-start | bytes 3076
  50.7 9.0 %copy-start.2 = (s32[128]{0:T(128)S(1)}, s32[128]{0:T(128)}, u32[]{:S(2)}) copy-start(s32[128]{0:T(128)} %refs_1_.1) | copy-start | bytes 1540
  50.7 9.0 %copy-start.3 = (s32[3]{0:T(128)S(1)}, s32[3]{0:T(128)}, u32[]{:S(2)}) copy-start(s32[3]{0:T(128)} %refs_2_.1) | copy-start | bytes 40
  50.7 9.1 %copy-start.4 = (s32[128]{0:T(128)S(1)}, s32[128]{0:T(128)}, u32[]{:S(2)}) copy-start(s32[128]{0:T(128)} %param.13) | copy-start | bytes 1540
  59.8 3.6 %copy-start = (f32[4,32,128]{2,1,0:T(8,128)S(1)}, f32[4,32,128]{2,1,0:T(8,128)}, u32[]{:S(2)}) copy-start(f32[4,32,128]{2,1,0:T(8,128)} %w_ref.1) | copy-start | bytes 196612
  64.1 8.6 %collective-permute-start.5 = (f32[16,3,16,128]{3,2,1,0:T(8,128)S(1)}, f32[16,3,16,128]{3,2,1,0:T(8,128)S(1)}, u32[]{:S(2)}, u32[]{:S(2)}) collective-permute-start(f32[16,3,16,128]{3,2,1,0:T(8,128)S(1)} %get-tuple-element.84), channel_id=1, source_target_pairs={{0,1},{1,0},{2,3},{3,2},{4,5},{5,4},{6,7},{7,6},{8,9},{9,8},{10,11... | collective-permute-start | bytes 1179656 | tf_op jit(solution)/shard_map/ppermute | solution.py:194

commit v6 on v5

--- a/solution.py
+++ b/solution.py
@@ -10,7 +10,6 @@
 LANES = 128
 ROWS = 4
 SLAB = 32
-PREPARE_FLOPS = 6_550_000_000
 PLACES = 32
 HOPS = ("z", "y_hi")
 PLANE = ("x", "y_lo")
@@ -67,31 +66,28 @@
     return high, (values - high.astype(jnp.float32)).astype(jnp.bfloat16)
 
 
-def prepare_kernel(*refs):
-    t_high, t_low = refs[4:]
-    for shift, t_ref in enumerate(refs[:4]):
-        for k in range(4):
-            high, low = halves(t_ref[k])
-            t_high[shift * LANES:(shift + 1) * LANES, k * 256:(k + 1) * 256] = high
-            t_low[shift * LANES:(shift + 1) * LANES, k * 256:(k + 1) * 256] = low
-
-
-def multiply_kernel(with_sum, round_ref, occ_ref, j_ref, vir_ref, b_ref, w_ref, t_high, t_low, *rest):
-    sums, (own_ref, given_ref, w_high, w_low) = rest[:2 * with_sum], rest[2 * with_sum:]
+def multiply_kernel(with_sum, round_ref, occ_ref, j_ref, vir_ref, b_ref, w_ref, *rest):
+    t_refs, sums, (own_ref, given_ref, w_high, w_low, t_high, t_low) = rest[:4], rest[4:4 + 2 * with_sum], rest[4 + 2 * with_sum:]
     label_b = b_ref[...]
     rank = ranks(label_b)
     label_c = jnp.concatenate([columns(vir_ref[half:half + 1, :]) for half in range(2)], axis=0)
     right = jnp.bitwise_xor(label_c, label_b)
-    puts = [jnp.where(placing(rank, round_ref[0], part), 1.0, 0.0).astype(jnp.bfloat16) for part in range(ROWS)]
-    split = [halves(w_ref[group]) for group in range(3)]
+    put = jnp.concatenate(
+        [jnp.where(placing(rank, round_ref[0], part), 1.0, 0.0).astype(jnp.bfloat16) for part in range(ROWS)], axis=1
+    )
+    spreads = [jnp.dot(piece, put, preferred_element_type=jnp.float32) for piece in halves(w_ref[...].reshape(768, LANES))]
     first = vir_index() * 16 + lax.axis_index("x") * 4
     for k in range(4):
         for j in range(J):
             group, part = divmod(k * J + j, ROWS)
             keep = right == jnp.bitwise_xor(occ_ref[first + k], j_ref[j])
-            for piece, target in zip(split[group], (w_high, w_low)):
-                spread = jnp.dot(piece, puts[part], preferred_element_type=jnp.float32)
-                target[k * 256:(k + 1) * 256, j * LANES:(j + 1) * LANES] = jnp.where(keep, spread, 0.0).astype(jnp.bfloat16)
+            for spread, target in zip(spreads, (w_high, w_low)):
+                piece = spread[group * 256:(group + 1) * 256, part * LANES:(part + 1) * LANES]
+                target[k * 256:(k + 1) * 256, j * LANES:(j + 1) * LANES] = jnp.where(keep, piece, 0.0).astype(jnp.bfloat16)
+        for shift, t_ref in enumerate(t_refs):
+            high, low = halves(t_ref[k])
+            t_high[shift * LANES:(shift + 1) * LANES, k * 256:(k + 1) * 256] = high
+            t_low[shift * LANES:(shift + 1) * LANES, k * 256:(k + 1) * 256] = low
     total = jnp.dot(t_high[...], w_high[...], preferred_element_type=jnp.float32)
     total = total + jnp.dot(t_high[...], w_low[...], preferred_element_type=jnp.float32)
     total = total + jnp.dot(t_low[...], w_high[...], preferred_element_type=jnp.float32)
@@ -129,29 +125,17 @@
     )(round_index, occ, j, vir, b, integrals)
 
 
-def prepare(*t):
-    return pl.pallas_call(
-        prepare_kernel,
-        out_shape=(jax.ShapeDtypeStruct((512, 1024), jnp.bfloat16),) * 2,
-        in_specs=[VMEM] * 4,
-        out_specs=(VMEM, VMEM),
-        compiler_params=pltpu.CompilerParams(vmem_limit_bytes=16 << 20),
-        cost_estimate=pl.CostEstimate(flops=PREPARE_FLOPS, bytes_accessed=4 << 20, transcendentals=0),
-        name="prepare",
-    )(*t)
-
-
-def multiply(round_index, occ, j, vir, b, w, t_high, t_low, sums=()):
+def multiply(round_index, occ, j, vir, b, w, t, sums=()):
     return pl.pallas_call(
         lambda *refs: multiply_kernel(bool(sums), *refs),
         out_shape=(jax.ShapeDtypeStruct((16, J, 16, LANES), jnp.float32),) * 2,
-        in_specs=[SMEM] * 3 + [VMEM] * (5 + len(sums)),
+        in_specs=[SMEM] * 3 + [VMEM] * (7 + len(sums)),
         out_specs=(VMEM, VMEM),
-        scratch_shapes=[pltpu.VMEM((1024, J * LANES), jnp.bfloat16)] * 2,
+        scratch_shapes=[pltpu.VMEM((1024, J * LANES), jnp.bfloat16)] * 2 + [pltpu.VMEM((512, 1024), jnp.bfloat16)] * 2,
         compiler_params=pltpu.CompilerParams(vmem_limit_bytes=24 << 20),
         cost_estimate=pl.CostEstimate(flops=3 * 2 * 512 * 1024 * 384, bytes_accessed=4 << 20, transcendentals=0),
         name="multiply",
-    )(round_index, occ, j, vir, b, w, t_high, t_low, *sums)
+    )(round_index, occ, j, vir, b, w, *t, *sums)
 
 
 def owners():
@@ -176,19 +160,26 @@
         return gathered.reshape(3, 256, LANES)
 
     packed, rounds = pack(jnp.zeros((1,), jnp.int32), *labels, integrals)
-    packed, amplitudes = lax.optimization_barrier((packed, amplitudes))
-    packed = lax.ppermute(packed, AXES, owners())
+    packed_before = packed
     x = lax.axis_index("x")
-    t = []
-    for shift in range(4):
-        piece = lax.dynamic_slice_in_dim(amplitudes[0], lax.rem(x + shift, 4) * 4, 4)
-        t.append(lax.ppermute(piece, "x", [(s, (s + shift) % 4) for s in range(4)]) if shift else piece)
-    t = prepare(*t)
-    sums = multiply(jnp.zeros((1,), jnp.int32), *labels, column(packed), *t)
+
+    def piece(amplitudes, shift):
+        return lax.dynamic_slice_in_dim(amplitudes[0], lax.rem(x + shift, 4) * 4, 4)
+
+    def exchanged(piece, shift):
+        return lax.ppermute(piece, "x", [(s, (s + shift) % 4) for s in range(4)])
+
+    opposite = exchanged(piece(amplitudes, 2), 2)
+    later, packed_before = lax.optimization_barrier((amplitudes, packed_before))
+    packed = lax.ppermute(packed_before, AXES, owners())
+    t = [piece(later, 0), piece(later, 1), opposite, piece(later, 3)]
+    packed, t = lax.optimization_barrier((packed, t))
+    t[1], t[3] = exchanged(t[1], 1), exchanged(t[3], 3)
+    sums = multiply(jnp.zeros((1,), jnp.int32), *labels, column(packed), t)
 
     def another(state):
         index, sums = state
-        return index + 1, multiply(index[None], *labels, column(owned(index[None])), *t, sums)
+        return index + 1, multiply(index[None], *labels, column(owned(index[None])), t, sums)
 
     _, (own, given) = lax.while_loop(lambda state: state[0] < rounds[0], another, (jnp.int32(1), sums))
     total = own + lax.ppermute(given, "core", [(0, 1), (1, 0)])

time: 94.9 us -> 92.6 us (0.976)
  starting transfers between devices: 42.8 us -> 50.8 us
  blocking collectives: 21.1 us -> 15.8 us
  waiting for transfers between devices: 19.2 us -> 15.2 us
  Pallas kernels: 6.5 us -> 5.33 us
    all_to_all x1, starting transfers between devices: 4.16 us -> 23.4 us  [column(): lax.all_to_all(copies, HOPS, split_axis=0, concat_axis=0, tiled=True)]
    ppermute x4, starting transfers between devices: 31.4 us -> 20.3 us  [the longest x3 12 us: exchanged(): return lax.ppermute(piece, 'x', [(s, (s + shift) % 4) for s in range(4)])]
    all_to_all x1, blocking collectives: 21.1 us -> 15.8 us  [local(): lax.all_to_all(total, PLANE, split_axis=0, concat_axis=0, tiled=True)]
    all_to_all x1, waiting for transfers between devices: 7.84 us -> 3.01 us  [column(): lax.all_to_all(copies, HOPS, split_axis=0, concat_axis=0, tiled=True)]
    pallas_call x1 -> x0, Pallas kernels: 1.19 us -> none  [prepare(): pl.pallas_call(prepare_kernel, out_shape=(jax.ShapeDtypeStruct((512, 1024...]
    dynamic_slice x1 -> x2, local copies, waits for them, and re-layouts: 2.54 us -> 2.57 us  [piece(): return lax.dynamic_slice_in_dim(amplitudes[0], lax.rem(x + shift, 4) * 4, 4)]
  transfers between devices with their start and end apart: 6 -> 6, of which waited for: 4 -> 5; matrix products, arithmetic and copies ran while one was open for 4% -> 2% of each run, Pallas kernels for 1% -> 2%
where the time goes in v6:
time: 92.6 us; the launch traced here: 92.1 us
  starting transfers between devices  50.8 us (55%)
  blocking collectives  15.8 us (17%)
  waiting for transfers between devices  15.2 us (16%)
  Pallas kernels  5.33 us (6%)
  local copies, waits for them, and re-layouts  3.42 us (4%)
    all_to_all x1, starting transfers between devices, column(): lax.all_to_all(copies, HOPS, split_axis=0, concat_axis=0, tiled=True)  23.4 us
    all_to_all x1, blocking collectives, local(): lax.all_to_all(total, PLANE, split_axis=0, concat_axis=0, tiled=True)  15.8 us
    ppermute x3, starting transfers between devices, exchanged(): return lax.ppermute(piece, 'x', [(s, (s + shift) % 4) for s in range(4)])  12 us
    ppermute x3, waiting for transfers between devices, exchanged(): return lax.ppermute(piece, 'x', [(s, (s + shift) % 4) for s in range(4)])  9.23 us
    ppermute x1, starting transfers between devices, local(): packed = lax.ppermute(packed_before, AXES, owners())  8.29 us
    ppermute x1, starting transfers between devices, local(): total = own + lax.ppermute(given, 'core', [(0, 1), (1, 0)])  7.22 us
    pallas_call x1, Pallas kernels, multiply(): pl.pallas_call(lambda *refs: multiply_kernel(bool(sums), *refs), out_shap...  3.62 us
    all_to_all x1, waiting for transfers between devices, column(): lax.all_to_all(copies, HOPS, split_axis=0, concat_axis=0, tiled=True)  3.01 us
  transfers between devices with their start and end apart: 6, of which 5 were waited for; matrix products, arithmetic and copies ran while one was open for 2% of the time, Pallas kernels for 2%

profile of v6, /device:TPU:1, one launch (start us, length us, event | category | flops | bytes accessed | tf_op | source)
XLA Modules:
  0.0 92.1 jit_solution(4568779149685714426)
XLA Ops:
  0.0 1.1 %dynamic-slice_bitcast_fusion.1 = f32[4,128,256]{2,1,0:T(8,128)S(1)} fusion(f32[1,16,128,256]{3,2,1,0:T(8,128)} %param.8, s32[]{:T(128)S(6)} %select_n.14), kind=kLoop, calls=%fused_computation.1 | loop fusion | bytes 1048580 | tf_op jit(solution)/shard_map/dynamic_slice | solution.py:167
  1.1 5.5 %collective-permute-start.2 = (f32[4,128,256]{2,1,0:T(8,128)S(1)}, f32[4,128,256]{2,1,0:T(8,128)S(1)}, u32[]{:S(2)}, u32[]{:S(2)}) collective-permute-start(f32[4,128,256]{2,1,0:T(8,128)S(1)} %dynamic-slice_bitcast_fusion.1), channel_id=1, source_target_pairs={{0,16},{8,24},{16,0},{24,8},{1,17},{9,25},{17,1},{25,9},{2,18},{10... | collective-permute-start | bytes 1572872 | tf_op jit(solution)/shard_map/ppermute | solution.py:170
  6.6 1.7 %pack.2 = (f32[32,128]{1,0:T(8,128)S(1)}, s32[1]{0:T(128)}) custom-call(s32[1]{0:T(128)} %constant.27.clone.1.round_ref.refs_0_, s32[128]{0:T(128)} %refs_1_.1, s32[3]{0:T(128)} %refs_2_.1, s32[2,128]{1,0:T(2,128)} %bitcast.22, s32[1,128]{1,0:T(1,128)} %bitcast.25, f32[4,32,128]{2,1,0:T(8,128)} %w_ref.1), custom_call_target="tpu_custom_call" | custom-call | tf_op jit(solution)/shard_map/pack/pallas_call | solution.py:117
  8.3 8.3 %collective-permute-start.1 = (f32[32,128]{1,0:T(8,128)S(1)}, f32[32,128]{1,0:T(8,128)S(1)}, u32[]{:S(2)}, u32[]{:S(2)}) collective-permute-start(f32[32,128]{1,0:T(8,128)S(1)} %get-tuple-element.89), channel_id=1, source_target_pairs={{0,0},{1,32},{2,64},{3,96},{4,128},{5,160},{6,192},{7,224},{8,256}... | collective-permute-start | bytes 49160 | tf_op jit(solution)/shard_map/ppermute | solution.py:174
  16.6 0.0 copy-start.1
  16.6 0.0 copy-start.2
  16.6 0.0 copy-start.3
  16.6 0.0 copy-start.4
  16.6 1.5 %dynamic-slice_bitcast_fusion = (f32[4,128,256]{2,1,0:T(8,128)S(1)}, f32[4,128,256]{2,1,0:T(8,128)S(1)}, f32[4,128,256]{2,1,0:T(8,128)S(1)}) fusion(f32[1,16,128,256]{3,2,1,0:T(8,128)} %param.8, s32[]{:T(128)S(6)} %select_n.15, s32[]{:T(128)S(6)} %select_n.13, s32[]{:T(128)S(6)} %select_n.12), kind=kLoop, calls=%fused_computation | loop fusion | bytes 3145740 | tf_op jit(solution)/shard_map/dynamic_slice | solution.py:167
  18.2 1.6 %collective-permute-done.1 = f32[32,128]{1,0:T(8,128)S(1)} collective-permute-done((f32[32,128]{1,0:T(8,128)S(1)}, f32[32,128]{1,0:T(8,128)S(1)}, u32[]{:S(2)}, u32[]{:S(2)}) %collective-permute-start.1) | collective-permute-done | bytes 16416 | tf_op jit(solution)/shard_map/ppermute | solution.py:174
  19.8 0.0 collective-permute-done.2.refs_8_
  19.8 0.8 broadcast_in_dim.8
  20.6 23.4 %all-to-all-start.1 = ((f32[24,32,128]{2,1,0:T(8,128)}), f32[24,32,128]{2,1,0:T(8,128)S(1)}, u32[]{:S(2)}, u32[]{:S(2)}) async-start(f32[24,32,128]{2,1,0:T(8,128)} %broadcast_in_dim.8), calls=%async_computation.1 | async-start | bytes 786432 | tf_op jit(solution)/shard_map/all_to_all | solution.py:159
  44.0 2.1 %collective-permute-start.3 = (f32[4,128,256]{2,1,0:T(8,128)S(1)}, f32[4,128,256]{2,1,0:T(8,128)S(1)}, u32[]{:S(2)}, u32[]{:S(2)}) collective-permute-start(f32[4,128,256]{2,1,0:T(8,128)S(1)} %get-tuple-element.93), channel_id=1, source_target_pairs={{0,8},{8,16},{16,24},{24,0},{1,9},{9,17},{17,25},{25,1},{2,10},{10... | collective-permute-start | bytes 1572872 | tf_op jit(solution)/shard_map/ppermute | solution.py:170
  46.1 4.4 %collective-permute-start.4 = (f32[4,128,256]{2,1,0:T(8,128)S(1)}, f32[4,128,256]{2,1,0:T(8,128)}, u32[]{:S(2)}, u32[]{:S(2)}) collective-permute-start(f32[4,128,256]{2,1,0:T(8,128)S(1)} %get-tuple-element.95), channel_id=1, source_target_pairs={{0,24},{8,0},{16,8},{24,16},{1,25},{9,1},{17,9},{25,17},{2,26},{10... | collective-permute-start | bytes 1572872 | tf_op jit(solution)/shard_map/ppermute | solution.py:170
  50.5 8.3 %collective-permute-done.3.refs_7_ = f32[4,128,256]{2,1,0:T(8,128)S(1)} collective-permute-done((f32[4,128,256]{2,1,0:T(8,128)S(1)}, f32[4,128,256]{2,1,0:T(8,128)S(1)}, u32[]{:S(2)}, u32[]{:S(2)}) %collective-permute-start.3) | collective-permute-done | bytes 524320 | tf_op jit(solution)/shard_map/ppermute | solution.py:170
  58.8 0.9 collective-permute-done.4.refs_9_
  59.7 3.0 %all-to-all-done.1 = f32[24,32,128]{2,1,0:T(8,128)S(1)} async-done(((f32[24,32,128]{2,1,0:T(8,128)}), f32[24,32,128]{2,1,0:T(8,128)S(1)}, u32[]{:S(2)}, u32[]{:S(2)}) %all-to-all-start.1) | async-done | bytes 393248 | tf_op jit(solution)/shard_map/all_to_all | solution.py:159
  62.7 0.0 copy-done.5
  62.7 0.0 copy-done.1
  62.7 0.0 copy-done.2
  62.7 0.0 copy-done.3
  62.7 0.0 copy-done.4
  62.8 0.0 copy-start
  62.8 3.6 %multiply.2 = (f32[16,3,16,128]{3,2,1,0:T(8,128)S(1)}, f32[16,3,16,128]{3,2,1,0:T(8,128)S(1)}) custom-call(s32[1]{0:T(128)} %constant.27.clone.1.round_ref.refs_0_, s32[128]{0:T(128)S(1)} %copy-done.2, s32[3]{0:T(128)S(1)} %copy-done.3, s32[2,128]{1,0:T(2,128)S(1)} %bitcast.23, s32[1,128]{1,0:T(1,128)S(1)} %bitcast.26, f32[3,256,128]{2,1,0:T(8,128)S(1)} %bitcast.21, ...), custom_call_target="tpu_custom_call" | custom-call | flops 1207959552 | bytes 4194304 | tf_op jit(solution)/shard_map/multiply/pallas_call | solution.py:129
  66.4 0.0 copy-done
  66.4 0.6 while.12
  67.1 7.2 %collective-permute-start.5 = (f32[16,3,16,128]{3,2,1,0:T(8,128)S(1)}, f32[16,3,16,128]{3,2,1,0:T(8,128)S(1)}, u32[]{:S(2)}, u32[]{:S(2)}) collective-permute-start(f32[16,3,16,128]{3,2,1,0:T(8,128)S(1)} %get-tuple-element.100), channel_id=1, source_target_pairs={{0,1},{1,0},{2,3},{3,2},{4,5},{5,4},{6,7},{7,6},{8,9},{9,8},{10,11... | collective-permute-start | bytes 1179656 | tf_op jit(solution)/shard_map/ppermute | solution.py:185
  74.3 1.3 %collective-permute-done.5 = f32[16,3,16,128]{3,2,1,0:T(8,128)S(1)} collective-permute-done((f32[16,3,16,128]{3,2,1,0:T(8,128)S(1)}, f32[16,3,16,128]{3,2,1,0:T(8,128)S(1)}, u32[]{:S(2)}, u32[]{:S(2)}) %collective-permute-start.5) | collective-permute-done | bytes 393248 | tf_op jit(solution)/shard_map/ppermute | solution.py:185
  75.6 0.1 add.34
  75.7 15.8 %all_to_all.16 = f32[16,3,16,128]{3,2,1,0:T(8,128)S(1)} all-to-all(f32[16,3,16,128]{3,2,1,0:T(8,128)S(1)} %add.34), channel_id=1, replica_groups=mesh['z'=12,'y_hi'=2,'x'=4,'y_lo'=4,'core'=2] {'x','y_lo'}, dimensions={0} | all-to-all | bytes 786432 | tf_op jit(solution)/shard_map/all_to_all | solution.py:186
  91.4 0.6 reduce_sum.9
  (1 shorter events, 0.0 us)
Async XLA Ops:
  1.1 18.7 %collective-permute-start.2 = (f32[4,128,256]{2,1,0:T(8,128)S(1)}, f32[4,128,256]{2,1,0:T(8,128)S(1)}, u32[]{:S(2)}, u32[]{:S(2)}) collective-permute-start(f32[4,128,256]{2,1,0:T(8,128)S(1)} %dynamic-slice_bitcast_fusion.1), channel_id=1, source_target_pairs={{0,16},{8,24},{16,0},{24,8},{1,17},{9,25},{17,1},{25,9},{2,18},{10... | collective-permute-start | bytes 1572872 | tf_op jit(solution)/shard_map/ppermute | solution.py:170
  8.3 11.5 %collective-permute-start.1 = (f32[32,128]{1,0:T(8,128)S(1)}, f32[32,128]{1,0:T(8,128)S(1)}, u32[]{:S(2)}, u32[]{:S(2)}) collective-permute-start(f32[32,128]{1,0:T(8,128)S(1)} %get-tuple-element.89), channel_id=1, source_target_pairs={{0,0},{1,32},{2,64},{3,96},{4,128},{5,160},{6,192},{7,224},{8,256}... | collective-permute-start | bytes 49160 | tf_op jit(solution)/shard_map/ppermute | solution.py:174
  16.6 46.1 %copy-start.1 = (s32[256]{0:T(256)S(1)}, s32[256]{0:T(256)}, u32[]{:S(2)}) copy-start(s32[256]{0:T(256)} %param.12) | copy-start | bytes 3076
  16.6 46.1 %copy-start.2 = (s32[128]{0:T(128)S(1)}, s32[128]{0:T(128)}, u32[]{:S(2)}) copy-start(s32[128]{0:T(128)} %refs_1_.1) | copy-start | bytes 1540
  16.6 46.1 %copy-start.3 = (s32[3]{0:T(128)S(1)}, s32[3]{0:T(128)}, u32[]{:S(2)}) copy-start(s32[3]{0:T(128)} %refs_2_.1) | copy-start | bytes 40
  16.6 46.1 %copy-start.4 = (s32[128]{0:T(128)S(1)}, s32[128]{0:T(128)}, u32[]{:S(2)}) copy-start(s32[128]{0:T(128)} %param.13) | copy-start | bytes 1540
  20.6 42.1 %all-to-all-start.1 = ((f32[24,32,128]{2,1,0:T(8,128)}), f32[24,32,128]{2,1,0:T(8,128)S(1)}, u32[]{:S(2)}, u32[]{:S(2)}) async-start(f32[24,32,128]{2,1,0:T(8,128)} %broadcast_in_dim.8), calls=%async_computation.1 | async-start | bytes 786432 | tf_op jit(solution)/shard_map/all_to_all | solution.py:159
  44.0 14.8 %collective-permute-start.3 = (f32[4,128,256]{2,1,0:T(8,128)S(1)}, f32[4,128,256]{2,1,0:T(8,128)S(1)}, u32[]{:S(2)}, u32[]{:S(2)}) collective-permute-start(f32[4,128,256]{2,1,0:T(8,128)S(1)} %get-tuple-element.93), channel_id=1, source_target_pairs={{0,8},{8,16},{16,24},{24,0},{1,9},{9,17},{17,25},{25,1},{2,10},{10... | collective-permute-start | bytes 1572872 | tf_op jit(solution)/shard_map/ppermute | solution.py:170
  46.1 13.6 %collective-permute-start.4 = (f32[4,128,256]{2,1,0:T(8,128)S(1)}, f32[4,128,256]{2,1,0:T(8,128)}, u32[]{:S(2)}, u32[]{:S(2)}) collective-permute-start(f32[4,128,256]{2,1,0:T(8,128)S(1)} %get-tuple-element.95), channel_id=1, source_target_pairs={{0,24},{8,0},{16,8},{24,16},{1,25},{9,1},{17,9},{25,17},{2,26},{10... | collective-permute-start | bytes 1572872 | tf_op jit(solution)/shard_map/ppermute | solution.py:170
  58.8 3.9 %copy-start.5 = (f32[4,128,256]{2,1,0:T(8,128)}, f32[4,128,256]{2,1,0:T(8,128)S(1)}, u32[]{:S(2)}) copy-start(f32[4,128,256]{2,1,0:T(8,128)S(1)} %collective-permute-done.3.refs_7_) | copy-start | bytes 1572868
  62.8 3.6 %copy-start = (f32[4,32,128]{2,1,0:T(8,128)S(1)}, f32[4,32,128]{2,1,0:T(8,128)}, u32[]{:S(2)}) copy-start(f32[4,32,128]{2,1,0:T(8,128)} %w_ref.1) | copy-start | bytes 196612
  67.1 8.6 %collective-permute-start.5 = (f32[16,3,16,128]{3,2,1,0:T(8,128)S(1)}, f32[16,3,16,128]{3,2,1,0:T(8,128)S(1)}, u32[]{:S(2)}, u32[]{:S(2)}) collective-permute-start(f32[16,3,16,128]{3,2,1,0:T(8,128)S(1)} %get-tuple-element.100), channel_id=1, source_target_pairs={{0,1},{1,0},{2,3},{3,2},{4,5},{5,4},{6,7},{7,6},{8,9},{9,8},{10,11... | collective-permute-start | bytes 1179656 | tf_op jit(solution)/shard_map/ppermute | solution.py:185

commit v7 on v6

--- a/solution.py
+++ b/solution.py
@@ -10,6 +10,7 @@
 LANES = 128
 ROWS = 4
 SLAB = 32
+PREPARE_WEIGHT = 6_550_000_000
 PLACES = 32
 HOPS = ("z", "y_hi")
 PLANE = ("x", "y_lo")
@@ -66,8 +67,14 @@
     return high, (values - high.astype(jnp.float32)).astype(jnp.bfloat16)
 
 
+def prepare_kernel(t_ref, high_ref, low_ref):
+    for k in range(4):
+        high_ref[:, k * 256:(k + 1) * 256], low_ref[:, k * 256:(k + 1) * 256] = halves(t_ref[k])
+
+
 def multiply_kernel(with_sum, round_ref, occ_ref, j_ref, vir_ref, b_ref, w_ref, *rest):
-    t_refs, sums, (own_ref, given_ref, w_high, w_low, t_high, t_low) = rest[:4], rest[4:4 + 2 * with_sum], rest[4 + 2 * with_sum:]
+    t_refs, ready, rest = rest[:3], rest[3:5], rest[5:]
+    sums, (own_ref, given_ref, w_high, w_low, t_high, t_low) = rest[:2 * with_sum], rest[2 * with_sum:]
     label_b = b_ref[...]
     rank = ranks(label_b)
     label_c = jnp.concatenate([columns(vir_ref[half:half + 1, :]) for half in range(2)], axis=0)
@@ -84,10 +91,12 @@
             for spread, target in zip(spreads, (w_high, w_low)):
                 piece = spread[group * 256:(group + 1) * 256, part * LANES:(part + 1) * LANES]
                 target[k * 256:(k + 1) * 256, j * LANES:(j + 1) * LANES] = jnp.where(keep, piece, 0.0).astype(jnp.bfloat16)
-        for shift, t_ref in enumerate(t_refs):
+        for shift, t_ref in zip((0, 1, 3), t_refs):
             high, low = halves(t_ref[k])
             t_high[shift * LANES:(shift + 1) * LANES, k * 256:(k + 1) * 256] = high
             t_low[shift * LANES:(shift + 1) * LANES, k * 256:(k + 1) * 256] = low
+    for ref, target in zip(ready, (t_high, t_low)):
+        target[2 * LANES:3 * LANES, :] = ref[...]
     total = jnp.dot(t_high[...], w_high[...], preferred_element_type=jnp.float32)
     total = total + jnp.dot(t_high[...], w_low[...], preferred_element_type=jnp.float32)
     total = total + jnp.dot(t_low[...], w_high[...], preferred_element_type=jnp.float32)
@@ -125,11 +134,23 @@
     )(round_index, occ, j, vir, b, integrals)
 
 
+def prepare(t):
+    return pl.pallas_call(
+        prepare_kernel,
+        out_shape=(jax.ShapeDtypeStruct((LANES, 1024), jnp.bfloat16),) * 2,
+        in_specs=[VMEM],
+        out_specs=(VMEM, VMEM),
+        compiler_params=pltpu.CompilerParams(vmem_limit_bytes=8 << 20),
+        cost_estimate=pl.CostEstimate(flops=PREPARE_WEIGHT, bytes_accessed=1 << 20, transcendentals=0),
+        name="prepare",
+    )(t)
+
+
 def multiply(round_index, occ, j, vir, b, w, t, sums=()):
     return pl.pallas_call(
         lambda *refs: multiply_kernel(bool(sums), *refs),
         out_shape=(jax.ShapeDtypeStruct((16, J, 16, LANES), jnp.float32),) * 2,
-        in_specs=[SMEM] * 3 + [VMEM] * (7 + len(sums)),
+        in_specs=[SMEM] * 3 + [VMEM] * (8 + len(sums)),
         out_specs=(VMEM, VMEM),
         scratch_shapes=[pltpu.VMEM((1024, J * LANES), jnp.bfloat16)] * 2 + [pltpu.VMEM((512, 1024), jnp.bfloat16)] * 2,
         compiler_params=pltpu.CompilerParams(vmem_limit_bytes=24 << 20),
@@ -160,21 +181,19 @@
         return gathered.reshape(3, 256, LANES)
 
     packed, rounds = pack(jnp.zeros((1,), jnp.int32), *labels, integrals)
-    packed_before = packed
+    packed, amplitudes = lax.optimization_barrier((packed, amplitudes))
+    packed = lax.ppermute(packed, AXES, owners())
     x = lax.axis_index("x")
 
-    def piece(amplitudes, shift):
+    def piece(shift):
         return lax.dynamic_slice_in_dim(amplitudes[0], lax.rem(x + shift, 4) * 4, 4)
 
     def exchanged(piece, shift):
         return lax.ppermute(piece, "x", [(s, (s + shift) % 4) for s in range(4)])
 
-    opposite = exchanged(piece(amplitudes, 2), 2)
-    later, packed_before = lax.optimization_barrier((amplitudes, packed_before))
-    packed = lax.ppermute(packed_before, AXES, owners())
-    t = [piece(later, 0), piece(later, 1), opposite, piece(later, 3)]
-    packed, t = lax.optimization_barrier((packed, t))
-    t[1], t[3] = exchanged(t[1], 1), exchanged(t[3], 3)
+    opposite = prepare(exchanged(piece(2), 2))
+    packed, *near = lax.optimization_barrier((packed, piece(0), piece(1), piece(3)))
+    t = [near[0], exchanged(near[1], 1), exchanged(near[2], 3), *opposite]
     sums = multiply(jnp.zeros((1,), jnp.int32), *labels, column(packed), t)
 
     def another(state):

time: 92.6 us -> 87.6 us (0.946)
  waiting for transfers between devices: 15.2 us -> 11.9 us
  starting transfers between devices: 50.8 us -> 47.5 us
    all_to_all x1, starting transfers between devices: 23.4 us -> 8.27 us  [column(): lax.all_to_all(copies, HOPS, split_axis=0, concat_axis=0, tiled=True)]
    ppermute x3, starting transfers between devices: 12 us -> 23.3 us  [exchanged(): return lax.ppermute(piece, 'x', [(s, (s + shift) % 4) for s in range(4)])]
    ppermute x1, waiting for transfers between devices: 1.64 us -> 0.01 us  [local(): packed = lax.ppermute(packed, AXES, owners())]
    ppermute x3, waiting for transfers between devices: 9.23 us -> 8.18 us  [exchanged(): return lax.ppermute(piece, 'x', [(s, (s + shift) % 4) for s in range(4)])]
    dynamic_slice x2 -> x1, local copies, waits for them, and re-layouts: 2.57 us -> 1.72 us  [piece(): return lax.dynamic_slice_in_dim(amplitudes[0], lax.rem(x + shift, 4) * 4, 4)]
  transfers between devices with their start and end apart: 6 -> 6, of which waited for: 5 -> 4; matrix products, arithmetic and copies ran while one was open for 2% -> 3% of each run, Pallas kernels for 2% -> 1%
where the time goes in v7:
time: 87.6 us; the launch traced here: 87.1 us
  starting transfers between devices  47.5 us (54%)
  blocking collectives  16.6 us (19%)
  waiting for transfers between devices  11.9 us (14%)
  Pallas kernels  6.15 us (7%)
  local copies, waits for them, and re-layouts  3.37 us (4%)
    ppermute x3, starting transfers between devices, exchanged(): return lax.ppermute(piece, 'x', [(s, (s + shift) % 4) for s in range(4)])  23.3 us
    all_to_all x1, blocking collectives, local(): lax.all_to_all(total, PLANE, split_axis=0, concat_axis=0, tiled=True)  16.6 us
    ppermute x1, starting transfers between devices, local(): packed = lax.ppermute(packed, AXES, owners())  8.84 us
    all_to_all x1, starting transfers between devices, column(): lax.all_to_all(copies, HOPS, split_axis=0, concat_axis=0, tiled=True)  8.27 us
    ppermute x3, waiting for transfers between devices, exchanged(): return lax.ppermute(piece, 'x', [(s, (s + shift) % 4) for s in range(4)])  8.18 us
    ppermute x1, starting transfers between devices, local(): total = own + lax.ppermute(given, 'core', [(0, 1), (1, 0)])  7.11 us
    pallas_call x1, Pallas kernels, multiply(): pl.pallas_call(lambda *refs: multiply_kernel(bool(sums), *refs), out_shap...  3.69 us
    all_to_all x1, waiting for transfers between devices, column(): lax.all_to_all(copies, HOPS, split_axis=0, concat_axis=0, tiled=True)  2.42 us
  transfers between devices with their start and end apart: 6, of which 4 were waited for; matrix products, arithmetic and copies ran while one was open for 3% of the time, Pallas kernels for 1%

profile of v7, /device:TPU:1, one launch (start us, length us, event | category | flops | bytes accessed | tf_op | source)
XLA Modules:
  0.0 87.1 jit_solution(15696316845832267243)
XLA Ops:
  0.0 1.7 %pack.2 = (f32[32,128]{1,0:T(8,128)S(1)}, s32[1]{0:T(128)}) custom-call(s32[1]{0:T(128)} %constant.27.clone.1.round_ref.refs_0_, s32[128]{0:T(128)} %refs_1_.1, s32[3]{0:T(128)} %refs_2_.1, s32[2,128]{1,0:T(2,128)} %bitcast.22, s32[1,128]{1,0:T(1,128)} %bitcast.25, f32[4,32,128]{2,1,0:T(8,128)} %w_ref.1), custom_call_target="tpu_custom_call" | custom-call | tf_op jit(solution)/shard_map/pack/pallas_call | solution.py:126
  1.7 8.8 %collective-permute-start.1 = (f32[32,128]{1,0:T(8,128)S(1)}, f32[32,128]{1,0:T(8,128)S(1)}, u32[]{:S(2)}, u32[]{:S(2)}) collective-permute-start(f32[32,128]{1,0:T(8,128)S(1)} %get-tuple-element.95), channel_id=1, source_target_pairs={{0,0},{1,32},{2,64},{3,96},{4,128},{5,160},{6,192},{7,224},{8,256}... | collective-permute-start | bytes 49160 | tf_op jit(solution)/shard_map/ppermute | solution.py:185
  10.6 1.7 %dynamic-slice_bitcast_fusion = (f32[4,128,256]{2,1,0:T(8,128)S(1)}, f32[4,128,256]{2,1,0:T(8,128)S(1)}, f32[4,128,256]{2,1,0:T(8,128)S(1)}, f32[4,128,256]{2,1,0:T(8,128)S(1)}) fusion(f32[1,16,128,256]{3,2,1,0:T(8,128)} %param.8, s32[]{:T(128)S(6)} %select_n.15, s32[]{:T(128)S(6)} %select_n.14, s32[]{:T(128)S(6)} %select_n.13, s32[]{:T(128)S(6)} %select_n.12), kind=kLoop, calls=%fused_computation | loop fusion | bytes 4194320 | tf_op jit(solution)/shard_map/dynamic_slice | solution.py:189
  12.3 16.7 %collective-permute-start.4 = (f32[4,128,256]{2,1,0:T(8,128)S(1)}, f32[4,128,256]{2,1,0:T(8,128)S(1)}, u32[]{:S(2)}, u32[]{:S(2)}) collective-permute-start(f32[4,128,256]{2,1,0:T(8,128)S(1)} %get-tuple-element.136), channel_id=1, source_target_pairs={{0,16},{8,24},{16,0},{24,8},{1,17},{9,25},{17,1},{25,9},{2,18},{10... | collective-permute-start | bytes 1572872 | tf_op jit(solution)/shard_map/ppermute | solution.py:192
  29.0 0.0 collective-permute-done.1
  29.0 0.8 broadcast_in_dim.8
  29.8 8.3 %all-to-all-start.1 = ((f32[24,32,128]{2,1,0:T(8,128)}), f32[24,32,128]{2,1,0:T(8,128)S(1)}, u32[]{:S(2)}, u32[]{:S(2)}) async-start(f32[24,32,128]{2,1,0:T(8,128)} %broadcast_in_dim.8), calls=%async_computation.1 | async-start | bytes 786432 | tf_op jit(solution)/shard_map/all_to_all | solution.py:180
  38.1 0.0 copy-start.1
  38.1 0.0 copy-start.2
  38.1 0.0 copy-start.3
  38.1 0.0 copy-start.4
  38.1 3.3 %collective-permute-start.2 = (f32[4,128,256]{2,1,0:T(8,128)S(1)}, f32[4,128,256]{2,1,0:T(8,128)S(1)}, u32[]{:S(2)}, u32[]{:S(2)}) collective-permute-start(f32[4,128,256]{2,1,0:T(8,128)S(1)} %get-tuple-element.99), channel_id=1, source_target_pairs={{0,8},{8,16},{16,24},{24,0},{1,9},{9,17},{17,25},{25,1},{2,10},{10... | collective-permute-start | bytes 1572872 | tf_op jit(solution)/shard_map/ppermute | solution.py:192
  41.4 3.4 %collective-permute-start.3 = (f32[4,128,256]{2,1,0:T(8,128)S(1)}, f32[4,128,256]{2,1,0:T(8,128)}, u32[]{:S(2)}, u32[]{:S(2)}) collective-permute-start(f32[4,128,256]{2,1,0:T(8,128)S(1)} %get-tuple-element.100), channel_id=1, source_target_pairs={{0,24},{8,0},{16,8},{24,16},{1,25},{9,1},{17,9},{25,17},{2,26},{10... | collective-permute-start | bytes 1572872 | tf_op jit(solution)/shard_map/ppermute | solution.py:192
  44.8 0.0 collective-permute-done.4.t_ref
  44.8 0.8 prepare.1
  45.6 7.6 %collective-permute-done.2.refs_7_ = f32[4,128,256]{2,1,0:T(8,128)S(1)} collective-permute-done((f32[4,128,256]{2,1,0:T(8,128)S(1)}, f32[4,128,256]{2,1,0:T(8,128)S(1)}, u32[]{:S(2)}, u32[]{:S(2)}) %collective-permute-start.2) | collective-permute-done | bytes 524320 | tf_op jit(solution)/shard_map/ppermute | solution.py:192
  53.2 0.8 copy-done.5
  54.0 0.6 collective-permute-done.3.refs_8_
  54.5 2.4 %all-to-all-done.1 = f32[24,32,128]{2,1,0:T(8,128)S(1)} async-done(((f32[24,32,128]{2,1,0:T(8,128)}), f32[24,32,128]{2,1,0:T(8,128)S(1)}, u32[]{:S(2)}, u32[]{:S(2)}) %all-to-all-start.1) | async-done | bytes 393248 | tf_op jit(solution)/shard_map/all_to_all | solution.py:180
  57.0 0.0 copy-done.1
  57.0 0.0 copy-done.2
  57.0 0.0 copy-done.3
  57.0 0.0 copy-done.4
  57.0 0.0 copy-start
  57.0 3.7 %multiply.2 = (f32[16,3,16,128]{3,2,1,0:T(8,128)S(1)}, f32[16,3,16,128]{3,2,1,0:T(8,128)S(1)}) custom-call(s32[1]{0:T(128)} %constant.27.clone.1.round_ref.refs_0_, s32[128]{0:T(128)S(1)} %copy-done.2, s32[3]{0:T(128)S(1)} %copy-done.3, s32[2,128]{1,0:T(2,128)S(1)} %bitcast.23, s32[1,128]{1,0:T(1,128)S(1)} %bitcast.26, f32[3,256,128]{2,1,0:T(8,128)S(1)} %bitcast.21, ...), custom_call_target="tpu_custom_call" | custom-call | flops 1207959552 | bytes 4194304 | tf_op jit(solution)/shard_map/multiply/pallas_call | solution.py:150
  60.7 0.0 copy-done
  60.7 0.7 while.12
  61.4 7.1 %collective-permute-start.5 = (f32[16,3,16,128]{3,2,1,0:T(8,128)S(1)}, f32[16,3,16,128]{3,2,1,0:T(8,128)S(1)}, u32[]{:S(2)}, u32[]{:S(2)}) collective-permute-start(f32[16,3,16,128]{3,2,1,0:T(8,128)S(1)} %get-tuple-element.107), channel_id=1, source_target_pairs={{0,1},{1,0},{2,3},{3,2},{4,5},{5,4},{6,7},{7,6},{8,9},{9,8},{10,11... | collective-permute-start | bytes 1179656 | tf_op jit(solution)/shard_map/ppermute | solution.py:204
  68.5 1.3 %collective-permute-done.5 = f32[16,3,16,128]{3,2,1,0:T(8,128)S(1)} collective-permute-done((f32[16,3,16,128]{3,2,1,0:T(8,128)S(1)}, f32[16,3,16,128]{3,2,1,0:T(8,128)S(1)}, u32[]{:S(2)}, u32[]{:S(2)}) %collective-permute-start.5) | collective-permute-done | bytes 393248 | tf_op jit(solution)/shard_map/ppermute | solution.py:204
  69.9 0.1 add.34
  69.9 16.6 %all_to_all.16 = f32[16,3,16,128]{3,2,1,0:T(8,128)S(1)} all-to-all(f32[16,3,16,128]{3,2,1,0:T(8,128)S(1)} %add.34), channel_id=1, replica_groups=mesh['z'=12,'y_hi'=2,'x'=4,'y_lo'=4,'core'=2] {'x','y_lo'}, dimensions={0} | all-to-all | bytes 786432 | tf_op jit(solution)/shard_map/all_to_all | solution.py:205
  86.5 0.6 reduce_sum.9
  (1 shorter events, 0.0 us)
Async XLA Ops:
  1.7 27.3 %collective-permute-start.1 = (f32[32,128]{1,0:T(8,128)S(1)}, f32[32,128]{1,0:T(8,128)S(1)}, u32[]{:S(2)}, u32[]{:S(2)}) collective-permute-start(f32[32,128]{1,0:T(8,128)S(1)} %get-tuple-element.95), channel_id=1, source_target_pairs={{0,0},{1,32},{2,64},{3,96},{4,128},{5,160},{6,192},{7,224},{8,256}... | collective-permute-start | bytes 49160 | tf_op jit(solution)/shard_map/ppermute | solution.py:185
  12.3 32.5 %collective-permute-start.4 = (f32[4,128,256]{2,1,0:T(8,128)S(1)}, f32[4,128,256]{2,1,0:T(8,128)S(1)}, u32[]{:S(2)}, u32[]{:S(2)}) collective-permute-start(f32[4,128,256]{2,1,0:T(8,128)S(1)} %get-tuple-element.136), channel_id=1, source_target_pairs={{0,16},{8,24},{16,0},{24,8},{1,17},{9,25},{17,1},{25,9},{2,18},{10... | collective-permute-start | bytes 1572872 | tf_op jit(solution)/shard_map/ppermute | solution.py:192
  29.8 27.1 %all-to-all-start.1 = ((f32[24,32,128]{2,1,0:T(8,128)}), f32[24,32,128]{2,1,0:T(8,128)S(1)}, u32[]{:S(2)}, u32[]{:S(2)}) async-start(f32[24,32,128]{2,1,0:T(8,128)} %broadcast_in_dim.8), calls=%async_computation.1 | async-start | bytes 786432 | tf_op jit(solution)/shard_map/all_to_all | solution.py:180
  38.1 18.9 %copy-start.1 = (s32[256]{0:T(256)S(1)}, s32[256]{0:T(256)}, u32[]{:S(2)}) copy-start(s32[256]{0:T(256)} %param.12) | copy-start | bytes 3076
  38.1 18.9 %copy-start.2 = (s32[128]{0:T(128)S(1)}, s32[128]{0:T(128)}, u32[]{:S(2)}) copy-start(s32[128]{0:T(128)} %refs_1_.1) | copy-start | bytes 1540
  38.1 18.9 %copy-start.3 = (s32[3]{0:T(128)S(1)}, s32[3]{0:T(128)}, u32[]{:S(2)}) copy-start(s32[3]{0:T(128)} %refs_2_.1) | copy-start | bytes 40
  38.1 18.8 %copy-start.4 = (s32[128]{0:T(128)S(1)}, s32[128]{0:T(128)}, u32[]{:S(2)}) copy-start(s32[128]{0:T(128)} %param.13) | copy-start | bytes 1540
  38.1 15.0 %collective-permute-start.2 = (f32[4,128,256]{2,1,0:T(8,128)S(1)}, f32[4,128,256]{2,1,0:T(8,128)S(1)}, u32[]{:S(2)}, u32[]{:S(2)}) collective-permute-start(f32[4,128,256]{2,1,0:T(8,128)S(1)} %get-tuple-element.99), channel_id=1, source_target_pairs={{0,8},{8,16},{16,24},{24,0},{1,9},{9,17},{17,25},{25,1},{2,10},{10... | collective-permute-start | bytes 1572872 | tf_op jit(solution)/shard_map/ppermute | solution.py:192
  41.4 13.1 %collective-permute-start.3 = (f32[4,128,256]{2,1,0:T(8,128)S(1)}, f32[4,128,256]{2,1,0:T(8,128)}, u32[]{:S(2)}, u32[]{:S(2)}) collective-permute-start(f32[4,128,256]{2,1,0:T(8,128)S(1)} %get-tuple-element.100), channel_id=1, source_target_pairs={{0,24},{8,0},{16,8},{24,16},{1,25},{9,1},{17,9},{25,17},{2,26},{10... | collective-permute-start | bytes 1572872 | tf_op jit(solution)/shard_map/ppermute | solution.py:192
  53.1 0.8 copy-start.5
  57.0 3.7 %copy-start = (f32[4,32,128]{2,1,0:T(8,128)S(1)}, f32[4,32,128]{2,1,0:T(8,128)}, u32[]{:S(2)}) copy-start(f32[4,32,128]{2,1,0:T(8,128)} %w_ref.1) | copy-start | bytes 196612
  61.4 8.4 %collective-permute-start.5 = (f32[16,3,16,128]{3,2,1,0:T(8,128)S(1)}, f32[16,3,16,128]{3,2,1,0:T(8,128)S(1)}, u32[]{:S(2)}, u32[]{:S(2)}) collective-permute-start(f32[16,3,16,128]{3,2,1,0:T(8,128)S(1)} %get-tuple-element.107), channel_id=1, source_target_pairs={{0,1},{1,0},{2,3},{3,2},{4,5},{5,4},{6,7},{7,6},{8,9},{9,8},{10,11... | collective-permute-start | bytes 1179656 | tf_op jit(solution)/shard_map/ppermute | solution.py:204

commit v8 on v7

--- a/solution.py
+++ b/solution.py
@@ -41,44 +41,50 @@
     return lax.axis_index("y_lo") * 2 + lax.axis_index("core")
 
 
+def halves(values):
+    high = values.astype(jnp.bfloat16)
+    return high, (values - high.astype(jnp.float32)).astype(jnp.bfloat16)
+
+
 def pack_kernel(round_ref, occ_ref, j_ref, vir_ref, b_ref, w_ref, out_ref, rounds_ref, labels):
     label_b = b_ref[...]
     rank = ranks(label_b)
-    for half in range(2):
-        labels[half * LANES:(half + 1) * LANES, :] = columns(vir_ref[half:half + 1, :])
-    start = pl.multiple_of(vir_index() * SLAB, SLAB)
+    slab = vir_index()
+    labels[...] = columns(vir_ref[pl.ds(slab // 4, 1), :])
+    start = pl.multiple_of(slab % 4 * SLAB, SLAB)
     right = jnp.bitwise_xor(labels[pl.ds(start, SLAB), :], label_b)
     first = occ_index() * ROWS
-    total = jnp.zeros((SLAB, LANES), jnp.float32)
+    kept, put = [], []
     for part in range(ROWS):
         k = lax.div(first + part, J)
         left = jnp.bitwise_xor(occ_ref[k], j_ref[first + part - k * J])
-        kept = jnp.where(right == left, w_ref[part], 0.0)
-        put = jnp.where(placing(rank, round_ref[0], part), 1.0, 0.0)
-        total = total + lax.dot_general(
-            kept, put, (((1,), (1,)), ((), ())), precision=lax.Precision.HIGHEST, preferred_element_type=jnp.float32
-        )
-    out_ref[...] = total
+        kept.append(jnp.where(right == left, w_ref[part], 0.0))
+        put.append(jnp.where(placing(rank, round_ref[0], part), 1.0, 0.0).astype(jnp.bfloat16))
+    kept, put = jnp.concatenate(kept, axis=1), jnp.concatenate(put, axis=1)
+    high = kept.astype(jnp.bfloat16)
+    rest = kept - high.astype(jnp.float32)
+    middle, low = halves(rest)
+    pieces = lax.dot_general(
+        jnp.concatenate([high, middle, low], axis=0), put, (((1,), (1,)), ((), ())), preferred_element_type=jnp.float32
+    )
+    out_ref[...] = (pieces[:SLAB] + pieces[SLAB:2 * SLAB]) + pieces[2 * SLAB:]
     rounds_ref[0] = lax.div(jnp.max(rank) + PLACES, PLACES)
 
 
-def halves(values):
-    high = values.astype(jnp.bfloat16)
-    return high, (values - high.astype(jnp.float32)).astype(jnp.bfloat16)
-
-
-def prepare_kernel(t_ref, high_ref, low_ref):
+def prepare_kernel(vir_ref, b_ref, t_ref, rank_ref, right_ref, high_ref, low_ref):
+    label_b = b_ref[...]
+    rank_ref[...] = ranks(label_b)
+    for half in range(2):
+        label_c = columns(vir_ref[half:half + 1, :])
+        right_ref[half * LANES:(half + 1) * LANES, :] = jnp.bitwise_xor(label_c, label_b)
     for k in range(4):
         high_ref[:, k * 256:(k + 1) * 256], low_ref[:, k * 256:(k + 1) * 256] = halves(t_ref[k])
 
 
-def multiply_kernel(with_sum, round_ref, occ_ref, j_ref, vir_ref, b_ref, w_ref, *rest):
+def multiply_kernel(with_sum, round_ref, occ_ref, j_ref, rank_ref, right_ref, w_ref, *rest):
     t_refs, ready, rest = rest[:3], rest[3:5], rest[5:]
-    sums, (own_ref, given_ref, w_high, w_low, t_high, t_low) = rest[:2 * with_sum], rest[2 * with_sum:]
-    label_b = b_ref[...]
-    rank = ranks(label_b)
-    label_c = jnp.concatenate([columns(vir_ref[half:half + 1, :]) for half in range(2)], axis=0)
-    right = jnp.bitwise_xor(label_c, label_b)
+    sums, (own_ref, given_ref, w_both, t_high, t_low) = rest[:2 * with_sum], rest[2 * with_sum:]
+    rank, right = rank_ref[...], right_ref[...]
     put = jnp.concatenate(
         [jnp.where(placing(rank, round_ref[0], part), 1.0, 0.0).astype(jnp.bfloat16) for part in range(ROWS)], axis=1
     )
@@ -88,18 +94,19 @@
         for j in range(J):
             group, part = divmod(k * J + j, ROWS)
             keep = right == jnp.bitwise_xor(occ_ref[first + k], j_ref[j])
-            for spread, target in zip(spreads, (w_high, w_low)):
+            for half, spread in enumerate(spreads):
                 piece = spread[group * 256:(group + 1) * 256, part * LANES:(part + 1) * LANES]
-                target[k * 256:(k + 1) * 256, j * LANES:(j + 1) * LANES] = jnp.where(keep, piece, 0.0).astype(jnp.bfloat16)
+                column = (half * J + j) * LANES
+                w_both[k * 256:(k + 1) * 256, column:column + LANES] = jnp.where(keep, piece, 0.0).astype(jnp.bfloat16)
         for shift, t_ref in zip((0, 1, 3), t_refs):
             high, low = halves(t_ref[k])
             t_high[shift * LANES:(shift + 1) * LANES, k * 256:(k + 1) * 256] = high
             t_low[shift * LANES:(shift + 1) * LANES, k * 256:(k + 1) * 256] = low
     for ref, target in zip(ready, (t_high, t_low)):
         target[2 * LANES:3 * LANES, :] = ref[...]
-    total = jnp.dot(t_high[...], w_high[...], preferred_element_type=jnp.float32)
-    total = total + jnp.dot(t_high[...], w_low[...], preferred_element_type=jnp.float32)
-    total = total + jnp.dot(t_low[...], w_high[...], preferred_element_type=jnp.float32)
+    both = jnp.dot(t_high[...], w_both[...], preferred_element_type=jnp.float32)
+    total = both[:, :J * LANES] + both[:, J * LANES:]
+    total = total + jnp.dot(t_low[...], w_both[:, :J * LANES], preferred_element_type=jnp.float32)
     core = lax.axis_index("core")
 
     def put_out(own, given):
@@ -128,35 +135,36 @@
         out_shape=(jax.ShapeDtypeStruct((SLAB, LANES), jnp.float32), jax.ShapeDtypeStruct((1,), jnp.int32)),
         in_specs=[SMEM, SMEM, SMEM, VMEM, VMEM, VMEM],
         out_specs=(VMEM, SMEM),
-        scratch_shapes=[pltpu.VMEM((256, LANES), jnp.int32)],
+        scratch_shapes=[pltpu.VMEM((LANES, LANES), jnp.int32)],
         compiler_params=pltpu.CompilerParams(vmem_limit_bytes=8 << 20),
         name="pack",
     )(round_index, occ, j, vir, b, integrals)
 
 
-def prepare(t):
+def prepare(vir, b, t):
     return pl.pallas_call(
         prepare_kernel,
-        out_shape=(jax.ShapeDtypeStruct((LANES, 1024), jnp.bfloat16),) * 2,
-        in_specs=[VMEM],
-        out_specs=(VMEM, VMEM),
+        out_shape=(jax.ShapeDtypeStruct((1, LANES), jnp.int32), jax.ShapeDtypeStruct((256, LANES), jnp.int32))
+        + (jax.ShapeDtypeStruct((LANES, 1024), jnp.bfloat16),) * 2,
+        in_specs=[VMEM] * 3,
+        out_specs=(VMEM,) * 4,
         compiler_params=pltpu.CompilerParams(vmem_limit_bytes=8 << 20),
         cost_estimate=pl.CostEstimate(flops=PREPARE_WEIGHT, bytes_accessed=1 << 20, transcendentals=0),
         name="prepare",
-    )(t)
-
-
-def multiply(round_index, occ, j, vir, b, w, t, sums=()):
+    )(vir, b, t)
+
+
+def multiply(round_index, occ, j, rank, right, w, t, sums=()):
     return pl.pallas_call(
         lambda *refs: multiply_kernel(bool(sums), *refs),
         out_shape=(jax.ShapeDtypeStruct((16, J, 16, LANES), jnp.float32),) * 2,
         in_specs=[SMEM] * 3 + [VMEM] * (8 + len(sums)),
         out_specs=(VMEM, VMEM),
-        scratch_shapes=[pltpu.VMEM((1024, J * LANES), jnp.bfloat16)] * 2 + [pltpu.VMEM((512, 1024), jnp.bfloat16)] * 2,
+        scratch_shapes=[pltpu.VMEM((1024, 2 * J * LANES), jnp.bfloat16)] + [pltpu.VMEM((512, 1024), jnp.bfloat16)] * 2,
         compiler_params=pltpu.CompilerParams(vmem_limit_bytes=24 << 20),
         cost_estimate=pl.CostEstimate(flops=3 * 2 * 512 * 1024 * 384, bytes_accessed=4 << 20, transcendentals=0),
         name="multiply",
-    )(round_index, occ, j, vir, b, w, *t, *sums)
+    )(round_index, occ, j, rank, right, w, *t, *sums)
 
 
 def owners():
@@ -191,14 +199,15 @@
     def exchanged(piece, shift):
         return lax.ppermute(piece, "x", [(s, (s + shift) % 4) for s in range(4)])
 
-    opposite = prepare(exchanged(piece(2), 2))
+    rank, right, *opposite = prepare(vir, b, exchanged(piece(2), 2))
+    known = (irrep_occ, irrep_j, rank, right)
     packed, *near = lax.optimization_barrier((packed, piece(0), piece(1), piece(3)))
     t = [near[0], exchanged(near[1], 1), exchanged(near[2], 3), *opposite]
-    sums = multiply(jnp.zeros((1,), jnp.int32), *labels, column(packed), t)
+    sums = multiply(jnp.zeros((1,), jnp.int32), *known, column(packed), t)
 
     def another(state):
         index, sums = state
-        return index + 1, multiply(index[None], *labels, column(owned(index[None])), t, sums)
+        return index + 1, multiply(index[None], *known, column(owned(index[None])), t, sums)
 
     _, (own, given) = lax.while_loop(lambda state: state[0] < rounds[0], another, (jnp.int32(1), sums))
     total = own + lax.ppermute(given, "core", [(0, 1), (1, 0)])

time: 87.6 us -> 87.3 us (level)
  no operation moved by 1% of the time
where the time goes in v8:
time: 87.3 us; the launch traced here: 86.8 us
  starting transfers between devices  47.4 us (54%)
  blocking collectives  16.6 us (19%)
  waiting for transfers between devices  12 us (14%)
  Pallas kernels  5.93 us (7%)
  local copies, waits for them, and re-layouts  3.35 us (4%)
    ppermute x3, starting transfers between devices, exchanged(): return lax.ppermute(piece, 'x', [(s, (s + shift) % 4) for s in range(4)])  23.2 us
    all_to_all x1, blocking collectives, local(): lax.all_to_all(total, PLANE, split_axis=0, concat_axis=0, tiled=True)  16.6 us
    ppermute x1, starting transfers between devices, local(): packed = lax.ppermute(packed, AXES, owners())  8.84 us
    all_to_all x1, starting transfers between devices, column(): lax.all_to_all(copies, HOPS, split_axis=0, concat_axis=0, tiled=True)  8.24 us
    ppermute x3, waiting for transfers between devices, exchanged(): return lax.ppermute(piece, 'x', [(s, (s + shift) % 4) for s in range(4)])  8.04 us
    ppermute x1, starting transfers between devices, local(): total = own + lax.ppermute(given, 'core', [(0, 1), (1, 0)])  7.17 us
    pallas_call x1, Pallas kernels, multiply(): pl.pallas_call(lambda *refs: multiply_kernel(bool(sums), *refs), out_shap...  3.34 us
    all_to_all x1, waiting for transfers between devices, column(): lax.all_to_all(copies, HOPS, split_axis=0, concat_axis=0, tiled=True)  2.59 us
  transfers between devices with their start and end apart: 6, of which 4 were waited for; matrix products, arithmetic and copies ran while one was open for 3% of the time, Pallas kernels for 1%

profile of v8, /device:TPU:1, one launch (start us, length us, event | category | flops | bytes accessed | tf_op | source)
XLA Modules:
  0.0 86.8 jit_solution(12326832216386589679)
XLA Ops:
  0.0 1.7 %pack.2 = (f32[32,128]{1,0:T(8,128)S(1)}, s32[1]{0:T(128)}) custom-call(s32[1]{0:T(128)} %constant.27.clone.1.round_ref.refs_0_, s32[128]{0:T(128)} %refs_1_.1, s32[3]{0:T(128)} %refs_2_.1, s32[2,128]{1,0:T(2,128)} %bitcast.22, s32[1,128]{1,0:T(1,128)} %bitcast.25, f32[4,32,128]{2,1,0:T(8,128)} %w_ref.1), custom_call_target="tpu_custom_call" | custom-call | tf_op jit(solution)/shard_map/pack/pallas_call | solution.py:133
  1.7 8.8 %collective-permute-start.2 = (f32[32,128]{1,0:T(8,128)S(1)}, f32[32,128]{1,0:T(8,128)S(1)}, u32[]{:S(2)}, u32[]{:S(2)}) collective-permute-start(f32[32,128]{1,0:T(8,128)S(1)} %get-tuple-element.110), channel_id=1, source_target_pairs={{0,0},{1,32},{2,64},{3,96},{4,128},{5,160},{6,192},{7,224},{8,256}... | collective-permute-start | bytes 49160 | tf_op jit(solution)/shard_map/ppermute | solution.py:193
  10.6 0.0 copy-start.1
  10.6 0.0 copy-start.4
  10.6 1.7 %dynamic-slice_bitcast_fusion = (f32[4,128,256]{2,1,0:T(8,128)S(1)}, f32[4,128,256]{2,1,0:T(8,128)S(1)}, f32[4,128,256]{2,1,0:T(8,128)S(1)}, f32[4,128,256]{2,1,0:T(8,128)S(1)}) fusion(f32[1,16,128,256]{3,2,1,0:T(8,128)} %param.8, s32[]{:T(128)S(6)} %select_n.15, s32[]{:T(128)S(6)} %select_n.14, s32[]{:T(128)S(6)} %select_n.13, s32[]{:T(128)S(6)} %select_n.12), kind=kLoop, calls=%fused_computation | loop fusion | bytes 4194320 | tf_op jit(solution)/shard_map/dynamic_slice | solution.py:197
  12.3 16.7 %collective-permute-start.1 = (f32[4,128,256]{2,1,0:T(8,128)S(1)}, f32[4,128,256]{2,1,0:T(8,128)S(1)}, u32[]{:S(2)}, u32[]{:S(2)}) collective-permute-start(f32[4,128,256]{2,1,0:T(8,128)S(1)} %get-tuple-element.157), channel_id=1, source_target_pairs={{0,16},{8,24},{16,0},{24,8},{1,17},{9,25},{17,1},{25,9},{2,18},{10... | collective-permute-start | bytes 1572872 | tf_op jit(solution)/shard_map/ppermute | solution.py:200
  29.0 0.0 collective-permute-done.2
  29.0 0.8 broadcast_in_dim.8
  29.8 8.2 %all-to-all-start.1 = ((f32[24,32,128]{2,1,0:T(8,128)}), f32[24,32,128]{2,1,0:T(8,128)S(1)}, u32[]{:S(2)}, u32[]{:S(2)}) async-start(f32[24,32,128]{2,1,0:T(8,128)} %broadcast_in_dim.8), calls=%async_computation.1 | async-start | bytes 786432 | tf_op jit(solution)/shard_map/all_to_all | solution.py:188
  38.1 0.0 copy-start.2
  38.1 0.0 copy-start.3
  38.1 3.1 %collective-permute-start.3 = (f32[4,128,256]{2,1,0:T(8,128)S(1)}, f32[4,128,256]{2,1,0:T(8,128)S(1)}, u32[]{:S(2)}, u32[]{:S(2)}) collective-permute-start(f32[4,128,256]{2,1,0:T(8,128)S(1)} %get-tuple-element.113), channel_id=1, source_target_pairs={{0,8},{8,16},{16,24},{24,0},{1,9},{9,17},{17,25},{25,1},{2,10},{10... | collective-permute-start | bytes 1572872 | tf_op jit(solution)/shard_map/ppermute | solution.py:200
  41.3 3.4 %collective-permute-start.4 = (f32[4,128,256]{2,1,0:T(8,128)S(1)}, f32[4,128,256]{2,1,0:T(8,128)}, u32[]{:S(2)}, u32[]{:S(2)}) collective-permute-start(f32[4,128,256]{2,1,0:T(8,128)S(1)} %get-tuple-element.114), channel_id=1, source_target_pairs={{0,24},{8,0},{16,8},{24,16},{1,25},{9,1},{17,9},{25,17},{2,26},{10... | collective-permute-start | bytes 1572872 | tf_op jit(solution)/shard_map/ppermute | solution.py:200
  44.6 0.0 collective-permute-done.1.t_ref
  44.6 0.0 copy-done.1
  44.6 0.0 copy-done.4
  44.7 0.9 %prepare.1 = (s32[1,128]{1,0:T(1,128)S(1)}, s32[256,128]{1,0:T(8,128)S(1)}, bf16[128,1024]{1,0:T(8,128)(2,1)S(1)}, bf16[128,1024]{1,0:T(8,128)(2,1)}) custom-call(s32[2,128]{1,0:T(2,128)S(1)} %bitcast.23, s32[1,128]{1,0:T(1,128)S(1)} %bitcast.26, f32[4,128,256]{2,1,0:T(8,128)S(1)} %collective-permute-done.1.t_ref), custom_call_target="tpu_custom_call" | custom-call | flops 6550000128 | bytes 1048576 | tf_op jit(solution)/shard_map/prepare/pallas_call | solution.py:145
  45.6 7.4 %collective-permute-done.3.refs_7_ = f32[4,128,256]{2,1,0:T(8,128)S(1)} collective-permute-done((f32[4,128,256]{2,1,0:T(8,128)S(1)}, f32[4,128,256]{2,1,0:T(8,128)S(1)}, u32[]{:S(2)}, u32[]{:S(2)}) %collective-permute-start.3) | collective-permute-done | bytes 524320 | tf_op jit(solution)/shard_map/ppermute | solution.py:200
  53.0 0.8 copy-done.5
  53.8 0.6 collective-permute-done.4.refs_8_
  54.4 2.6 %all-to-all-done.1 = f32[24,32,128]{2,1,0:T(8,128)S(1)} async-done(((f32[24,32,128]{2,1,0:T(8,128)}), f32[24,32,128]{2,1,0:T(8,128)S(1)}, u32[]{:S(2)}, u32[]{:S(2)}) %all-to-all-start.1) | async-done | bytes 393248 | tf_op jit(solution)/shard_map/all_to_all | solution.py:188
  57.0 0.0 copy-done.2
  57.0 0.0 copy-done.3
  57.0 3.3 %multiply.2 = (f32[16,3,16,128]{3,2,1,0:T(8,128)S(1)}, f32[16,3,16,128]{3,2,1,0:T(8,128)S(1)}) custom-call(s32[1]{0:T(128)} %constant.27.clone.1.round_ref.refs_0_, s32[128]{0:T(128)S(1)} %copy-done.2, s32[3]{0:T(128)S(1)} %copy-done.3, s32[1,128]{1,0:T(1,128)S(1)} %get-tuple-element.271.refs_3_, s32[256,128]{1,0:T(8,128)S(1)} %get-tuple-element.272.refs_4_, ...), custom_call_target="tpu_custom_call" | custom-call | flops 1207959552 | bytes 4194304 | tf_op jit(solution)/shard_map/multiply/pallas_call | solution.py:158
  60.3 0.0 copy-done
  60.3 0.0 copy-done.6
  60.4 0.7 while.12
  61.1 7.2 %collective-permute-start.5 = (f32[16,3,16,128]{3,2,1,0:T(8,128)S(1)}, f32[16,3,16,128]{3,2,1,0:T(8,128)S(1)}, u32[]{:S(2)}, u32[]{:S(2)}) collective-permute-start(f32[16,3,16,128]{3,2,1,0:T(8,128)S(1)} %get-tuple-element.121), channel_id=1, source_target_pairs={{0,1},{1,0},{2,3},{3,2},{4,5},{5,4},{6,7},{7,6},{8,9},{9,8},{10,11... | collective-permute-start | bytes 1179656 | tf_op jit(solution)/shard_map/ppermute | solution.py:213
  68.2 1.3 %collective-permute-done.5 = f32[16,3,16,128]{3,2,1,0:T(8,128)S(1)} collective-permute-done((f32[16,3,16,128]{3,2,1,0:T(8,128)S(1)}, f32[16,3,16,128]{3,2,1,0:T(8,128)S(1)}, u32[]{:S(2)}, u32[]{:S(2)}) %collective-permute-start.5) | collective-permute-done | bytes 393248 | tf_op jit(solution)/shard_map/ppermute | solution.py:213
  69.6 0.1 add.34
  69.6 16.6 %all_to_all.16 = f32[16,3,16,128]{3,2,1,0:T(8,128)S(1)} all-to-all(f32[16,3,16,128]{3,2,1,0:T(8,128)S(1)} %add.34), channel_id=1, replica_groups=mesh['z'=12,'y_hi'=2,'x'=4,'y_lo'=4,'core'=2] {'x','y_lo'}, dimensions={0} | all-to-all | bytes 786432 | tf_op jit(solution)/shard_map/all_to_all | solution.py:214
  86.2 0.6 reduce_sum.9
  (3 shorter events, 0.0 us)
Async XLA Ops:
  1.7 27.3 %collective-permute-start.2 = (f32[32,128]{1,0:T(8,128)S(1)}, f32[32,128]{1,0:T(8,128)S(1)}, u32[]{:S(2)}, u32[]{:S(2)}) collective-permute-start(f32[32,128]{1,0:T(8,128)S(1)} %get-tuple-element.110), channel_id=1, source_target_pairs={{0,0},{1,32},{2,64},{3,96},{4,128},{5,160},{6,192},{7,224},{8,256}... | collective-permute-start | bytes 49160 | tf_op jit(solution)/shard_map/ppermute | solution.py:193
  10.6 34.1 %copy-start.1 = (s32[256]{0:T(256)S(1)}, s32[256]{0:T(256)}, u32[]{:S(2)}) copy-start(s32[256]{0:T(256)} %param.12) | copy-start | bytes 3076
  10.6 34.1 %copy-start.4 = (s32[128]{0:T(128)S(1)}, s32[128]{0:T(128)}, u32[]{:S(2)}) copy-start(s32[128]{0:T(128)} %param.13) | copy-start | bytes 1540
  12.3 32.3 %collective-permute-start.1 = (f32[4,128,256]{2,1,0:T(8,128)S(1)}, f32[4,128,256]{2,1,0:T(8,128)S(1)}, u32[]{:S(2)}, u32[]{:S(2)}) collective-permute-start(f32[4,128,256]{2,1,0:T(8,128)S(1)} %get-tuple-element.157), channel_id=1, source_target_pairs={{0,16},{8,24},{16,0},{24,8},{1,17},{9,25},{17,1},{25,9},{2,18},{10... | collective-permute-start | bytes 1572872 | tf_op jit(solution)/shard_map/ppermute | solution.py:200
  29.8 27.1 %all-to-all-start.1 = ((f32[24,32,128]{2,1,0:T(8,128)}), f32[24,32,128]{2,1,0:T(8,128)S(1)}, u32[]{:S(2)}, u32[]{:S(2)}) async-start(f32[24,32,128]{2,1,0:T(8,128)} %broadcast_in_dim.8), calls=%async_computation.1 | async-start | bytes 786432 | tf_op jit(solution)/shard_map/all_to_all | solution.py:188
  38.1 18.9 %copy-start.2 = (s32[128]{0:T(128)S(1)}, s32[128]{0:T(128)}, u32[]{:S(2)}) copy-start(s32[128]{0:T(128)} %refs_1_.1) | copy-start | bytes 1540
  38.1 18.9 %copy-start.3 = (s32[3]{0:T(128)S(1)}, s32[3]{0:T(128)}, u32[]{:S(2)}) copy-start(s32[3]{0:T(128)} %refs_2_.1) | copy-start | bytes 40
  38.1 14.9 %collective-permute-start.3 = (f32[4,128,256]{2,1,0:T(8,128)S(1)}, f32[4,128,256]{2,1,0:T(8,128)S(1)}, u32[]{:S(2)}, u32[]{:S(2)}) collective-permute-start(f32[4,128,256]{2,1,0:T(8,128)S(1)} %get-tuple-element.113), channel_id=1, source_target_pairs={{0,8},{8,16},{16,24},{24,0},{1,9},{9,17},{17,25},{25,1},{2,10},{10... | collective-permute-start | bytes 1572872 | tf_op jit(solution)/shard_map/ppermute | solution.py:200
  41.3 13.1 %collective-permute-start.4 = (f32[4,128,256]{2,1,0:T(8,128)S(1)}, f32[4,128,256]{2,1,0:T(8,128)}, u32[]{:S(2)}, u32[]{:S(2)}) collective-permute-start(f32[4,128,256]{2,1,0:T(8,128)S(1)} %get-tuple-element.114), channel_id=1, source_target_pairs={{0,24},{8,0},{16,8},{24,16},{1,25},{9,1},{17,9},{25,17},{2,26},{10... | collective-permute-start | bytes 1572872 | tf_op jit(solution)/shard_map/ppermute | solution.py:200
  53.0 0.8 copy-start.5
  57.0 3.4 %copy-start = (f32[4,32,128]{2,1,0:T(8,128)S(1)}, f32[4,32,128]{2,1,0:T(8,128)}, u32[]{:S(2)}) copy-start(f32[4,32,128]{2,1,0:T(8,128)} %w_ref.1) | copy-start | bytes 196612
  57.0 3.4 %copy-start.6 = (f32[4,128,256]{2,1,0:T(8,128)S(1)}, f32[4,128,256]{2,1,0:T(8,128)}, u32[]{:S(2)}) copy-start(f32[4,128,256]{2,1,0:T(8,128)} %copy-done.5) | copy-start | bytes 1572868
  61.1 8.5 %collective-permute-start.5 = (f32[16,3,16,128]{3,2,1,0:T(8,128)S(1)}, f32[16,3,16,128]{3,2,1,0:T(8,128)S(1)}, u32[]{:S(2)}, u32[]{:S(2)}) collective-permute-start(f32[16,3,16,128]{3,2,1,0:T(8,128)S(1)} %get-tuple-element.121), channel_id=1, source_target_pairs={{0,1},{1,0},{2,3},{3,2},{4,5},{5,4},{6,7},{7,6},{8,9},{9,8},{10,11... | collective-permute-start | bytes 1179656 | tf_op jit(solution)/shard_map/ppermute | solution.py:213

commit v9 on v8

--- a/solution.py
+++ b/solution.py
@@ -81,14 +81,16 @@
         high_ref[:, k * 256:(k + 1) * 256], low_ref[:, k * 256:(k + 1) * 256] = halves(t_ref[k])
 
 
-def multiply_kernel(with_sum, round_ref, occ_ref, j_ref, rank_ref, right_ref, w_ref, *rest):
+def multiply_kernel(with_sum, table_ref, round_ref, occ_ref, j_ref, rank_ref, right_ref, w_ref, *rest):
     t_refs, ready, rest = rest[:3], rest[3:5], rest[5:]
     sums, (own_ref, given_ref, w_both, t_high, t_low) = rest[:2 * with_sum], rest[2 * with_sum:]
     rank, right = rank_ref[...], right_ref[...]
     put = jnp.concatenate(
         [jnp.where(placing(rank, round_ref[0], part), 1.0, 0.0).astype(jnp.bfloat16) for part in range(ROWS)], axis=1
     )
-    spreads = [jnp.dot(piece, put, preferred_element_type=jnp.float32) for piece in halves(w_ref[...].reshape(768, LANES))]
+    column = (lax.axis_index("x") * 8 + vir_index()) * 24
+    w = jnp.concatenate([w_ref[table_ref[column + block]] for block in range(24)], axis=0)
+    spreads = [jnp.dot(piece, put, preferred_element_type=jnp.float32) for piece in halves(w)]
     first = vir_index() * 16 + lax.axis_index("x") * 4
     for k in range(4):
         for j in range(J):
@@ -96,8 +98,8 @@
             keep = right == jnp.bitwise_xor(occ_ref[first + k], j_ref[j])
             for half, spread in enumerate(spreads):
                 piece = spread[group * 256:(group + 1) * 256, part * LANES:(part + 1) * LANES]
-                column = (half * J + j) * LANES
-                w_both[k * 256:(k + 1) * 256, column:column + LANES] = jnp.where(keep, piece, 0.0).astype(jnp.bfloat16)
+                lane = (half * J + j) * LANES
+                w_both[k * 256:(k + 1) * 256, lane:lane + LANES] = jnp.where(keep, piece, 0.0).astype(jnp.bfloat16)
         for shift, t_ref in zip((0, 1, 3), t_refs):
             high, low = halves(t_ref[k])
             t_high[shift * LANES:(shift + 1) * LANES, k * 256:(k + 1) * 256] = high
@@ -154,43 +156,74 @@
     )(vir, b, t)
 
 
-def multiply(round_index, occ, j, rank, right, w, t, sums=()):
+def multiply(table, round_index, occ, j, rank, right, w, t, sums=()):
     return pl.pallas_call(
         lambda *refs: multiply_kernel(bool(sums), *refs),
         out_shape=(jax.ShapeDtypeStruct((16, J, 16, LANES), jnp.float32),) * 2,
-        in_specs=[SMEM] * 3 + [VMEM] * (8 + len(sums)),
+        in_specs=[SMEM] * 4 + [VMEM] * (8 + len(sums)),
         out_specs=(VMEM, VMEM),
         scratch_shapes=[pltpu.VMEM((1024, 2 * J * LANES), jnp.bfloat16)] + [pltpu.VMEM((512, 1024), jnp.bfloat16)] * 2,
         compiler_params=pltpu.CompilerParams(vmem_limit_bytes=24 << 20),
         cost_estimate=pl.CostEstimate(flops=3 * 2 * 512 * 1024 * 384, bytes_accessed=4 << 20, transcendentals=0),
         name="multiply",
-    )(round_index, occ, j, rank, right, w, *t, *sums)
+    )(table, round_index, occ, j, rank, right, w, *t, *sums)
+
+
+def hops(source, target):
+    (occ, vir), (occ_to, vir_to) = source, target
+    spans = (
+        (occ % 4 - occ_to % 4, 4),
+        (occ // 4 % 2 * 4 + vir // 2 - occ_to // 4 % 2 * 4 - vir_to // 2, 8),
+        (occ // 8 - occ_to // 8, 12),
+    )
+    return sum(min(span % ring, -span % ring) for span, ring in spans)
+
+
+def matched(costs, limit):
+    held = [None] * 24
+
+    def placed(block, seen):
+        for place in sorted(range(24), key=lambda place: costs[block][place]):
+            if costs[block][place] <= limit and place not in seen:
+                seen.add(place)
+                if held[place] is None or placed(held[place], seen):
+                    held[place] = block
+                    return True
+        return False
+
+    return held if all(placed(block, set()) for block in range(24)) else None
 
 
 def owners():
-    pairs = []
-    for o in range(96):
+    pairs, table = [], []
+    for x in range(4):
         for v in range(8):
-            place = o % 3 * 8 + v
-            pairs.append((o * 8 + v, (place * 4 + o % 12 // 3) * 8 + o // 12))
-    return pairs
+            blocks = [(v * 12 + x * 3 + block // 8, block % 8) for block in range(24)]
+            costs = [[hops(block, (place * 4 + x, v)) for place in range(24)] for block in blocks]
+            held = next(found for found in (matched(costs, limit) for limit in range(20)) if found)
+            for place, block in enumerate(held):
+                pairs.append((blocks[block][0] * 8 + blocks[block][1], (place * 4 + x) * 8 + v))
+            table += [held.index(block) for block in range(24)]
+    return pairs, table
 
 
 def local(amplitudes, integrals, irrep_occ, irrep_j, irrep_vir, irrep_b):
     vir, b = irrep_vir.reshape(2, LANES), irrep_b.reshape(1, LANES)
+    pairs, table = owners()
+    table = jnp.asarray(table, jnp.int32)
     labels = (irrep_occ, irrep_j, vir, b)
 
     def owned(round_index):
-        return lax.ppermute(pack(round_index, *labels, integrals)[0], AXES, owners())
+        return lax.ppermute(pack(round_index, *labels, integrals)[0], AXES, pairs)
 
     def column(packed):
         copies = jnp.broadcast_to(packed[None], (24, SLAB, LANES))
         gathered = lax.all_to_all(copies, HOPS, split_axis=0, concat_axis=0, tiled=True)
-        return gathered.reshape(3, 256, LANES)
+        return gathered
 
     packed, rounds = pack(jnp.zeros((1,), jnp.int32), *labels, integrals)
     packed, amplitudes = lax.optimization_barrier((packed, amplitudes))
-    packed = lax.ppermute(packed, AXES, owners())
+    packed = lax.ppermute(packed, AXES, pairs)
     x = lax.axis_index("x")
 
     def piece(shift):
@@ -203,11 +236,11 @@
     known = (irrep_occ, irrep_j, rank, right)
     packed, *near = lax.optimization_barrier((packed, piece(0), piece(1), piece(3)))
     t = [near[0], exchanged(near[1], 1), exchanged(near[2], 3), *opposite]
-    sums = multiply(jnp.zeros((1,), jnp.int32), *known, column(packed), t)
+    sums = multiply(table, jnp.zeros((1,), jnp.int32), *known, column(packed), t)
 
     def another(state):
         index, sums = state
-        return index + 1, multiply(index[None], *known, column(owned(index[None])), t, sums)
+        return index + 1, multiply(table, index[None], *known, column(owned(index[None])), t, sums)
 
     _, (own, given) = lax.while_loop(lambda state: state[0] < rounds[0], another, (jnp.int32(1), sums))
     total = own + lax.ppermute(given, "core", [(0, 1), (1, 0)])

time: 87.3 us -> 86 us (0.985)
  blocking collectives: 16.6 us -> 15.7 us
    ppermute x3, starting transfers between devices: 23.2 us -> 10 us  [exchanged(): return lax.ppermute(piece, 'x', [(s, (s + shift) % 4) for s in range(4)])]
    ppermute x1, starting transfers between devices: 8.84 us -> 16.9 us  [local(): packed = lax.ppermute(packed, AXES, pairs)]
    all_to_all x1, starting transfers between devices: 8.24 us -> 12.6 us  [column(): lax.all_to_all(copies, HOPS, split_axis=0, concat_axis=0, tiled=True)]
    all_to_all x1, waiting for transfers between devices: 2.59 us -> 1.38 us  [column(): lax.all_to_all(copies, HOPS, split_axis=0, concat_axis=0, tiled=True)]
    ppermute x3, waiting for transfers between devices: 8.04 us -> 9.21 us  [exchanged(): return lax.ppermute(piece, 'x', [(s, (s + shift) % 4) for s in range(4)])]
where the time goes in v9:
time: 86 us; the launch traced here: 85.5 us
  starting transfers between devices  47.1 us (55%)
  blocking collectives  15.7 us (18%)
  waiting for transfers between devices  11.9 us (14%)
  Pallas kernels  5.92 us (7%)
  local copies, waits for them, and re-layouts  3.38 us (4%)
    ppermute x1, starting transfers between devices, local(): packed = lax.ppermute(packed, AXES, pairs)  16.9 us
    all_to_all x1, blocking collectives, local(): lax.all_to_all(total, PLANE, split_axis=0, concat_axis=0, tiled=True)  15.7 us
    all_to_all x1, starting transfers between devices, column(): lax.all_to_all(copies, HOPS, split_axis=0, concat_axis=0, tiled=True)  12.6 us
    ppermute x3, starting transfers between devices, exchanged(): return lax.ppermute(piece, 'x', [(s, (s + shift) % 4) for s in range(4)])  10 us
    ppermute x3, waiting for transfers between devices, exchanged(): return lax.ppermute(piece, 'x', [(s, (s + shift) % 4) for s in range(4)])  9.21 us
    ppermute x1, starting transfers between devices, local(): total = own + lax.ppermute(given, 'core', [(0, 1), (1, 0)])  7.59 us
    pallas_call x1, Pallas kernels, multiply(): pl.pallas_call(lambda *refs: multiply_kernel(bool(sums), *refs), out_shap...  3.32 us
    dynamic_slice x1, local copies, waits for them, and re-layouts, piece(): return lax.dynamic_slice_in_dim(amplitudes[0], lax.rem(x + shift, 4) * 4, 4)  1.72 us
  transfers between devices with their start and end apart: 6, of which 4 were waited for; matrix products, arithmetic and copies ran while one was open for 3% of the time, Pallas kernels for 1%

profile of v9, /device:TPU:1, one launch (start us, length us, event | category | flops | bytes accessed | tf_op | source)
XLA Modules:
  0.0 85.5 jit_solution(15535131045595435498)
XLA Ops:
  0.0 1.7 %pack.2 = (f32[32,128]{1,0:T(8,128)S(1)}, s32[1]{0:T(128)}) custom-call(s32[1]{0:T(128)} %constant.29.clone.1.round_ref.refs_1_, s32[128]{0:T(128)} %refs_2_.1, s32[3]{0:T(128)} %refs_3_.1, s32[2,128]{1,0:T(2,128)} %bitcast.16, s32[1,128]{1,0:T(1,128)} %bitcast.19, f32[4,32,128]{2,1,0:T(8,128)} %w_ref.1), custom_call_target="tpu_custom_call" | custom-call | tf_op jit(solution)/shard_map/pack/pallas_call | solution.py:135
  1.7 16.9 %collective-permute-start.2 = (f32[32,128]{1,0:T(8,128)S(1)}, f32[32,128]{1,0:T(8,128)S(1)}, u32[]{:S(2)}, u32[]{:S(2)}) collective-permute-start(f32[32,128]{1,0:T(8,128)S(1)} %get-tuple-element.115), channel_id=1, source_target_pairs={{11,0},{23,32},{20,64},{22,96},{2,128},{3,160},{18,192},{13,224},{... | collective-permute-start | bytes 49160 | tf_op jit(solution)/shard_map/ppermute | solution.py:226
  18.6 0.0 copy-start.1
  18.6 0.0 copy-start.4
  18.6 1.7 %dynamic-slice_bitcast_fusion = (f32[4,128,256]{2,1,0:T(8,128)S(1)}, f32[4,128,256]{2,1,0:T(8,128)S(1)}, f32[4,128,256]{2,1,0:T(8,128)S(1)}, f32[4,128,256]{2,1,0:T(8,128)S(1)}) fusion(f32[1,16,128,256]{3,2,1,0:T(8,128)} %param.9, s32[]{:T(128)S(6)} %select_n.15, s32[]{:T(128)S(6)} %select_n.14, s32[]{:T(128)S(6)} %select_n.13, s32[]{:T(128)S(6)} %select_n.12), kind=kLoop, calls=%fused_computation | loop fusion | bytes 4194320 | tf_op jit(solution)/shard_map/dynamic_slice | solution.py:230
  20.4 3.4 %collective-permute-start.1 = (f32[4,128,256]{2,1,0:T(8,128)S(1)}, f32[4,128,256]{2,1,0:T(8,128)S(1)}, u32[]{:S(2)}, u32[]{:S(2)}) collective-permute-start(f32[4,128,256]{2,1,0:T(8,128)S(1)} %get-tuple-element.220), channel_id=1, source_target_pairs={{0,16},{8,24},{16,0},{24,8},{1,17},{9,25},{17,1},{25,9},{2,18},{10... | collective-permute-start | bytes 1572872 | tf_op jit(solution)/shard_map/ppermute | solution.py:233
  23.8 0.0 collective-permute-done.2
  23.8 0.8 broadcast_in_dim.8
  24.6 12.6 %all-to-all-start.1 = ((f32[24,32,128]{2,1,0:T(8,128)}), f32[24,32,128]{2,1,0:T(8,128)S(1)}, u32[]{:S(2)}, u32[]{:S(2)}) async-start(f32[24,32,128]{2,1,0:T(8,128)} %broadcast_in_dim.8), calls=%async_computation.1 | async-start | bytes 786432 | tf_op jit(solution)/shard_map/all_to_all | solution.py:221
  37.2 0.0 copy-start.2
  37.2 0.0 copy-start.3
  37.3 0.0 copy-start.7
  37.3 2.7 %collective-permute-start.3 = (f32[4,128,256]{2,1,0:T(8,128)S(1)}, f32[4,128,256]{2,1,0:T(8,128)S(1)}, u32[]{:S(2)}, u32[]{:S(2)}) collective-permute-start(f32[4,128,256]{2,1,0:T(8,128)S(1)} %get-tuple-element.118), channel_id=1, source_target_pairs={{0,8},{8,16},{16,24},{24,0},{1,9},{9,17},{17,25},{25,1},{2,10},{10... | collective-permute-start | bytes 1572872 | tf_op jit(solution)/shard_map/ppermute | solution.py:233
  40.0 3.9 %collective-permute-start.4 = (f32[4,128,256]{2,1,0:T(8,128)S(1)}, f32[4,128,256]{2,1,0:T(8,128)}, u32[]{:S(2)}, u32[]{:S(2)}) collective-permute-start(f32[4,128,256]{2,1,0:T(8,128)S(1)} %get-tuple-element.119), channel_id=1, source_target_pairs={{0,24},{8,0},{16,8},{24,16},{1,25},{9,1},{17,9},{25,17},{2,26},{10... | collective-permute-start | bytes 1572872 | tf_op jit(solution)/shard_map/ppermute | solution.py:233
  43.9 0.0 collective-permute-done.1.t_ref
  43.9 0.0 copy-done.1
  43.9 0.0 copy-done.4
  43.9 0.9 %prepare.1 = (s32[1,128]{1,0:T(1,128)S(1)}, s32[256,128]{1,0:T(8,128)S(1)}, bf16[128,1024]{1,0:T(8,128)(2,1)S(1)}, bf16[128,1024]{1,0:T(8,128)(2,1)}) custom-call(s32[2,128]{1,0:T(2,128)S(1)} %bitcast.17, s32[1,128]{1,0:T(1,128)S(1)} %bitcast.20, f32[4,128,256]{2,1,0:T(8,128)S(1)} %collective-permute-done.1.t_ref), custom_call_target="tpu_custom_call" | custom-call | flops 6550000128 | bytes 1048576 | tf_op jit(solution)/shard_map/prepare/pallas_call | solution.py:147
  44.8 8.1 %collective-permute-done.3.refs_8_ = f32[4,128,256]{2,1,0:T(8,128)S(1)} collective-permute-done((f32[4,128,256]{2,1,0:T(8,128)S(1)}, f32[4,128,256]{2,1,0:T(8,128)S(1)}, u32[]{:S(2)}, u32[]{:S(2)}) %collective-permute-start.3) | collective-permute-done | bytes 524320 | tf_op jit(solution)/shard_map/ppermute | solution.py:233
  52.9 0.8 copy-done.5
  53.7 1.2 %collective-permute-done.4.refs_9_ = f32[4,128,256]{2,1,0:T(8,128)} collective-permute-done((f32[4,128,256]{2,1,0:T(8,128)S(1)}, f32[4,128,256]{2,1,0:T(8,128)}, u32[]{:S(2)}, u32[]{:S(2)}) %collective-permute-start.4) | collective-permute-done | bytes 524320 | tf_op jit(solution)/shard_map/ppermute | solution.py:233
  54.9 1.4 %all-to-all-done.1.refs_6_ = f32[24,32,128]{2,1,0:T(8,128)S(1)} async-done(((f32[24,32,128]{2,1,0:T(8,128)}), f32[24,32,128]{2,1,0:T(8,128)S(1)}, u32[]{:S(2)}, u32[]{:S(2)}) %all-to-all-start.1) | async-done | bytes 393248 | tf_op jit(solution)/shard_map/all_to_all | solution.py:221
  56.2 0.0 copy-done.2
  56.2 0.0 copy-done.7
  56.3 0.0 copy-start
  56.3 3.3 %multiply.2 = (f32[16,3,16,128]{3,2,1,0:T(8,128)S(1)}, f32[16,3,16,128]{3,2,1,0:T(8,128)S(1)}) custom-call(s32[768]{0:T(1024)S(1)} %copy-done.7, s32[1]{0:T(128)} %constant.29.clone.1.round_ref.refs_1_, s32[128]{0:T(128)S(1)} %copy-done.2, s32[3]{0:T(128)S(1)} %copy-done.3, s32[1,128]{1,0:T(1,128)S(1)} %get-tuple-element.334.refs_4_, ...), custom_call_target="tpu_custom_call" | custom-call | flops 1207959552 | bytes 4194304 | tf_op jit(solution)/shard_map/multiply/pallas_call | solution.py:160
  59.6 0.6 while.13
  60.2 7.6 %collective-permute-start.5 = (f32[16,3,16,128]{3,2,1,0:T(8,128)S(1)}, f32[16,3,16,128]{3,2,1,0:T(8,128)S(1)}, u32[]{:S(2)}, u32[]{:S(2)}) collective-permute-start(f32[16,3,16,128]{3,2,1,0:T(8,128)S(1)} %get-tuple-element.126), channel_id=1, source_target_pairs={{0,1},{1,0},{2,3},{3,2},{4,5},{5,4},{6,7},{7,6},{8,9},{9,8},{10,11... | collective-permute-start | bytes 1179656 | tf_op jit(solution)/shard_map/ppermute | solution.py:246
  67.8 1.3 %collective-permute-done.5 = f32[16,3,16,128]{3,2,1,0:T(8,128)S(1)} collective-permute-done((f32[16,3,16,128]{3,2,1,0:T(8,128)S(1)}, f32[16,3,16,128]{3,2,1,0:T(8,128)S(1)}, u32[]{:S(2)}, u32[]{:S(2)}) %collective-permute-start.5) | collective-permute-done | bytes 393248 | tf_op jit(solution)/shard_map/ppermute | solution.py:246
  69.1 0.1 add.34
  69.2 15.7 %all_to_all.18 = f32[16,3,16,128]{3,2,1,0:T(8,128)S(1)} all-to-all(f32[16,3,16,128]{3,2,1,0:T(8,128)S(1)} %add.34), channel_id=1, replica_groups=mesh['z'=12,'y_hi'=2,'x'=4,'y_lo'=4,'core'=2] {'x','y_lo'}, dimensions={0} | all-to-all | bytes 786432 | tf_op jit(solution)/shard_map/all_to_all | solution.py:247
  84.9 0.6 reduce_sum.9
  (3 shorter events, 0.0 us)
Async XLA Ops:
  1.7 22.1 %collective-permute-start.2 = (f32[32,128]{1,0:T(8,128)S(1)}, f32[32,128]{1,0:T(8,128)S(1)}, u32[]{:S(2)}, u32[]{:S(2)}) collective-permute-start(f32[32,128]{1,0:T(8,128)S(1)} %get-tuple-element.115), channel_id=1, source_target_pairs={{11,0},{23,32},{20,64},{22,96},{2,128},{3,160},{18,192},{13,224},{... | collective-permute-start | bytes 49160 | tf_op jit(solution)/shard_map/ppermute | solution.py:226
  18.6 25.3 %copy-start.1 = (s32[256]{0:T(256)S(1)}, s32[256]{0:T(256)}, u32[]{:S(2)}) copy-start(s32[256]{0:T(256)} %param.13) | copy-start | bytes 3076
  18.6 25.3 %copy-start.4 = (s32[128]{0:T(128)S(1)}, s32[128]{0:T(128)}, u32[]{:S(2)}) copy-start(s32[128]{0:T(128)} %param.14) | copy-start | bytes 1540
  20.4 23.5 %collective-permute-start.1 = (f32[4,128,256]{2,1,0:T(8,128)S(1)}, f32[4,128,256]{2,1,0:T(8,128)S(1)}, u32[]{:S(2)}, u32[]{:S(2)}) collective-permute-start(f32[4,128,256]{2,1,0:T(8,128)S(1)} %get-tuple-element.220), channel_id=1, source_target_pairs={{0,16},{8,24},{16,0},{24,8},{1,17},{9,25},{17,1},{25,9},{2,18},{10... | collective-permute-start | bytes 1572872 | tf_op jit(solution)/shard_map/ppermute | solution.py:233
  24.6 31.6 %all-to-all-start.1 = ((f32[24,32,128]{2,1,0:T(8,128)}), f32[24,32,128]{2,1,0:T(8,128)S(1)}, u32[]{:S(2)}, u32[]{:S(2)}) async-start(f32[24,32,128]{2,1,0:T(8,128)} %broadcast_in_dim.8), calls=%async_computation.1 | async-start | bytes 786432 | tf_op jit(solution)/shard_map/all_to_all | solution.py:221
  37.2 19.0 %copy-start.2 = (s32[128]{0:T(128)S(1)}, s32[128]{0:T(128)}, u32[]{:S(2)}) copy-start(s32[128]{0:T(128)} %refs_2_.1) | copy-start | bytes 1540
  37.2 19.0 %copy-start.3 = (s32[3]{0:T(128)S(1)}, s32[3]{0:T(128)}, u32[]{:S(2)}) copy-start(s32[3]{0:T(128)} %refs_3_.1) | copy-start | bytes 40
  37.3 19.0 %copy-start.7 = (s32[768]{0:T(1024)S(1)}, s32[768]{0:T(1024)}, u32[]{:S(2)}) copy-start(s32[768]{0:T(1024)} %constant.37.clone.refs_0_) | copy-start | bytes 9220
  37.3 15.6 %collective-permute-start.3 = (f32[4,128,256]{2,1,0:T(8,128)S(1)}, f32[4,128,256]{2,1,0:T(8,128)S(1)}, u32[]{:S(2)}, u32[]{:S(2)}) collective-permute-start(f32[4,128,256]{2,1,0:T(8,128)S(1)} %get-tuple-element.118), channel_id=1, source_target_pairs={{0,8},{8,16},{16,24},{24,0},{1,9},{9,17},{17,25},{25,1},{2,10},{10... | collective-permute-start | bytes 1572872 | tf_op jit(solution)/shard_map/ppermute | solution.py:233
  40.0 14.9 %collective-permute-start.4 = (f32[4,128,256]{2,1,0:T(8,128)S(1)}, f32[4,128,256]{2,1,0:T(8,128)}, u32[]{:S(2)}, u32[]{:S(2)}) collective-permute-start(f32[4,128,256]{2,1,0:T(8,128)S(1)} %get-tuple-element.119), channel_id=1, source_target_pairs={{0,24},{8,0},{16,8},{24,16},{1,25},{9,1},{17,9},{25,17},{2,26},{10... | collective-permute-start | bytes 1572872 | tf_op jit(solution)/shard_map/ppermute | solution.py:233
  52.9 0.8 copy-start.5
  56.3 3.3 %copy-start = (f32[4,32,128]{2,1,0:T(8,128)S(1)}, f32[4,32,128]{2,1,0:T(8,128)}, u32[]{:S(2)}) copy-start(f32[4,32,128]{2,1,0:T(8,128)} %w_ref.1) | copy-start | bytes 196612
  60.2 8.9 %collective-permute-start.5 = (f32[16,3,16,128]{3,2,1,0:T(8,128)S(1)}, f32[16,3,16,128]{3,2,1,0:T(8,128)S(1)}, u32[]{:S(2)}, u32[]{:S(2)}) collective-permute-start(f32[16,3,16,128]{3,2,1,0:T(8,128)S(1)} %get-tuple-element.126), channel_id=1, source_target_pairs={{0,1},{1,0},{2,3},{3,2},{4,5},{5,4},{6,7},{7,6},{8,9},{9,8},{10,11... | collective-permute-start | bytes 1179656 | tf_op jit(solution)/shard_map/ppermute | solution.py:246

commit v10 on v9

--- a/solution.py
+++ b/solution.py
@@ -71,18 +71,21 @@
     rounds_ref[0] = lax.div(jnp.max(rank) + PLACES, PLACES)
 
 
-def prepare_kernel(vir_ref, b_ref, t_ref, rank_ref, right_ref, high_ref, low_ref):
+def prepare_kernel(vir_ref, b_ref, near_ref, far_ref, rank_ref, right_ref, high_ref, low_ref):
     label_b = b_ref[...]
     rank_ref[...] = ranks(label_b)
     for half in range(2):
         label_c = columns(vir_ref[half:half + 1, :])
         right_ref[half * LANES:(half + 1) * LANES, :] = jnp.bitwise_xor(label_c, label_b)
     for k in range(4):
-        high_ref[:, k * 256:(k + 1) * 256], low_ref[:, k * 256:(k + 1) * 256] = halves(t_ref[k])
+        for shift, t_ref in enumerate((near_ref, far_ref)):
+            high, low = halves(t_ref[k])
+            high_ref[shift * LANES:(shift + 1) * LANES, k * 256:(k + 1) * 256] = high
+            low_ref[shift * LANES:(shift + 1) * LANES, k * 256:(k + 1) * 256] = low
 
 
 def multiply_kernel(with_sum, table_ref, round_ref, occ_ref, j_ref, rank_ref, right_ref, w_ref, *rest):
-    t_refs, ready, rest = rest[:3], rest[3:5], rest[5:]
+    t_refs, ready, rest = rest[:2], rest[2:4], rest[4:]
     sums, (own_ref, given_ref, w_both, t_high, t_low) = rest[:2 * with_sum], rest[2 * with_sum:]
     rank, right = rank_ref[...], right_ref[...]
     put = jnp.concatenate(
@@ -100,12 +103,12 @@
                 piece = spread[group * 256:(group + 1) * 256, part * LANES:(part + 1) * LANES]
                 lane = (half * J + j) * LANES
                 w_both[k * 256:(k + 1) * 256, lane:lane + LANES] = jnp.where(keep, piece, 0.0).astype(jnp.bfloat16)
-        for shift, t_ref in zip((0, 1, 3), t_refs):
+        for shift, t_ref in zip((0, 3), t_refs):
             high, low = halves(t_ref[k])
             t_high[shift * LANES:(shift + 1) * LANES, k * 256:(k + 1) * 256] = high
             t_low[shift * LANES:(shift + 1) * LANES, k * 256:(k + 1) * 256] = low
     for ref, target in zip(ready, (t_high, t_low)):
-        target[2 * LANES:3 * LANES, :] = ref[...]
+        target[LANES:3 * LANES, :] = ref[...]
     both = jnp.dot(t_high[...], w_both[...], preferred_element_type=jnp.float32)
     total = both[:, :J * LANES] + both[:, J * LANES:]
     total = total + jnp.dot(t_low[...], w_both[:, :J * LANES], preferred_element_type=jnp.float32)
@@ -143,24 +146,24 @@
     )(round_index, occ, j, vir, b, integrals)
 
 
-def prepare(vir, b, t):
+def prepare(vir, b, near, far):
     return pl.pallas_call(
         prepare_kernel,
         out_shape=(jax.ShapeDtypeStruct((1, LANES), jnp.int32), jax.ShapeDtypeStruct((256, LANES), jnp.int32))
-        + (jax.ShapeDtypeStruct((LANES, 1024), jnp.bfloat16),) * 2,
-        in_specs=[VMEM] * 3,
+        + (jax.ShapeDtypeStruct((2 * LANES, 1024), jnp.bfloat16),) * 2,
+        in_specs=[VMEM] * 4,
         out_specs=(VMEM,) * 4,
         compiler_params=pltpu.CompilerParams(vmem_limit_bytes=8 << 20),
         cost_estimate=pl.CostEstimate(flops=PREPARE_WEIGHT, bytes_accessed=1 << 20, transcendentals=0),
         name="prepare",
-    )(vir, b, t)
+    )(vir, b, near, far)
 
 
 def multiply(table, round_index, occ, j, rank, right, w, t, sums=()):
     return pl.pallas_call(
         lambda *refs: multiply_kernel(bool(sums), *refs),
         out_shape=(jax.ShapeDtypeStruct((16, J, 16, LANES), jnp.float32),) * 2,
-        in_specs=[SMEM] * 4 + [VMEM] * (8 + len(sums)),
+        in_specs=[SMEM] * 4 + [VMEM] * (7 + len(sums)),
         out_specs=(VMEM, VMEM),
         scratch_shapes=[pltpu.VMEM((1024, 2 * J * LANES), jnp.bfloat16)] + [pltpu.VMEM((512, 1024), jnp.bfloat16)] * 2,
         compiler_params=pltpu.CompilerParams(vmem_limit_bytes=24 << 20),
@@ -232,10 +235,10 @@
     def exchanged(piece, shift):
         return lax.ppermute(piece, "x", [(s, (s + shift) % 4) for s in range(4)])
 
-    rank, right, *opposite = prepare(vir, b, exchanged(piece(2), 2))
+    rank, right, *early = prepare(vir, b, exchanged(piece(1), 1), exchanged(piece(2), 2))
     known = (irrep_occ, irrep_j, rank, right)
-    packed, *near = lax.optimization_barrier((packed, piece(0), piece(1), piece(3)))
-    t = [near[0], exchanged(near[1], 1), exchanged(near[2], 3), *opposite]
+    packed, *near = lax.optimization_barrier((packed, piece(0), piece(3)))
+    t = [near[0], exchanged(near[1], 3), *early]
     sums = multiply(table, jnp.zeros((1,), jnp.int32), *known, column(packed), t)
 
     def another(state):

time: 86 us -> 88.8 us (1.033)
  waiting for transfers between devices: 11.9 us -> 15.1 us
  starting transfers between devices: 47.1 us -> 46.1 us
    all_to_all x1, waiting for transfers between devices: 1.38 us -> 3.45 us  [column(): lax.all_to_all(copies, HOPS, split_axis=0, concat_axis=0, tiled=True)]
    ppermute x3, waiting for transfers between devices: 9.21 us -> 10.3 us  [exchanged(): return lax.ppermute(piece, 'x', [(s, (s + shift) % 4) for s in range(4)])]
  transfers between devices with their start and end apart: 6 -> 6, of which waited for: 4 -> 4; matrix products, arithmetic and copies ran while one was open for 3% -> 4% of each run, Pallas kernels for 1% -> 1%
where the time goes in v10:
time: 88.8 us; the launch traced here: 88.3 us
  starting transfers between devices  46.1 us (52%)
  blocking collectives  16.3 us (18%)
  waiting for transfers between devices  15.1 us (17%)
  Pallas kernels  6.1 us (7%)
  local copies, waits for them, and re-layouts  3.36 us (4%)
    ppermute x1, starting transfers between devices, local(): packed = lax.ppermute(packed, AXES, pairs)  16.9 us
    all_to_all x1, blocking collectives, local(): lax.all_to_all(total, PLANE, split_axis=0, concat_axis=0, tiled=True)  16.3 us
    all_to_all x1, starting transfers between devices, column(): lax.all_to_all(copies, HOPS, split_axis=0, concat_axis=0, tiled=True)  12.6 us
    ppermute x3, waiting for transfers between devices, exchanged(): return lax.ppermute(piece, 'x', [(s, (s + shift) % 4) for s in range(4)])  10.3 us
    ppermute x3, starting transfers between devices, exchanged(): return lax.ppermute(piece, 'x', [(s, (s + shift) % 4) for s in range(4)])  9.28 us
    ppermute x1, starting transfers between devices, local(): total = own + lax.ppermute(given, 'core', [(0, 1), (1, 0)])  7.31 us
    all_to_all x1, waiting for transfers between devices, column(): lax.all_to_all(copies, HOPS, split_axis=0, concat_axis=0, tiled=True)  3.45 us
    pallas_call x1, Pallas kernels, multiply(): pl.pallas_call(lambda *refs: multiply_kernel(bool(sums), *refs), out_shap...  3.32 us
  transfers between devices with their start and end apart: 6, of which 4 were waited for; matrix products, arithmetic and copies ran while one was open for 4% of the time, Pallas kernels for 1%

profile of v10, /device:TPU:1, one launch (start us, length us, event | category | flops | bytes accessed | tf_op | source)
XLA Modules:
  0.0 88.3 jit_solution(9348124478436344815)
XLA Ops:
  0.0 1.7 %pack.2 = (f32[32,128]{1,0:T(8,128)S(1)}, s32[1]{0:T(128)}) custom-call(s32[1]{0:T(128)} %constant.29.clone.1.round_ref.refs_1_, s32[128]{0:T(128)} %refs_2_.1, s32[3]{0:T(128)} %refs_3_.1, s32[2,128]{1,0:T(2,128)} %bitcast.16, s32[1,128]{1,0:T(1,128)} %bitcast.19, f32[4,32,128]{2,1,0:T(8,128)} %w_ref.1), custom_call_target="tpu_custom_call" | custom-call | tf_op jit(solution)/shard_map/pack/pallas_call | solution.py:138
  1.7 16.9 %collective-permute-start.3 = (f32[32,128]{1,0:T(8,128)S(1)}, f32[32,128]{1,0:T(8,128)S(1)}, u32[]{:S(2)}, u32[]{:S(2)}) collective-permute-start(f32[32,128]{1,0:T(8,128)S(1)} %get-tuple-element.109), channel_id=1, source_target_pairs={{11,0},{23,32},{20,64},{22,96},{2,128},{3,160},{18,192},{13,224},{... | collective-permute-start | bytes 49160 | tf_op jit(solution)/shard_map/ppermute | solution.py:229
  18.6 0.0 copy-start.1
  18.6 0.0 copy-start.4
  18.6 2.5 %dynamic-slice_bitcast_fusion = (f32[4,128,256]{2,1,0:T(8,128)S(1)}, f32[4,128,256]{2,1,0:T(8,128)S(1)}, f32[4,128,256]{2,1,0:T(8,128)S(1)}, f32[4,128,256]{2,1,0:T(8,128)}) fusion(f32[1,16,128,256]{3,2,1,0:T(8,128)} %param.9, s32[]{:T(128)S(6)} %select_n.15, s32[]{:T(128)S(6)} %select_n.14, s32[]{:T(128)S(6)} %select_n.13, s32[]{:T(128)S(6)} %select_n.12), kind=kLoop, calls=%fused_computation | loop fusion | bytes 4194320 | tf_op jit(solution)/shard_map/dynamic_slice | solution.py:233
  21.1 1.9 %collective-permute-start.1 = (f32[4,128,256]{2,1,0:T(8,128)}, f32[4,128,256]{2,1,0:T(8,128)S(1)}, u32[]{:S(2)}, u32[]{:S(2)}) collective-permute-start(f32[4,128,256]{2,1,0:T(8,128)} %get-tuple-element.208), channel_id=1, source_target_pairs={{0,8},{8,16},{16,24},{24,0},{1,9},{9,17},{17,25},{25,1},{2,10},{10... | collective-permute-start | bytes 1572872 | tf_op jit(solution)/shard_map/ppermute | solution.py:236
  23.1 3.4 %collective-permute-start.2 = (f32[4,128,256]{2,1,0:T(8,128)S(1)}, f32[4,128,256]{2,1,0:T(8,128)S(1)}, u32[]{:S(2)}, u32[]{:S(2)}) collective-permute-start(f32[4,128,256]{2,1,0:T(8,128)S(1)} %get-tuple-element.207), channel_id=1, source_target_pairs={{0,16},{8,24},{16,0},{24,8},{1,17},{9,25},{17,1},{25,9},{2,18},{10... | collective-permute-start | bytes 1572872 | tf_op jit(solution)/shard_map/ppermute | solution.py:236
  26.5 0.0 collective-permute-done.3
  26.5 0.8 broadcast_in_dim.8
  27.3 12.6 %all-to-all-start.1 = ((f32[24,32,128]{2,1,0:T(8,128)}), f32[24,32,128]{2,1,0:T(8,128)S(1)}, u32[]{:S(2)}, u32[]{:S(2)}) async-start(f32[24,32,128]{2,1,0:T(8,128)} %broadcast_in_dim.8), calls=%async_computation.1 | async-start | bytes 786432 | tf_op jit(solution)/shard_map/all_to_all | solution.py:224
  39.9 0.0 copy-start.2
  39.9 0.0 copy-start.3
  40.0 4.0 %collective-permute-start.4 = (f32[4,128,256]{2,1,0:T(8,128)S(1)}, f32[4,128,256]{2,1,0:T(8,128)}, u32[]{:S(2)}, u32[]{:S(2)}) collective-permute-start(f32[4,128,256]{2,1,0:T(8,128)S(1)} %get-tuple-element.112), channel_id=1, source_target_pairs={{0,24},{8,0},{16,8},{24,16},{1,25},{9,1},{17,9},{25,17},{2,26},{10... | collective-permute-start | bytes 1572872 | tf_op jit(solution)/shard_map/ppermute | solution.py:236
  43.9 0.0 collective-permute-done.1.near_ref
  43.9 2.3 %collective-permute-done.2.far_ref = f32[4,128,256]{2,1,0:T(8,128)S(1)} collective-permute-done((f32[4,128,256]{2,1,0:T(8,128)S(1)}, f32[4,128,256]{2,1,0:T(8,128)S(1)}, u32[]{:S(2)}, u32[]{:S(2)}) %collective-permute-start.2) | collective-permute-done | bytes 524320 | tf_op jit(solution)/shard_map/ppermute | solution.py:236
  46.2 0.0 copy-done.1
  46.2 0.0 copy-done.4
  46.2 1.1 %prepare.1 = (s32[1,128]{1,0:T(1,128)}, s32[256,128]{1,0:T(8,128)}, bf16[256,1024]{1,0:T(8,128)(2,1)S(1)}, bf16[256,1024]{1,0:T(8,128)(2,1)}) custom-call(s32[2,128]{1,0:T(2,128)S(1)} %bitcast.17, s32[1,128]{1,0:T(1,128)S(1)} %bitcast.20, f32[4,128,256]{2,1,0:T(8,128)S(1)} %collective-permute-done.1.near_ref, f32[4,128,256]{2,1,0:T(8,128)S(1)} %collective-permute-done.2.far_ref), custom_call_target="tpu_custom_call" | custom-call | flops 6550000128 | bytes 1048576 | tf_op jit(solution)/shard_map/prepare/pallas_call | solution.py:150
  47.3 8.0 %collective-permute-done.4.refs_8_ = f32[4,128,256]{2,1,0:T(8,128)} collective-permute-done((f32[4,128,256]{2,1,0:T(8,128)S(1)}, f32[4,128,256]{2,1,0:T(8,128)}, u32[]{:S(2)}, u32[]{:S(2)}) %collective-permute-start.4) | collective-permute-done | bytes 524320 | tf_op jit(solution)/shard_map/ppermute | solution.py:236
  55.3 3.4 %all-to-all-done.1.refs_6_ = f32[24,32,128]{2,1,0:T(8,128)S(1)} async-done(((f32[24,32,128]{2,1,0:T(8,128)}), f32[24,32,128]{2,1,0:T(8,128)S(1)}, u32[]{:S(2)}, u32[]{:S(2)}) %all-to-all-start.1) | async-done | bytes 393248 | tf_op jit(solution)/shard_map/all_to_all | solution.py:224
  58.8 0.0 copy-done.2
  58.8 0.0 copy-done.3
  58.8 0.0 copy-start
  58.8 3.3 %multiply.2 = (f32[16,3,16,128]{3,2,1,0:T(8,128)S(1)}, f32[16,3,16,128]{3,2,1,0:T(8,128)S(1)}) custom-call(s32[768]{0:T(1024)} %constant.37.clone.refs_0_, s32[1]{0:T(128)} %constant.29.clone.1.round_ref.refs_1_, s32[128]{0:T(128)S(1)} %copy-done.2, s32[3]{0:T(128)S(1)} %copy-done.3, s32[1,128]{1,0:T(1,128)} %get-tuple-element.316.refs_4_, ...), custom_call_target="tpu_custom_call" | custom-call | flops 1207959552 | bytes 4194304 | tf_op jit(solution)/shard_map/multiply/pallas_call | solution.py:163
  62.1 0.0 copy-done
  62.1 0.0 copy-done.5
  62.1 0.6 while.13
  62.7 7.3 %collective-permute-start.5 = (f32[16,3,16,128]{3,2,1,0:T(8,128)S(1)}, f32[16,3,16,128]{3,2,1,0:T(8,128)S(1)}, u32[]{:S(2)}, u32[]{:S(2)}) collective-permute-start(f32[16,3,16,128]{3,2,1,0:T(8,128)S(1)} %get-tuple-element.119), channel_id=1, source_target_pairs={{0,1},{1,0},{2,3},{3,2},{4,5},{5,4},{6,7},{7,6},{8,9},{9,8},{10,11... | collective-permute-start | bytes 1179656 | tf_op jit(solution)/shard_map/ppermute | solution.py:249
  70.0 1.3 %collective-permute-done.5 = f32[16,3,16,128]{3,2,1,0:T(8,128)S(1)} collective-permute-done((f32[16,3,16,128]{3,2,1,0:T(8,128)S(1)}, f32[16,3,16,128]{3,2,1,0:T(8,128)S(1)}, u32[]{:S(2)}, u32[]{:S(2)}) %collective-permute-start.5) | collective-permute-done | bytes 393248 | tf_op jit(solution)/shard_map/ppermute | solution.py:249
  71.3 0.1 add.34
  71.4 16.3 %all_to_all.18 = f32[16,3,16,128]{3,2,1,0:T(8,128)S(1)} all-to-all(f32[16,3,16,128]{3,2,1,0:T(8,128)S(1)} %add.34), channel_id=1, replica_groups=mesh['z'=12,'y_hi'=2,'x'=4,'y_lo'=4,'core'=2] {'x','y_lo'}, dimensions={0} | all-to-all | bytes 786432 | tf_op jit(solution)/shard_map/all_to_all | solution.py:250
  87.7 0.6 reduce_sum.9
  (1 shorter events, 0.0 us)
Async XLA Ops:
  1.7 24.8 %collective-permute-start.3 = (f32[32,128]{1,0:T(8,128)S(1)}, f32[32,128]{1,0:T(8,128)S(1)}, u32[]{:S(2)}, u32[]{:S(2)}) collective-permute-start(f32[32,128]{1,0:T(8,128)S(1)} %get-tuple-element.109), channel_id=1, source_target_pairs={{11,0},{23,32},{20,64},{22,96},{2,128},{3,160},{18,192},{13,224},{... | collective-permute-start | bytes 49160 | tf_op jit(solution)/shard_map/ppermute | solution.py:229
  18.6 27.6 %copy-start.1 = (s32[256]{0:T(256)S(1)}, s32[256]{0:T(256)}, u32[]{:S(2)}) copy-start(s32[256]{0:T(256)} %param.13) | copy-start | bytes 3076
  18.6 27.6 %copy-start.4 = (s32[128]{0:T(128)S(1)}, s32[128]{0:T(128)}, u32[]{:S(2)}) copy-start(s32[128]{0:T(128)} %param.14) | copy-start | bytes 1540
  21.1 22.8 %collective-permute-start.1 = (f32[4,128,256]{2,1,0:T(8,128)}, f32[4,128,256]{2,1,0:T(8,128)S(1)}, u32[]{:S(2)}, u32[]{:S(2)}) collective-permute-start(f32[4,128,256]{2,1,0:T(8,128)} %get-tuple-element.208), channel_id=1, source_target_pairs={{0,8},{8,16},{16,24},{24,0},{1,9},{9,17},{17,25},{25,1},{2,10},{10... | collective-permute-start | bytes 1572872 | tf_op jit(solution)/shard_map/ppermute | solution.py:236
  23.1 23.2 %collective-permute-start.2 = (f32[4,128,256]{2,1,0:T(8,128)S(1)}, f32[4,128,256]{2,1,0:T(8,128)S(1)}, u32[]{:S(2)}, u32[]{:S(2)}) collective-permute-start(f32[4,128,256]{2,1,0:T(8,128)S(1)} %get-tuple-element.207), channel_id=1, source_target_pairs={{0,16},{8,24},{16,0},{24,8},{1,17},{9,25},{17,1},{25,9},{2,18},{10... | collective-permute-start | bytes 1572872 | tf_op jit(solution)/shard_map/ppermute | solution.py:236
  27.3 31.5 %all-to-all-start.1 = ((f32[24,32,128]{2,1,0:T(8,128)}), f32[24,32,128]{2,1,0:T(8,128)S(1)}, u32[]{:S(2)}, u32[]{:S(2)}) async-start(f32[24,32,128]{2,1,0:T(8,128)} %broadcast_in_dim.8), calls=%async_computation.1 | async-start | bytes 786432 | tf_op jit(solution)/shard_map/all_to_all | solution.py:224
  39.9 18.8 %copy-start.2 = (s32[128]{0:T(128)S(1)}, s32[128]{0:T(128)}, u32[]{:S(2)}) copy-start(s32[128]{0:T(128)} %refs_2_.1) | copy-start | bytes 1540
  39.9 18.8 %copy-start.3 = (s32[3]{0:T(128)S(1)}, s32[3]{0:T(128)}, u32[]{:S(2)}) copy-start(s32[3]{0:T(128)} %refs_3_.1) | copy-start | bytes 40
  40.0 15.4 %collective-permute-start.4 = (f32[4,128,256]{2,1,0:T(8,128)S(1)}, f32[4,128,256]{2,1,0:T(8,128)}, u32[]{:S(2)}, u32[]{:S(2)}) collective-permute-start(f32[4,128,256]{2,1,0:T(8,128)S(1)} %get-tuple-element.112), channel_id=1, source_target_pairs={{0,24},{8,0},{16,8},{24,16},{1,25},{9,1},{17,9},{25,17},{2,26},{10... | collective-permute-start | bytes 1572872 | tf_op jit(solution)/shard_map/ppermute | solution.py:236
  58.8 3.3 %copy-start = (f32[4,32,128]{2,1,0:T(8,128)S(1)}, f32[4,32,128]{2,1,0:T(8,128)}, u32[]{:S(2)}) copy-start(f32[4,32,128]{2,1,0:T(8,128)} %w_ref.1) | copy-start | bytes 196612
  58.8 3.3 %copy-start.5 = (s32[768]{0:T(1024)S(1)}, s32[768]{0:T(1024)}, u32[]{:S(2)}) copy-start(s32[768]{0:T(1024)} %constant.37.clone.refs_0_) | copy-start | bytes 9220
  62.7 8.6 %collective-permute-start.5 = (f32[16,3,16,128]{3,2,1,0:T(8,128)S(1)}, f32[16,3,16,128]{3,2,1,0:T(8,128)S(1)}, u32[]{:S(2)}, u32[]{:S(2)}) collective-permute-start(f32[16,3,16,128]{3,2,1,0:T(8,128)S(1)} %get-tuple-element.119), channel_id=1, source_target_pairs={{0,1},{1,0},{2,3},{3,2},{4,5},{5,4},{6,7},{7,6},{8,9},{9,8},{10,11... | collective-permute-start | bytes 1179656 | tf_op jit(solution)/shard_map/ppermute | solution.py:249

commit v11 on v9

--- a/solution.py
+++ b/solution.py
@@ -226,15 +226,16 @@
     packed = lax.ppermute(packed, AXES, pairs)
     x = lax.axis_index("x")
 
-    def piece(shift):
+    def piece(amplitudes, shift):
         return lax.dynamic_slice_in_dim(amplitudes[0], lax.rem(x + shift, 4) * 4, 4)
 
     def exchanged(piece, shift):
         return lax.ppermute(piece, "x", [(s, (s + shift) % 4) for s in range(4)])
 
-    rank, right, *opposite = prepare(vir, b, exchanged(piece(2), 2))
+    far, amplitudes = lax.optimization_barrier((piece(amplitudes, 2), amplitudes))
+    rank, right, *opposite = prepare(vir, b, exchanged(far, 2))
     known = (irrep_occ, irrep_j, rank, right)
-    packed, *near = lax.optimization_barrier((packed, piece(0), piece(1), piece(3)))
+    packed, *near = lax.optimization_barrier((packed, *(piece(amplitudes, shift) for shift in (0, 1, 3))))
     t = [near[0], exchanged(near[1], 1), exchanged(near[2], 3), *opposite]
     sums = multiply(table, jnp.zeros((1,), jnp.int32), *known, column(packed), t)
 

time: 86 us -> 86.5 us (level)
  starting transfers between devices: 47.1 us -> 45 us
  waiting for transfers between devices: 11.9 us -> 13.6 us
    ppermute x1, starting transfers between devices: 7.59 us -> 5.48 us  [local(): total = own + lax.ppermute(given, 'core', [(0, 1), (1, 0)])]
    all_to_all x1, waiting for transfers between devices: 1.38 us -> 3.22 us  [column(): lax.all_to_all(copies, HOPS, split_axis=0, concat_axis=0, tiled=True)]
    dynamic_slice x1 -> x2, local copies, waits for them, and re-layouts: 1.72 us -> 2.57 us  [piece(): return lax.dynamic_slice_in_dim(amplitudes[0], lax.rem(x + shift, 4) * 4, 4)]
  transfers between devices with their start and end apart: 6 -> 6, of which waited for: 4 -> 4; matrix products, arithmetic and copies ran while one was open for 3% -> 4% of each run, Pallas kernels for 1% -> 1%
where the time goes in v11:
time: 86.5 us; the launch traced here: 86 us
  starting transfers between devices  45 us (52%)
  blocking collectives  15.7 us (18%)
  waiting for transfers between devices  13.6 us (16%)
  Pallas kernels  5.92 us (7%)
  local copies, waits for them, and re-layouts  4.23 us (5%)
    ppermute x1, starting transfers between devices, local(): packed = lax.ppermute(packed, AXES, pairs)  16.9 us
    all_to_all x1, blocking collectives, local(): lax.all_to_all(total, PLANE, split_axis=0, concat_axis=0, tiled=True)  15.7 us
    all_to_all x1, starting transfers between devices, column(): lax.all_to_all(copies, HOPS, split_axis=0, concat_axis=0, tiled=True)  12.6 us
    ppermute x3, starting transfers between devices, exchanged(): return lax.ppermute(piece, 'x', [(s, (s + shift) % 4) for s in range(4)])  10 us
    ppermute x3, waiting for transfers between devices, exchanged(): return lax.ppermute(piece, 'x', [(s, (s + shift) % 4) for s in range(4)])  9.09 us
    ppermute x1, starting transfers between devices, local(): total = own + lax.ppermute(given, 'core', [(0, 1), (1, 0)])  5.48 us
    pallas_call x1, Pallas kernels, multiply(): pl.pallas_call(lambda *refs: multiply_kernel(bool(sums), *refs), out_shap...  3.32 us
    all_to_all x1, waiting for transfers between devices, column(): lax.all_to_all(copies, HOPS, split_axis=0, concat_axis=0, tiled=True)  3.22 us
  transfers between devices with their start and end apart: 6, of which 4 were waited for; matrix products, arithmetic and copies ran while one was open for 4% of the time, Pallas kernels for 1%

profile of v11, /device:TPU:1, one launch (start us, length us, event | category | flops | bytes accessed | tf_op | source)
XLA Modules:
  0.0 86.0 jit_solution(4317098246207420071)
XLA Ops:
  0.0 1.7 %pack.2 = (f32[32,128]{1,0:T(8,128)S(1)}, s32[1]{0:T(128)}) custom-call(s32[1]{0:T(128)} %constant.29.clone.1.round_ref.refs_1_, s32[128]{0:T(128)} %refs_2_.1, s32[3]{0:T(128)} %refs_3_.1, s32[2,128]{1,0:T(2,128)} %bitcast.16, s32[1,128]{1,0:T(1,128)} %bitcast.19, f32[4,32,128]{2,1,0:T(8,128)} %w_ref.1), custom_call_target="tpu_custom_call" | custom-call | tf_op jit(solution)/shard_map/pack/pallas_call | solution.py:135
  1.7 16.9 %collective-permute-start.2 = (f32[32,128]{1,0:T(8,128)S(1)}, f32[32,128]{1,0:T(8,128)S(1)}, u32[]{:S(2)}, u32[]{:S(2)}) collective-permute-start(f32[32,128]{1,0:T(8,128)S(1)} %get-tuple-element.118), channel_id=1, source_target_pairs={{11,0},{23,32},{20,64},{22,96},{2,128},{3,160},{18,192},{13,224},{... | collective-permute-start | bytes 49160 | tf_op jit(solution)/shard_map/ppermute | solution.py:226
  18.6 1.1 %dynamic-slice_bitcast_fusion.3 = f32[4,128,256]{2,1,0:T(8,128)S(1)} fusion(f32[1,16,128,256]{3,2,1,0:T(8,128)} %param.9, s32[]{:T(128)S(6)} %select_n.12), kind=kLoop, calls=%fused_computation.3 | loop fusion | bytes 1048580 | tf_op jit(solution)/shard_map/dynamic_slice | solution.py:230
  19.7 3.4 %collective-permute-start.1 = (f32[4,128,256]{2,1,0:T(8,128)S(1)}, f32[4,128,256]{2,1,0:T(8,128)S(1)}, u32[]{:S(2)}, u32[]{:S(2)}) collective-permute-start(f32[4,128,256]{2,1,0:T(8,128)S(1)} %dynamic-slice_bitcast_fusion.3), channel_id=1, source_target_pairs={{0,16},{8,24},{16,0},{24,8},{1,17},{9,25},{17,1},{25,9},{2,18},{10... | collective-permute-start | bytes 1572872 | tf_op jit(solution)/shard_map/ppermute | solution.py:233
  23.1 0.0 copy-start.1
  23.1 0.0 copy-start.4
  23.1 1.5 %dynamic-slice_bitcast_fusion = (f32[4,128,256]{2,1,0:T(8,128)S(1)}, f32[4,128,256]{2,1,0:T(8,128)S(1)}, f32[4,128,256]{2,1,0:T(8,128)S(1)}) fusion(f32[1,16,128,256]{3,2,1,0:T(8,128)} %param.9, s32[]{:T(128)S(6)} %select_n.15, s32[]{:T(128)S(6)} %select_n.14, s32[]{:T(128)S(6)} %select_n.13), kind=kLoop, calls=%fused_computation | loop fusion | bytes 3145740 | tf_op jit(solution)/shard_map/dynamic_slice | solution.py:230
  24.6 0.0 collective-permute-done.2
  24.6 0.8 broadcast_in_dim.8
  25.5 12.6 %all-to-all-start.1 = ((f32[24,32,128]{2,1,0:T(8,128)}), f32[24,32,128]{2,1,0:T(8,128)S(1)}, u32[]{:S(2)}, u32[]{:S(2)}) async-start(f32[24,32,128]{2,1,0:T(8,128)} %broadcast_in_dim.8), calls=%async_computation.1 | async-start | bytes 786432 | tf_op jit(solution)/shard_map/all_to_all | solution.py:221
  38.1 0.0 copy-start.2
  38.1 0.0 copy-start.3
  38.1 0.0 copy-start.7
  38.1 2.1 %collective-permute-start.3 = (f32[4,128,256]{2,1,0:T(8,128)S(1)}, f32[4,128,256]{2,1,0:T(8,128)S(1)}, u32[]{:S(2)}, u32[]{:S(2)}) collective-permute-start(f32[4,128,256]{2,1,0:T(8,128)S(1)} %get-tuple-element.122), channel_id=1, source_target_pairs={{0,8},{8,16},{16,24},{24,0},{1,9},{9,17},{17,25},{25,1},{2,10},{10... | collective-permute-start | bytes 1572872 | tf_op jit(solution)/shard_map/ppermute | solution.py:233
  40.2 4.6 %collective-permute-start.4 = (f32[4,128,256]{2,1,0:T(8,128)S(1)}, f32[4,128,256]{2,1,0:T(8,128)}, u32[]{:S(2)}, u32[]{:S(2)}) collective-permute-start(f32[4,128,256]{2,1,0:T(8,128)S(1)} %get-tuple-element.123), channel_id=1, source_target_pairs={{0,24},{8,0},{16,8},{24,16},{1,25},{9,1},{17,9},{25,17},{2,26},{10... | collective-permute-start | bytes 1572872 | tf_op jit(solution)/shard_map/ppermute | solution.py:233
  44.8 0.0 collective-permute-done.1.t_ref
  44.8 0.0 copy-done.1
  44.8 0.9 %prepare.1 = (s32[1,128]{1,0:T(1,128)S(1)}, s32[256,128]{1,0:T(8,128)S(1)}, bf16[128,1024]{1,0:T(8,128)(2,1)S(1)}, bf16[128,1024]{1,0:T(8,128)(2,1)}) custom-call(s32[2,128]{1,0:T(2,128)S(1)} %bitcast.17, s32[1,128]{1,0:T(1,128)S(1)} %bitcast.20, f32[4,128,256]{2,1,0:T(8,128)S(1)} %collective-permute-done.1.t_ref), custom_call_target="tpu_custom_call" | custom-call | flops 6550000128 | bytes 1048576 | tf_op jit(solution)/shard_map/prepare/pallas_call | solution.py:147
  45.7 9.0 %collective-permute-done.3.refs_8_ = f32[4,128,256]{2,1,0:T(8,128)S(1)} collective-permute-done((f32[4,128,256]{2,1,0:T(8,128)S(1)}, f32[4,128,256]{2,1,0:T(8,128)S(1)}, u32[]{:S(2)}, u32[]{:S(2)}) %collective-permute-start.3) | collective-permute-done | bytes 524320 | tf_op jit(solution)/shard_map/ppermute | solution.py:233
  54.7 0.8 copy-done.5
  55.5 0.1 collective-permute-done.4.refs_9_
  55.6 3.2 %all-to-all-done.1.refs_6_ = f32[24,32,128]{2,1,0:T(8,128)S(1)} async-done(((f32[24,32,128]{2,1,0:T(8,128)}), f32[24,32,128]{2,1,0:T(8,128)S(1)}, u32[]{:S(2)}, u32[]{:S(2)}) %all-to-all-start.1) | async-done | bytes 393248 | tf_op jit(solution)/shard_map/all_to_all | solution.py:221
  58.8 0.0 copy-done.7
  58.8 0.0 copy-start
  58.8 3.3 %multiply.2 = (f32[16,3,16,128]{3,2,1,0:T(8,128)S(1)}, f32[16,3,16,128]{3,2,1,0:T(8,128)S(1)}) custom-call(s32[768]{0:T(1024)S(1)} %copy-done.7, s32[1]{0:T(128)} %constant.29.clone.1.round_ref.refs_1_, s32[128]{0:T(128)S(1)} %copy-done.2, s32[3]{0:T(128)S(1)} %copy-done.3, s32[1,128]{1,0:T(1,128)S(1)} %get-tuple-element.337.refs_4_, ...), custom_call_target="tpu_custom_call" | custom-call | flops 1207959552 | bytes 4194304 | tf_op jit(solution)/shard_map/multiply/pallas_call | solution.py:160
  62.2 0.0 copy-done
  62.2 0.6 while.13
  62.8 5.5 %collective-permute-start.5 = (f32[16,3,16,128]{3,2,1,0:T(8,128)S(1)}, f32[16,3,16,128]{3,2,1,0:T(8,128)S(1)}, u32[]{:S(2)}, u32[]{:S(2)}) collective-permute-start(f32[16,3,16,128]{3,2,1,0:T(8,128)S(1)} %get-tuple-element.130), channel_id=1, source_target_pairs={{0,1},{1,0},{2,3},{3,2},{4,5},{5,4},{6,7},{7,6},{8,9},{9,8},{10,11... | collective-permute-start | bytes 1179656 | tf_op jit(solution)/shard_map/ppermute | solution.py:247
  68.2 1.3 %collective-permute-done.5 = f32[16,3,16,128]{3,2,1,0:T(8,128)S(1)} collective-permute-done((f32[16,3,16,128]{3,2,1,0:T(8,128)S(1)}, f32[16,3,16,128]{3,2,1,0:T(8,128)S(1)}, u32[]{:S(2)}, u32[]{:S(2)}) %collective-permute-start.5) | collective-permute-done | bytes 393248 | tf_op jit(solution)/shard_map/ppermute | solution.py:247
  69.6 0.1 add.34
  69.6 15.7 %all_to_all.18 = f32[16,3,16,128]{3,2,1,0:T(8,128)S(1)} all-to-all(f32[16,3,16,128]{3,2,1,0:T(8,128)S(1)} %add.34), channel_id=1, replica_groups=mesh['z'=12,'y_hi'=2,'x'=4,'y_lo'=4,'core'=2] {'x','y_lo'}, dimensions={0} | all-to-all | bytes 786432 | tf_op jit(solution)/shard_map/all_to_all | solution.py:248
  85.4 0.6 reduce_sum.9
  (4 shorter events, 0.0 us)
Async XLA Ops:
  1.7 22.9 %collective-permute-start.2 = (f32[32,128]{1,0:T(8,128)S(1)}, f32[32,128]{1,0:T(8,128)S(1)}, u32[]{:S(2)}, u32[]{:S(2)}) collective-permute-start(f32[32,128]{1,0:T(8,128)S(1)} %get-tuple-element.118), channel_id=1, source_target_pairs={{11,0},{23,32},{20,64},{22,96},{2,128},{3,160},{18,192},{13,224},{... | collective-permute-start | bytes 49160 | tf_op jit(solution)/shard_map/ppermute | solution.py:226
  19.7 25.1 %collective-permute-start.1 = (f32[4,128,256]{2,1,0:T(8,128)S(1)}, f32[4,128,256]{2,1,0:T(8,128)S(1)}, u32[]{:S(2)}, u32[]{:S(2)}) collective-permute-start(f32[4,128,256]{2,1,0:T(8,128)S(1)} %dynamic-slice_bitcast_fusion.3), channel_id=1, source_target_pairs={{0,16},{8,24},{16,0},{24,8},{1,17},{9,25},{17,1},{25,9},{2,18},{10... | collective-permute-start | bytes 1572872 | tf_op jit(solution)/shard_map/ppermute | solution.py:233
  23.1 21.7 %copy-start.1 = (s32[256]{0:T(256)S(1)}, s32[256]{0:T(256)}, u32[]{:S(2)}) copy-start(s32[256]{0:T(256)} %param.13) | copy-start | bytes 3076
  23.1 21.7 %copy-start.4 = (s32[128]{0:T(128)S(1)}, s32[128]{0:T(128)}, u32[]{:S(2)}) copy-start(s32[128]{0:T(128)} %param.14) | copy-start | bytes 1540
  25.5 33.4 %all-to-all-start.1 = ((f32[24,32,128]{2,1,0:T(8,128)}), f32[24,32,128]{2,1,0:T(8,128)S(1)}, u32[]{:S(2)}, u32[]{:S(2)}) async-start(f32[24,32,128]{2,1,0:T(8,128)} %broadcast_in_dim.8), calls=%async_computation.1 | async-start | bytes 786432 | tf_op jit(solution)/shard_map/all_to_all | solution.py:221
  38.1 20.7 %copy-start.2 = (s32[128]{0:T(128)S(1)}, s32[128]{0:T(128)}, u32[]{:S(2)}) copy-start(s32[128]{0:T(128)} %refs_2_.1) | copy-start | bytes 1540
  38.1 20.7 %copy-start.3 = (s32[3]{0:T(128)S(1)}, s32[3]{0:T(128)}, u32[]{:S(2)}) copy-start(s32[3]{0:T(128)} %refs_3_.1) | copy-start | bytes 40
  38.1 20.7 %copy-start.7 = (s32[768]{0:T(1024)S(1)}, s32[768]{0:T(1024)}, u32[]{:S(2)}) copy-start(s32[768]{0:T(1024)} %constant.37.clone.refs_0_) | copy-start | bytes 9220
  38.1 16.6 %collective-permute-start.3 = (f32[4,128,256]{2,1,0:T(8,128)S(1)}, f32[4,128,256]{2,1,0:T(8,128)S(1)}, u32[]{:S(2)}, u32[]{:S(2)}) collective-permute-start(f32[4,128,256]{2,1,0:T(8,128)S(1)} %get-tuple-element.122), channel_id=1, source_target_pairs={{0,8},{8,16},{16,24},{24,0},{1,9},{9,17},{17,25},{25,1},{2,10},{10... | collective-permute-start | bytes 1572872 | tf_op jit(solution)/shard_map/ppermute | solution.py:233
  40.2 15.4 %collective-permute-start.4 = (f32[4,128,256]{2,1,0:T(8,128)S(1)}, f32[4,128,256]{2,1,0:T(8,128)}, u32[]{:S(2)}, u32[]{:S(2)}) collective-permute-start(f32[4,128,256]{2,1,0:T(8,128)S(1)} %get-tuple-element.123), channel_id=1, source_target_pairs={{0,24},{8,0},{16,8},{24,16},{1,25},{9,1},{17,9},{25,17},{2,26},{10... | collective-permute-start | bytes 1572872 | tf_op jit(solution)/shard_map/ppermute | solution.py:233
  54.7 0.8 copy-start.5
  58.8 3.3 %copy-start = (f32[4,32,128]{2,1,0:T(8,128)S(1)}, f32[4,32,128]{2,1,0:T(8,128)}, u32[]{:S(2)}) copy-start(f32[4,32,128]{2,1,0:T(8,128)} %w_ref.1) | copy-start | bytes 196612
  62.8 6.8 %collective-permute-start.5 = (f32[16,3,16,128]{3,2,1,0:T(8,128)S(1)}, f32[16,3,16,128]{3,2,1,0:T(8,128)S(1)}, u32[]{:S(2)}, u32[]{:S(2)}) collective-permute-start(f32[16,3,16,128]{3,2,1,0:T(8,128)S(1)} %get-tuple-element.130), channel_id=1, source_target_pairs={{0,1},{1,0},{2,3},{3,2},{4,5},{5,4},{6,7},{7,6},{8,9},{9,8},{10,11... | collective-permute-start | bytes 1179656 | tf_op jit(solution)/shard_map/ppermute | solution.py:247

commit v12 on v9

--- a/solution.py
+++ b/solution.py
@@ -1,3 +1,5 @@
+import itertools
+
 import jax
 import jax.numpy as jnp
 from jax import lax
@@ -201,6 +203,10 @@
             blocks = [(v * 12 + x * 3 + block // 8, block % 8) for block in range(24)]
             costs = [[hops(block, (place * 4 + x, v)) for place in range(24)] for block in blocks]
             held = next(found for found in (matched(costs, limit) for limit in range(20)) if found)
+            for first, second in list(itertools.combinations(range(24), 2)) * 6:
+                one, two = held[first], held[second]
+                if costs[one][first] ** 4 + costs[two][second] ** 4 > costs[one][second] ** 4 + costs[two][first] ** 4:
+                    held[first], held[second] = two, one
             for place, block in enumerate(held):
                 pairs.append((blocks[block][0] * 8 + blocks[block][1], (place * 4 + x) * 8 + v))
             table += [held.index(block) for block in range(24)]

time: 86 us -> 86.4 us (level)
  starting transfers between devices: 47.1 us -> 42.6 us
  blocking collectives: 15.7 us -> 19.8 us
  waiting for transfers between devices: 11.9 us -> 12.8 us
    all_to_all x1, blocking collectives: 15.7 us -> 19.8 us  [local(): lax.all_to_all(total, PLANE, split_axis=0, concat_axis=0, tiled=True)]
    all_to_all x1, starting transfers between devices: 12.6 us -> 9.9 us  [column(): lax.all_to_all(copies, HOPS, split_axis=0, concat_axis=0, tiled=True)]
    ppermute x3, waiting for transfers between devices: 9.21 us -> 11.4 us  [exchanged(): return lax.ppermute(piece, 'x', [(s, (s + shift) % 4) for s in range(4)])]
    ppermute x1, starting transfers between devices: 7.59 us -> 5.78 us  [local(): total = own + lax.ppermute(given, 'core', [(0, 1), (1, 0)])]
    all_to_all x1, waiting for transfers between devices: 1.38 us -> 0.01 us  [column(): lax.all_to_all(copies, HOPS, split_axis=0, concat_axis=0, tiled=True)]
  transfers between devices with their start and end apart: 6 -> 6, of which waited for: 4 -> 3; matrix products, arithmetic and copies ran while one was open for 3% -> 3% of each run, Pallas kernels for 1% -> 1%
where the time goes in v12:
time: 86.4 us; the launch traced here: 85.9 us
  starting transfers between devices  42.6 us (49%)
  blocking collectives  19.8 us (23%)
  waiting for transfers between devices  12.8 us (15%)
  Pallas kernels  5.92 us (7%)
  local copies, waits for them, and re-layouts  3.38 us (4%)
    all_to_all x1, blocking collectives, local(): lax.all_to_all(total, PLANE, split_axis=0, concat_axis=0, tiled=True)  19.8 us
    ppermute x1, starting transfers between devices, local(): packed = lax.ppermute(packed, AXES, pairs)  16.9 us
    ppermute x3, waiting for transfers between devices, exchanged(): return lax.ppermute(piece, 'x', [(s, (s + shift) % 4) for s in range(4)])  11.4 us
    ppermute x3, starting transfers between devices, exchanged(): return lax.ppermute(piece, 'x', [(s, (s + shift) % 4) for s in range(4)])  10 us
    all_to_all x1, starting transfers between devices, column(): lax.all_to_all(copies, HOPS, split_axis=0, concat_axis=0, tiled=True)  9.9 us
    ppermute x1, starting transfers between devices, local(): total = own + lax.ppermute(given, 'core', [(0, 1), (1, 0)])  5.78 us
    pallas_call x1, Pallas kernels, multiply(): pl.pallas_call(lambda *refs: multiply_kernel(bool(sums), *refs), out_shap...  3.32 us
  transfers between devices with their start and end apart: 6, of which 3 were waited for; matrix products, arithmetic and copies ran while one was open for 3% of the time, Pallas kernels for 1%

profile of v12, /device:TPU:1, one launch (start us, length us, event | category | flops | bytes accessed | tf_op | source)
XLA Modules:
  0.0 85.9 jit_solution(2896378241797118208)
XLA Ops:
  0.0 1.7 %pack.2 = (f32[32,128]{1,0:T(8,128)S(1)}, s32[1]{0:T(128)}) custom-call(s32[1]{0:T(128)} %constant.29.clone.1.round_ref.refs_1_, s32[128]{0:T(128)} %refs_2_.1, s32[3]{0:T(128)} %refs_3_.1, s32[2,128]{1,0:T(2,128)} %bitcast.16, s32[1,128]{1,0:T(1,128)} %bitcast.19, f32[4,32,128]{2,1,0:T(8,128)} %w_ref.1), custom_call_target="tpu_custom_call" | custom-call | tf_op jit(solution)/shard_map/pack/pallas_call | solution.py:137
  1.7 16.9 %collective-permute-start.2 = (f32[32,128]{1,0:T(8,128)S(1)}, f32[32,128]{1,0:T(8,128)S(1)}, u32[]{:S(2)}, u32[]{:S(2)}) collective-permute-start(f32[32,128]{1,0:T(8,128)S(1)} %get-tuple-element.115), channel_id=1, source_target_pairs={{21,0},{20,32},{19,64},{22,96},{11,128},{3,160},{16,192},{4,224},{... | collective-permute-start | bytes 49160 | tf_op jit(solution)/shard_map/ppermute | solution.py:232
  18.6 0.0 copy-start.1
  18.6 0.0 copy-start.4
  18.6 1.7 %dynamic-slice_bitcast_fusion = (f32[4,128,256]{2,1,0:T(8,128)S(1)}, f32[4,128,256]{2,1,0:T(8,128)S(1)}, f32[4,128,256]{2,1,0:T(8,128)S(1)}, f32[4,128,256]{2,1,0:T(8,128)S(1)}) fusion(f32[1,16,128,256]{3,2,1,0:T(8,128)} %param.9, s32[]{:T(128)S(6)} %select_n.15, s32[]{:T(128)S(6)} %select_n.14, s32[]{:T(128)S(6)} %select_n.13, s32[]{:T(128)S(6)} %select_n.12), kind=kLoop, calls=%fused_computation | loop fusion | bytes 4194320 | tf_op jit(solution)/shard_map/dynamic_slice | solution.py:236
  20.4 3.4 %collective-permute-start.1 = (f32[4,128,256]{2,1,0:T(8,128)S(1)}, f32[4,128,256]{2,1,0:T(8,128)S(1)}, u32[]{:S(2)}, u32[]{:S(2)}) collective-permute-start(f32[4,128,256]{2,1,0:T(8,128)S(1)} %get-tuple-element.220), channel_id=1, source_target_pairs={{0,16},{8,24},{16,0},{24,8},{1,17},{9,25},{17,1},{25,9},{2,18},{10... | collective-permute-start | bytes 1572872 | tf_op jit(solution)/shard_map/ppermute | solution.py:239
  23.8 0.0 collective-permute-done.2
  23.8 0.8 broadcast_in_dim.8
  24.6 9.9 %all-to-all-start.1 = ((f32[24,32,128]{2,1,0:T(8,128)}), f32[24,32,128]{2,1,0:T(8,128)S(1)}, u32[]{:S(2)}, u32[]{:S(2)}) async-start(f32[24,32,128]{2,1,0:T(8,128)} %broadcast_in_dim.8), calls=%async_computation.1 | async-start | bytes 786432 | tf_op jit(solution)/shard_map/all_to_all | solution.py:227
  34.5 0.0 copy-start.2
  34.5 0.0 copy-start.3
  34.5 0.0 copy-start.7
  34.5 4.7 %collective-permute-start.3 = (f32[4,128,256]{2,1,0:T(8,128)S(1)}, f32[4,128,256]{2,1,0:T(8,128)S(1)}, u32[]{:S(2)}, u32[]{:S(2)}) collective-permute-start(f32[4,128,256]{2,1,0:T(8,128)S(1)} %get-tuple-element.118), channel_id=1, source_target_pairs={{0,8},{8,16},{16,24},{24,0},{1,9},{9,17},{17,25},{25,1},{2,10},{10... | collective-permute-start | bytes 1572872 | tf_op jit(solution)/shard_map/ppermute | solution.py:239
  39.3 1.9 %collective-permute-start.4 = (f32[4,128,256]{2,1,0:T(8,128)S(1)}, f32[4,128,256]{2,1,0:T(8,128)}, u32[]{:S(2)}, u32[]{:S(2)}) collective-permute-start(f32[4,128,256]{2,1,0:T(8,128)S(1)} %get-tuple-element.119), channel_id=1, source_target_pairs={{0,24},{8,0},{16,8},{24,16},{1,25},{9,1},{17,9},{25,17},{2,26},{10... | collective-permute-start | bytes 1572872 | tf_op jit(solution)/shard_map/ppermute | solution.py:239
  41.2 0.0 collective-permute-done.1.t_ref
  41.2 0.0 copy-done.1
  41.2 0.0 copy-done.4
  41.2 0.9 %prepare.1 = (s32[1,128]{1,0:T(1,128)S(1)}, s32[256,128]{1,0:T(8,128)S(1)}, bf16[128,1024]{1,0:T(8,128)(2,1)S(1)}, bf16[128,1024]{1,0:T(8,128)(2,1)}) custom-call(s32[2,128]{1,0:T(2,128)S(1)} %bitcast.17, s32[1,128]{1,0:T(1,128)S(1)} %bitcast.20, f32[4,128,256]{2,1,0:T(8,128)S(1)} %collective-permute-done.1.t_ref), custom_call_target="tpu_custom_call" | custom-call | flops 6550000128 | bytes 1048576 | tf_op jit(solution)/shard_map/prepare/pallas_call | solution.py:149
  42.1 7.6 %collective-permute-done.3.refs_8_ = f32[4,128,256]{2,1,0:T(8,128)S(1)} collective-permute-done((f32[4,128,256]{2,1,0:T(8,128)S(1)}, f32[4,128,256]{2,1,0:T(8,128)S(1)}, u32[]{:S(2)}, u32[]{:S(2)}) %collective-permute-start.3) | collective-permute-done | bytes 524320 | tf_op jit(solution)/shard_map/ppermute | solution.py:239
  49.7 0.8 copy-done.5
  50.5 3.8 %collective-permute-done.4.refs_9_ = f32[4,128,256]{2,1,0:T(8,128)} collective-permute-done((f32[4,128,256]{2,1,0:T(8,128)S(1)}, f32[4,128,256]{2,1,0:T(8,128)}, u32[]{:S(2)}, u32[]{:S(2)}) %collective-permute-start.4) | collective-permute-done | bytes 524320 | tf_op jit(solution)/shard_map/ppermute | solution.py:239
  54.4 0.0 all-to-all-done.1.refs_6_
  54.4 0.0 copy-done.2
  54.4 0.0 copy-done.3
  54.4 0.0 copy-start
  54.4 3.3 %multiply.2 = (f32[16,3,16,128]{3,2,1,0:T(8,128)S(1)}, f32[16,3,16,128]{3,2,1,0:T(8,128)S(1)}) custom-call(s32[768]{0:T(1024)S(1)} %copy-done.7, s32[1]{0:T(128)} %constant.29.clone.1.round_ref.refs_1_, s32[128]{0:T(128)S(1)} %copy-done.2, s32[3]{0:T(128)S(1)} %copy-done.3, s32[1,128]{1,0:T(1,128)S(1)} %get-tuple-element.334.refs_4_, ...), custom_call_target="tpu_custom_call" | custom-call | flops 1207959552 | bytes 4194304 | tf_op jit(solution)/shard_map/multiply/pallas_call | solution.py:162
  57.7 0.6 while.13
  58.3 5.8 %collective-permute-start.5 = (f32[16,3,16,128]{3,2,1,0:T(8,128)S(1)}, f32[16,3,16,128]{3,2,1,0:T(8,128)S(1)}, u32[]{:S(2)}, u32[]{:S(2)}) collective-permute-start(f32[16,3,16,128]{3,2,1,0:T(8,128)S(1)} %get-tuple-element.126), channel_id=1, source_target_pairs={{0,1},{1,0},{2,3},{3,2},{4,5},{5,4},{6,7},{7,6},{8,9},{9,8},{10,11... | collective-permute-start | bytes 1179656 | tf_op jit(solution)/shard_map/ppermute | solution.py:252
  64.1 1.3 %collective-permute-done.5 = f32[16,3,16,128]{3,2,1,0:T(8,128)S(1)} collective-permute-done((f32[16,3,16,128]{3,2,1,0:T(8,128)S(1)}, f32[16,3,16,128]{3,2,1,0:T(8,128)S(1)}, u32[]{:S(2)}, u32[]{:S(2)}) %collective-permute-start.5) | collective-permute-done | bytes 393248 | tf_op jit(solution)/shard_map/ppermute | solution.py:252
  65.4 0.1 add.34
  65.5 19.8 %all_to_all.18 = f32[16,3,16,128]{3,2,1,0:T(8,128)S(1)} all-to-all(f32[16,3,16,128]{3,2,1,0:T(8,128)S(1)} %add.34), channel_id=1, replica_groups=mesh['z'=12,'y_hi'=2,'x'=4,'y_lo'=4,'core'=2] {'x','y_lo'}, dimensions={0} | all-to-all | bytes 786432 | tf_op jit(solution)/shard_map/all_to_all | solution.py:253
  85.3 0.6 reduce_sum.9
  (3 shorter events, 0.0 us)
Async XLA Ops:
  1.7 22.1 %collective-permute-start.2 = (f32[32,128]{1,0:T(8,128)S(1)}, f32[32,128]{1,0:T(8,128)S(1)}, u32[]{:S(2)}, u32[]{:S(2)}) collective-permute-start(f32[32,128]{1,0:T(8,128)S(1)} %get-tuple-element.115), channel_id=1, source_target_pairs={{21,0},{20,32},{19,64},{22,96},{11,128},{3,160},{16,192},{4,224},{... | collective-permute-start | bytes 49160 | tf_op jit(solution)/shard_map/ppermute | solution.py:232
  18.6 22.6 %copy-start.1 = (s32[256]{0:T(256)S(1)}, s32[256]{0:T(256)}, u32[]{:S(2)}) copy-start(s32[256]{0:T(256)} %param.13) | copy-start | bytes 3076
  18.6 22.6 %copy-start.4 = (s32[128]{0:T(128)S(1)}, s32[128]{0:T(128)}, u32[]{:S(2)}) copy-start(s32[128]{0:T(128)} %param.14) | copy-start | bytes 1540
  20.4 20.8 %collective-permute-start.1 = (f32[4,128,256]{2,1,0:T(8,128)S(1)}, f32[4,128,256]{2,1,0:T(8,128)S(1)}, u32[]{:S(2)}, u32[]{:S(2)}) collective-permute-start(f32[4,128,256]{2,1,0:T(8,128)S(1)} %get-tuple-element.220), channel_id=1, source_target_pairs={{0,16},{8,24},{16,0},{24,8},{1,17},{9,25},{17,1},{25,9},{2,18},{10... | collective-permute-start | bytes 1572872 | tf_op jit(solution)/shard_map/ppermute | solution.py:239
  24.6 29.8 %all-to-all-start.1 = ((f32[24,32,128]{2,1,0:T(8,128)}), f32[24,32,128]{2,1,0:T(8,128)S(1)}, u32[]{:S(2)}, u32[]{:S(2)}) async-start(f32[24,32,128]{2,1,0:T(8,128)} %broadcast_in_dim.8), calls=%async_computation.1 | async-start | bytes 786432 | tf_op jit(solution)/shard_map/all_to_all | solution.py:227
  34.5 19.9 %copy-start.2 = (s32[128]{0:T(128)S(1)}, s32[128]{0:T(128)}, u32[]{:S(2)}) copy-start(s32[128]{0:T(128)} %refs_2_.1) | copy-start | bytes 1540
  34.5 19.9 %copy-start.3 = (s32[3]{0:T(128)S(1)}, s32[3]{0:T(128)}, u32[]{:S(2)}) copy-start(s32[3]{0:T(128)} %refs_3_.1) | copy-start | bytes 40
  34.5 19.8 %copy-start.7 = (s32[768]{0:T(1024)S(1)}, s32[768]{0:T(1024)}, u32[]{:S(2)}) copy-start(s32[768]{0:T(1024)} %constant.37.clone.refs_0_) | copy-start | bytes 9220
  34.5 15.2 %collective-permute-start.3 = (f32[4,128,256]{2,1,0:T(8,128)S(1)}, f32[4,128,256]{2,1,0:T(8,128)S(1)}, u32[]{:S(2)}, u32[]{:S(2)}) collective-permute-start(f32[4,128,256]{2,1,0:T(8,128)S(1)} %get-tuple-element.118), channel_id=1, source_target_pairs={{0,8},{8,16},{16,24},{24,0},{1,9},{9,17},{17,25},{25,1},{2,10},{10... | collective-permute-start | bytes 1572872 | tf_op jit(solution)/shard_map/ppermute | solution.py:239
  39.3 15.1 %collective-permute-start.4 = (f32[4,128,256]{2,1,0:T(8,128)S(1)}, f32[4,128,256]{2,1,0:T(8,128)}, u32[]{:S(2)}, u32[]{:S(2)}) collective-permute-start(f32[4,128,256]{2,1,0:T(8,128)S(1)} %get-tuple-element.119), channel_id=1, source_target_pairs={{0,24},{8,0},{16,8},{24,16},{1,25},{9,1},{17,9},{25,17},{2,26},{10... | collective-permute-start | bytes 1572872 | tf_op jit(solution)/shard_map/ppermute | solution.py:239
  49.7 0.8 copy-start.5
  54.4 3.3 %copy-start = (f32[4,32,128]{2,1,0:T(8,128)S(1)}, f32[4,32,128]{2,1,0:T(8,128)}, u32[]{:S(2)}) copy-start(f32[4,32,128]{2,1,0:T(8,128)} %w_ref.1) | copy-start | bytes 196612
  58.3 7.1 %collective-permute-start.5 = (f32[16,3,16,128]{3,2,1,0:T(8,128)S(1)}, f32[16,3,16,128]{3,2,1,0:T(8,128)S(1)}, u32[]{:S(2)}, u32[]{:S(2)}) collective-permute-start(f32[16,3,16,128]{3,2,1,0:T(8,128)S(1)} %get-tuple-element.126), channel_id=1, source_target_pairs={{0,1},{1,0},{2,3},{3,2},{4,5},{5,4},{6,7},{7,6},{8,9},{9,8},{10,11... | collective-permute-start | bytes 1179656 | tf_op jit(solution)/shard_map/ppermute | solution.py:252
